TPU v7x, 128 devices: a whole 4x4x4 slice. The times are simulated.
128 devices in a mesh: row: 8 (over z, x_lo), col: 16 (over x_hi, y, core).
Axes of the slice: x: 4 (x_hi: 2, x_lo: 2; x = x_hi * 2 + x_lo), y: 4, z: 4, core: 2. Of those that a mesh axis runs over, the one named last changes fastest.
Arguments:
- amplitudes: bfloat16 [2048, 8, 4096], P('col', None, 'row'), may hold values from -6 to 6
- integrals: bfloat16 [32, 4096, 4096], P(None, 'row', 'col'), may hold values from -0.046875 to 0.046875
- blocks: int32 [32, 2], replicated, may hold values from 0 to 7, as said below
Outputs:
- ladder: bfloat16 [2048, 8, 4096], P(('row', 'col'))
Inputs may be any that keep to these rules, and one draw needn't show every extreme that they name: No (contracted tile, output tile) pair appears twice; each of the 8 contracted tiles and each output tile appears in exactly 4 blocks.
All inputs are finite; a program needn't handle non-finite values.
Results may differ from a plain program's by a relative error of at most 0.001.
Values may be sent and summed in bfloat16 or wider, within the bound.
No kernel may reach another device: no remote copies, remote signals or barrier semaphores. Data moves between devices by JAX's collectives and lax.ppermute only.
A program may use at most 192 MiB of HBM per device.

v0:
```python
import jax
import jax.numpy as jnp
from jax import lax
from jax.sharding import PartitionSpec as P


def contract(panel_rows, integrals, sorted_rows, sorted_blocks, per_column):
    pair_count = panel_rows.shape[0]
    tile_total = panel_rows.shape[1]
    inner_size = panel_rows.shape[2]
    outer_size = integrals.shape[2]
    columns = []
    for tile in range(tile_total):
        lower = tile * per_column
        left_rows = jnp.take(panel_rows, sorted_rows[lower : lower + per_column], axis=1)
        left_rows = left_rows.reshape(pair_count, per_column * inner_size)
        right_cols = jnp.take(integrals, sorted_blocks[lower : lower + per_column], axis=0)
        right_cols = right_cols.reshape(per_column * inner_size, outer_size)
        columns.append(jnp.dot(left_rows, right_cols, preferred_element_type=jnp.float32))
    return jnp.stack(columns, axis=1)


def on_device(amplitudes, integrals, blocks):
    tile_total = amplitudes.shape[1]
    per_column = integrals.shape[0] // tile_total
    sorted_blocks = jnp.argsort(blocks[:, 1], stable=True)
    sorted_rows = jnp.take(blocks[:, 0], sorted_blocks, axis=0)
    gathered = lax.all_gather(amplitudes, "col", axis=0, tiled=True)
    summed = lax.psum_scatter(
        contract(gathered, integrals, sorted_rows, sorted_blocks, per_column),
        "row",
        scatter_dimension=0,
        tiled=True,
    )
    ladder = lax.all_to_all(
        summed.astype(jnp.bfloat16), "col", split_axis=0, concat_axis=2, tiled=True
    )
    return ladder


def solution(mesh):
    return jax.shard_map(
        on_device,
        mesh=mesh,
        in_specs=(P("col", None, "row"), P(None, "row", "col"), P()),
        out_specs=P(("row", "col"), None, None),
        check_vma=False,
    )
```

profile of v0, /device:TPU:0, one launch (start us, length us, event | category | flops | bytes accessed | tf_op | source)
XLA Modules:
  0.0 641.3 jit_solution(9710852810644849945)
XLA Ops:
  11.8 5.0 gather_fusion.3
  21.8 5.5 gather_fusion.9
  32.3 5.0 gather_fusion.15
  50.3 80.7 %all-gather.2.cloned.1.call-done = bf16[2048,8,512]{0,2,1:T(8,128)(2,1)} async-done(((bf16[128,8,512]{0,2,1:T(8,128)(2,1)}), bf16[2048,8,512]{0,2,1:T(8,128)(2,1)}) %all-gather.2.cloned.1.call-update) | async-done | bytes 16777232 | tf_op jit(solution)/shard_map/all_gather | solution.py:28
  131.0 11.7 %fusion.96 = (bf16[1024,8,512]{0,2,1:T(8,128)(2,1)}, bf16[1024,8,512]{0,2,1:T(8,128)(2,1)}) fusion(bf16[2048,8,512]{0,2,1:T(8,128)(2,1)} %all-gather.2.cloned.1.call-done), kind=kLoop, calls=%fused_computation.182 | loop fusion | bytes 33554432 | tf_op jit(solution)/shard_map/jit(_take)/gather | solution.py:15
  142.7 6.4 gather_fusion.1
  149.0 6.3 gather_fusion.2
  155.3 6.3 gather_fusion.4
  161.6 6.2 gather_fusion.5
  167.8 6.2 gather_fusion.7
  174.0 6.2 gather_fusion.8
  180.2 6.3 gather_fusion.10
  186.5 6.2 gather_fusion.11
  192.7 6.3 gather_fusion.13
  199.0 6.2 gather_fusion.14
  205.1 6.2 gather_fusion.16
  211.3 6.2 gather_fusion.17
  217.5 6.2 gather_fusion.19
  223.7 6.2 gather_fusion.20
  229.9 6.2 gather_fusion.22
  236.1 6.3 gather_fusion.23
  242.4 8.0 %fusion.55 = f32[2048,8,256]{2,0,1:T(8,128)} fusion(bf16[1024,4,512]{0,2,1:T(8,128)(2,1)} %bitcast.79, bf16[1024,4,512]{0,2,1:T(8,128)(2,1)} %bitcast.78, pred[4]{0:T(512)(128)(4,1)S(1)} %get-tuple-element.71, bf16[4,512,256]{2,1,0:T(8,128)(2,1)} %gather_fusion.3, pred[4]{0:T(512)(128)(4,1)S(1)} %get-tuple-element.55), kind=kOutput, calls=%fused_computation.88 | convolution fusion | flops 2168979456 | bytes 11534344 | tf_op jit(solution)/shard_map/dot_general | solution.py:19
  282.9 323.9 %reduce-scatter.2.cloned.1.call-done = f32[256,8,256]{2,0,1:T(8,128)} async-done(((f32[2048,8,256]{2,0,1:T(8,128)}), f32[256,8,256]{2,0,1:T(8,128)}) %reduce-scatter.2.cloned.1.call-update) | async-done | bytes 2097168 | tf_op jit(solution)/shard_map/reduce_scatter | solution.py:29
  609.0 24.3 %all_to_all.18 = bf16[256,8,256]{2,1,0:T(8,128)(2,1)S(1)} all-to-all(bf16[256,8,256]{2,1,0:T(8,128)(2,1)S(1)} %copy.32), channel_id=1, replica_groups=mesh['row'=8,'col'=16] {'col'}, dimensions={0} | all-to-all | bytes 2097152 | tf_op jit(solution)/shard_map/all_to_all | solution.py:35
  (73 shorter events, 63.7 us)
Async XLA Ops:
  6.5 124.4 %all-gather.2.cloned.1.call-start = ((), (), s32[]{:S(2)}) async-start(), calls=%async_computation.2 | async-start | bytes 17825792 | tf_op jit(solution)/shard_map/all_gather | solution.py:28
  9.2 597.5 %reduce-scatter.2.cloned.1.call-start = ((), (), s32[]{:S(2)}) async-start(), calls=%async_computation.3 | async-start | bytes 18874368 | tf_op jit(solution)/shard_map/reduce_scatter | solution.py:29
  242.4 8.1 %copy-start.12 = (bf16[4,1024,512]{1,2,0:T(8,128)(2,1)S(1)}, bf16[4,1024,512]{1,2,0:T(8,128)(2,1)}, u32[]{:S(2)}) copy-start(bf16[4,1024,512]{1,2,0:T(8,128)(2,1)} %gather_fusion.4) | copy-start | bytes 12582916
  242.4 8.1 %copy-start.13 = (bf16[4,1024,512]{1,2,0:T(8,128)(2,1)S(1)}, bf16[4,1024,512]{1,2,0:T(8,128)(2,1)}, u32[]{:S(2)}) copy-start(bf16[4,1024,512]{1,2,0:T(8,128)(2,1)} %gather_fusion.5) | copy-start | bytes 12582916
  242.4 8.1 %copy-start.16 = (bf16[4,512,256]{2,1,0:T(8,128)(2,1)S(1)}, bf16[4,512,256]{2,1,0:T(8,128)(2,1)}, u32[]{:S(2)}) copy-start(bf16[4,512,256]{2,1,0:T(8,128)(2,1)} %gather_fusion.6) | copy-start | bytes 3145732
  250.5 4.6 copy-start.10
  250.5 4.6 copy-start.11
  250.5 4.6 copy-start.17
  255.1 4.8 copy-start.8
  255.1 4.8 copy-start.9
  255.1 4.8 copy-start.14
  259.9 4.6 copy-start.6
  259.9 4.6 copy-start.7
  259.9 4.6 copy-start.15
  264.5 4.5 copy-start.4
  264.5 4.5 copy-start.5
  269.1 4.5 copy-start.2
  269.1 4.5 copy-start.3
  273.6 4.8 copy-start
  273.6 4.8 copy-start.1
Sparse Core Ops, SparseCore 0:
  9.6 121.2 all-gather.1
  283.0 323.6 reduce-scatter.1
where the time goes:
time: 643 us; the launch traced here: 641 us
  waiting for transfers between devices  405 us (63%)
  local copies, waits for them, and re-layouts  155 us (24%)
  matrix products  40.2 us (6%)
  blocking collectives  24.3 us (4%)
  between operations  13.6 us (2%)
    reduce_scatter x1, waiting for transfers between devices, on_device(): lax.psum_scatter(contract(gathered, integrals, sorted_rows, sorted_blocks...  324 us
    gather x17, local copies, waits for them, and re-layouts, contract(): jnp.take(panel_rows, sorted_rows[lower:lower + per_column], axis=1)  111 us
    all_gather x1, waiting for transfers between devices, on_device(): gathered = lax.all_gather(amplitudes, 'col', axis=0, tiled=True)  80.7 us
    dot_general x8, matrix products, contract(): jnp.dot(left_rows, right_cols, preferred_element_type=jnp.float32)  40.2 us
    gather x8, local copies, waits for them, and re-layouts, contract(): jnp.take(integrals, sorted_blocks[lower:lower + per_column], axis=0)  37.5 us
    all_to_all x1, blocking collectives, on_device(): lax.all_to_all(summed.astype(jnp.bfloat16), 'col', split_axis=0, concat_a...  24.3 us
  transfers between devices with their start and end apart: 2, of which 2 were waited for; matrix products, arithmetic and copies ran while one was open for 6% of the time, Pallas kernels for 0%

commit v1 on v0

v1 whole, which is shorter than its diff:
```python
import functools

import jax
import jax.numpy as jnp
from jax import lax
from jax.experimental import pallas as pl
from jax.experimental.pallas import tpu as pltpu
from jax.sharding import PartitionSpec as P

PIECES = 4
STEP = 256.0
TOP = 32700.0
TAIL = 16


def table(target):
    pairs = []
    for z in range(4):
        for xl in range(2):
            for xh in range(2):
                for y in range(4):
                    for k in range(2):
                        src = (z * 2 + xl) * 16 + xh * 8 + y * 2 + k
                        z2, xl2, xh2, y2, k2 = target(z, xl, xh, y, k)
                        dst = ((z2 % 4) * 2 + xl2) * 16 + xh2 * 8 + (y2 % 4) * 2 + k2
                        pairs.append((src, dst))
    return pairs


def way(k):
    return 1 - 2 * k


CORE = table(lambda z, xl, xh, y, k: (z, xl, xh, y, 1 - k))
X_HI = table(lambda z, xl, xh, y, k: (z, xl, 1 - xh, y, k))
Y_FORE = table(lambda z, xl, xh, y, k: (z, xl, xh, y + way(k), k))
Y_BACK = table(lambda z, xl, xh, y, k: (z, xl, xh, y - way(k), k))
Z_FORE = table(lambda z, xl, xh, y, k: (z + way(k), xl, xh, y, k))
Z_BACK = table(lambda z, xl, xh, y, k: (z - way(k), xl, xh, y, k))
X_SAME = table(lambda z, xl, xh, y, k: (z, xl, k, y, xh))
X_OTHER = table(lambda z, xl, xh, y, k: (z, 1 - xl, k, y, xh))
GROUPS = [list(range(8)), list(range(8, 16))]


def move(array, pairs):
    return lax.ppermute(array, ("row", "col"), pairs)


def encode(values):
    top = jnp.max(jnp.abs(values), axis=0, keepdims=True)
    code = jnp.ceil(jnp.log2(jnp.maximum(top, 1e-30)) * STEP) + 1.0
    scaled = jnp.round(values * (jnp.exp2(code * (-1.0 / STEP)) * TOP))
    return scaled.astype(jnp.int32).astype(jnp.int16), code


def scales(message_ref):
    rows = message_ref.shape[0]
    codes = message_ref[rows - TAIL :, :].astype(jnp.int32).astype(jnp.float32)
    return jnp.exp2(codes * (1.0 / STEP)) * (1.0 / TOP)


def decode(message_ref, scale, group, rows):
    held = message_ref[group * rows : (group + 1) * rows, :]
    return held.astype(jnp.int32).astype(jnp.float32) * scale[group : group + 1, :]


def put_codes(message_ref, codes):
    rows, width = message_ref.shape
    codes = codes + [jnp.zeros((1, width), jnp.float32)] * (TAIL - len(codes))
    block = jnp.concatenate(codes, axis=0)
    message_ref[rows - TAIL :, :] = block.astype(jnp.int32).astype(jnp.int16)


def partial_kernel(blk, prow, pos, a0, a1, a2, a3, *rest):
    v_own, v_other = rest[0:4], rest[4:8]
    far_ref, back_ref, own_ref, next_ref, held, far_codes, back_codes = rest[8:]
    q = pl.program_id(0)
    rows = a0.shape[2]
    width = held.shape[2]
    half = width // 2
    for part, v in enumerate((v_own, v_other)):
        total = None
        for j in range(4):
            tile = prow[q * 4 + j]
            left = jnp.concatenate([a[s, tile] for a in (a0, a1, a2, a3) for s in range(2)], axis=0)
            term = jnp.dot(left, v[j][0], preferred_element_type=jnp.float32)
            total = term if total is None else total + term
        for s in range(8):
            held[pos[s], :, part * half : (part + 1) * half] = total[s * rows : (s + 1) * rows]
    own_ref[...] = held[0:2]
    next_ref[...] = held[2:4]
    for g in range(2):
        at = pl.ds(pl.multiple_of((q * 2 + g) * rows, rows), rows)
        for ref, codes, slot in ((far_ref, far_codes, 4), (back_ref, back_codes, 6)):
            message, code = encode(held[slot + g])
            ref[at, :] = message
            codes[pl.ds(q * 2 + g, 1), :] = code

    @pl.when(q == pl.num_programs(0) - 1)
    def _():
        for ref, codes in ((far_ref, far_codes), (back_ref, back_codes)):
            last = ref.shape[0] - TAIL
            ref[last:, :] = codes[...].astype(jnp.int32).astype(jnp.int16)


def relay_kernel(next_ref, came_ref, out_ref):
    groups, rows, _ = next_ref.shape
    scale = scales(came_ref)
    codes = []
    for g in range(groups):
        total = next_ref[g] + decode(came_ref, scale, g, rows)
        out_ref[g * rows : (g + 1) * rows, :], code = encode(total)
        codes.append(code)
    put_codes(out_ref, codes)


def gather_kernel(own_ref, came_ref, back_ref, same_ref, other_ref):
    groups, rows, _ = own_ref.shape
    came_scale, back_scale = scales(came_ref), scales(back_ref)
    codes = ([], [])
    for g in range(groups):
        total = own_ref[g] + decode(came_ref, came_scale, g, rows) + decode(back_ref, back_scale, g, rows)
        message, code = encode(total)
        at = g // 2
        (same_ref, other_ref)[g % 2][at * rows : (at + 1) * rows, :] = message
        codes[g % 2].append(code)
    put_codes(same_ref, codes[0])
    put_codes(other_ref, codes[1])


def finish_kernel(swap, same_ref, other_ref, out_ref):
    tiles, rows, width = out_ref.shape
    half = width // 2
    same_scale, other_scale = scales(same_ref), scales(other_ref)
    for q in range(tiles):
        total = decode(same_ref, same_scale, q, rows) + decode(other_ref, other_scale, q, rows)
        turned = jnp.concatenate([total[:, half:], total[:, :half]], axis=1)
        out_ref[q] = jnp.where(swap[0] == 1, turned, total).astype(out_ref.dtype)


LIMIT = 48 * 2**20


def partial(blk, prow, pos, gathered, v_own, v_other):
    _, tiles, rows, depth = gathered[0].shape
    half = v_own.shape[2]
    width = 2 * half
    groups = 2 * tiles

    def whole(shape):
        return pl.BlockSpec(shape, lambda q, *_: (0,) * len(shape))

    def block(j):
        return pl.BlockSpec((1, depth, half), lambda q, blk, prow, pos, j=j: (blk[q * 4 + j], 0, 0))

    message = jax.ShapeDtypeStruct((groups * rows + TAIL, width), jnp.int16)
    kept = jax.ShapeDtypeStruct((groups, rows, width), jnp.float32)
    flops = 2 * 8 * rows * 4 * depth * width * tiles
    return pl.pallas_call(
        partial_kernel,
        grid_spec=pltpu.PrefetchScalarGridSpec(
            num_scalar_prefetch=3,
            grid=(tiles,),
            in_specs=[whole(gathered[0].shape)] * 4 + [block(j) for j in range(4)] * 2,
            out_specs=[whole(message.shape)] * 2 + [pl.BlockSpec((2, rows, width), lambda q, *_: (q, 0, 0))] * 2,
            scratch_shapes=[
                pltpu.VMEM((8, rows, width), jnp.float32),
                pltpu.VMEM((TAIL, width), jnp.float32),
                pltpu.VMEM((TAIL, width), jnp.float32),
            ],
        ),
        out_shape=[message, message, kept, kept],
        compiler_params=pltpu.CompilerParams(vmem_limit_bytes=LIMIT),
        cost_estimate=pl.CostEstimate(flops=flops, bytes_accessed=24 * 2**20, transcendentals=0),
        name="partial",
    )(blk, prow, pos, *gathered, *[v_own] * 4, *[v_other] * 4)


def simple(kernel, outs, args, name, scalars=0):
    vmem = pl.BlockSpec(memory_space=pltpu.VMEM)
    smem = pl.BlockSpec(memory_space=pltpu.SMEM)
    return pl.pallas_call(
        kernel,
        out_shape=outs,
        in_specs=[smem] * scalars + [vmem] * (len(args) - scalars),
        out_specs=jax.tree.map(lambda _: vmem, outs),
        compiler_params=pltpu.CompilerParams(vmem_limit_bytes=LIMIT),
        cost_estimate=pl.CostEstimate(flops=2**22, bytes_accessed=2**22, transcendentals=0),
        name=name,
    )(*args)


def on_device(amplitudes, integrals, blocks):
    pairs, tiles, depth = amplitudes.shape
    half = integrals.shape[2]
    width = 2 * half
    per = pairs // 8 // PIECES
    rows = 8 * per
    row, col = lax.axis_index("row"), lax.axis_index("col")
    z, x_lo = row // 2, row % 2
    x_hi, y, core = col // 8, (col // 2) % 4, col % 2
    turn = 1 - 2 * core

    key = blocks[:, 1] * 32 + jnp.arange(32, dtype=jnp.int32)
    rank = jnp.sum((key[None, :] < key[:, None]).astype(jnp.int32), axis=1)
    hit = (rank[None, :] == jnp.arange(32, dtype=jnp.int32)[:, None]).astype(jnp.int32)
    blk = jnp.sum(hit * jnp.arange(32, dtype=jnp.int32)[None, :], axis=1)
    prow = jnp.sum(hit * blocks[:, 0][None, :], axis=1)

    slots = []
    for shift in (0, -turn, turn, 2):
        for flip in (0, 1):
            from_y = (y + shift + 4) % 4
            from_x = x_hi ^ flip
            to_z = 2 * from_x + from_y // 2
            ahead = ((to_z - z) * turn + 8) % 4
            slots.append(ahead * 2 + ((from_y % 2) ^ x_lo))
    pos = jnp.stack(slots).astype(jnp.int32)
    swap = x_hi.astype(jnp.int32).reshape(1)

    shards = amplitudes.reshape(8, PIECES, per, tiles, depth).transpose(1, 3, 0, 2, 4)
    shards = shards.reshape(PIECES, 1, tiles, rows, depth)
    v_other = move(integrals, CORE)

    message = jax.ShapeDtypeStruct((2 * tiles * rows + TAIL, width), jnp.int16)
    small = jax.ShapeDtypeStruct((tiles * rows + TAIL, width), jnp.int16)
    outs = []
    for p in range(PIECES):
        own = shards[p]
        a0 = jnp.concatenate([own, move(own, X_HI)], axis=0)
        a1 = move(a0, Y_FORE)
        a2 = move(a0, Y_BACK)
        a3 = move(a1, Y_FORE)
        far, back, kept, nxt = partial(blk, prow, pos, (a0, a1, a2, a3), integrals, v_other)
        came = move(far, Z_FORE)
        back = move(back, Z_BACK)
        relayed = simple(relay_kernel, message, (nxt, came), "relay")
        came = move(relayed, Z_FORE)
        same, other = simple(gather_kernel, [small, small], (kept, came, back), "collect")
        same = move(same, X_SAME)
        other = move(other, X_OTHER)
        done = simple(
            finish_kernel,
            jax.ShapeDtypeStruct((tiles, rows, width), jnp.bfloat16),
            (swap, same, other),
            "finish",
            scalars=1,
        )
        outs.append(done.reshape(tiles, 8, per, width))
    done = jnp.stack(outs, axis=2).reshape(tiles, 8, PIECES * per, width).transpose(1, 2, 0, 3)
    done = lax.all_to_all(done, "col", 0, 0, axis_index_groups=GROUPS, tiled=True)
    done = done.reshape(4, 2, PIECES * per, tiles, width).transpose(2, 3, 1, 0, 4)
    return done.reshape(PIECES * per, tiles, 8 * width)


def solution(mesh):
    return jax.shard_map(
        on_device,
        mesh=mesh,
        in_specs=(P("col", None, "row"), P(None, "row", "col"), P()),
        out_specs=P(("row", "col"), None, None),
        check_vma=False,
    )
```

time: 643 us -> 206 us (0.32)
  waiting for transfers between devices: 405 us -> 64.2 us
  local copies, waits for them, and re-layouts: 155 us -> 8.87 us
  Pallas kernels: 0 us -> 56.2 us
  starting transfers between devices: 0.04 us -> 49.1 us
  matrix products: 40.2 us -> 0 us
  between operations: 13.6 us -> 0.29 us
    reduce_scatter x1 -> x0, waiting for transfers between devices: 324 us -> none  [on_device(): lax.psum_scatter(contract(gathered, integrals, sorted_rows, sorted_blocks...]
    gather x26 -> x0, local copies, waits for them, and re-layouts: 150 us -> none  [the longest x17 111 us: contract(): jnp.take(panel_rows, sorted_rows[lower:lower + per_column], axis=1)]
    all_gather x1 -> x0, waiting for transfers between devices: 80.7 us -> none  [on_device(): gathered = lax.all_gather(amplitudes, 'col', axis=0, tiled=True)]
    ppermute x0 -> x37, waiting for transfers between devices: none -> 64.2 us  [move(): return lax.ppermute(array, ('row', 'col'), pairs)]
    pallas_call x0 -> x16, Pallas kernels: none -> 56.2 us  [the longest x4 49.2 us: partial(): pl.pallas_call(partial_kernel, grid_spec=pltpu.PrefetchScalarGridSpec(num...]
    ppermute x0 -> x37, starting transfers between devices: none -> 49.1 us  [move(): return lax.ppermute(array, ('row', 'col'), pairs)]
    dot_general x8 -> x0, matrix products: 40.2 us -> none  [contract(): jnp.dot(left_rows, right_cols, preferred_element_type=jnp.float32)]
  transfers between devices with their start and end apart: 2 -> 37, of which waited for: 2 -> 13; matrix products, arithmetic and copies ran while one was open for 6% -> 3% of each run, Pallas kernels for 0% -> 27%
where the time goes in v1:
time: 206 us; the launch traced here: 205 us
  waiting for transfers between devices  64.2 us (31%)
  Pallas kernels  56.2 us (27%)
  starting transfers between devices  49.1 us (24%)
  blocking collectives  24.9 us (12%)
  local copies, waits for them, and re-layouts  8.87 us (4%)
    ppermute x37, waiting for transfers between devices, move(): return lax.ppermute(array, ('row', 'col'), pairs)  64.2 us
    pallas_call x4, Pallas kernels, partial(): pl.pallas_call(partial_kernel, grid_spec=pltpu.PrefetchScalarGridSpec(num...  49.2 us
    ppermute x37, starting transfers between devices, move(): return lax.ppermute(array, ('row', 'col'), pairs)  49.1 us
    all_to_all x1, blocking collectives, on_device(): lax.all_to_all(done, 'col', 0, 0, axis_index_groups=GROUPS, tiled=True)  24.9 us
    pallas_call x12, Pallas kernels, simple(): pl.pallas_call(kernel, out_shape=outs, in_specs=[smem] * scalars + [vmem]...  6.94 us
  transfers between devices with their start and end apart: 37, of which 13 were waited for; matrix products, arithmetic and copies ran while one was open for 3% of the time, Pallas kernels for 27%

profile of v1, /device:TPU:0, one launch (start us, length us, event | category | flops | bytes accessed | tf_op | source)
XLA Modules:
  0.0 204.7 jit_solution(6712878271310921838)
XLA Ops:
  2.5 3.2 %collective-permute-start = (bf16[1,8,32,512]{3,2,1,0:T(8,128)(2,1)S(1)}, bf16[1,8,32,512]{3,2,1,0:T(8,128)(2,1)S(1)}, u32[]{:S(2)}, u32[]{:S(2)}) collective-permute-start(bf16[1,8,32,512]{3,2,1,0:T(8,128)(2,1)S(1)} %squeeze.13), channel_id=1, source_target_pairs={{0,8},{1,9},{2,10},{3,11},{4,12},{5,13},{6,14},{7,15},{8,0},{9,1},... | collective-permute-start | bytes 786440 | tf_op jit(solution)/shard_map/ppermute | solution.py:46
  6.3 3.2 %collective-permute-start.19 = (bf16[1,8,32,512]{3,2,1,0:T(8,128)(2,1)S(1)}, bf16[1,8,32,512]{3,2,1,0:T(8,128)(2,1)S(1)}, u32[]{:S(2)}, u32[]{:S(2)}) collective-permute-start(bf16[1,8,32,512]{3,2,1,0:T(8,128)(2,1)S(1)} %squeeze.15), channel_id=1, source_target_pairs={{0,8},{1,9},{2,10},{3,11},{4,12},{5,13},{6,14},{7,15},{8,0},{9,1},... | collective-permute-start | bytes 786440 | tf_op jit(solution)/shard_map/ppermute | solution.py:46
  10.1 3.1 %collective-permute-done = bf16[1,8,32,512]{3,2,1,0:T(8,128)(2,1)S(1)} collective-permute-done((bf16[1,8,32,512]{3,2,1,0:T(8,128)(2,1)S(1)}, bf16[1,8,32,512]{3,2,1,0:T(8,128)(2,1)S(1)}, u32[]{:S(2)}, u32[]{:S(2)}) %collective-permute-start) | collective-permute-done | bytes 262176 | tf_op jit(solution)/shard_map/ppermute | solution.py:46
  15.7 3.1 %collective-permute-done.10 = bf16[1,8,32,512]{3,2,1,0:T(8,128)(2,1)S(1)} collective-permute-done((bf16[1,8,32,512]{3,2,1,0:T(8,128)(2,1)S(1)}, bf16[1,8,32,512]{3,2,1,0:T(8,128)(2,1)S(1)}, u32[]{:S(2)}, u32[]{:S(2)}) %collective-permute-start.10) | collective-permute-done | bytes 262176 | tf_op jit(solution)/shard_map/ppermute | solution.py:46
  18.8 3.1 %collective-permute-start.2 = (bf16[2,8,32,512]{3,2,1,0:T(8,128)(2,1)S(1)}, bf16[2,8,32,512]{3,2,1,0:T(8,128)(2,1)}, u32[]{:S(2)}, u32[]{:S(2)}) collective-permute-start(bf16[2,8,32,512]{3,2,1,0:T(8,128)(2,1)S(1)} %constant_dynamic-update-slice_fusion.a0), channel_id=1, source_target_pairs={{0,6},{1,3},{2,0},{3,5},{4,2},{5,7},{6,4},{7,1},{8,14},{9,11},{10,... | collective-permute-start | bytes 1572872 | tf_op jit(solution)/shard_map/ppermute | solution.py:46
  21.9 2.5 %collective-permute-done.19 = bf16[1,8,32,512]{3,2,1,0:T(8,128)(2,1)S(1)} collective-permute-done((bf16[1,8,32,512]{3,2,1,0:T(8,128)(2,1)S(1)}, bf16[1,8,32,512]{3,2,1,0:T(8,128)(2,1)S(1)}, u32[]{:S(2)}, u32[]{:S(2)}) %collective-permute-start.19) | collective-permute-done | bytes 262176 | tf_op jit(solution)/shard_map/ppermute | solution.py:46
  26.1 3.5 %collective-permute-done.28 = bf16[1,8,32,512]{3,2,1,0:T(8,128)(2,1)S(1)} collective-permute-done((bf16[1,8,32,512]{3,2,1,0:T(8,128)(2,1)S(1)}, bf16[1,8,32,512]{3,2,1,0:T(8,128)(2,1)S(1)}, u32[]{:S(2)}, u32[]{:S(2)}) %collective-permute-start.28) | collective-permute-done | bytes 262176 | tf_op jit(solution)/shard_map/ppermute | solution.py:46
  36.2 6.8 %collective-permute-done.20.a1 = bf16[2,8,32,512]{3,2,1,0:T(8,128)(2,1)S(1)} collective-permute-done((bf16[2,8,32,512]{3,2,1,0:T(8,128)(2,1)S(1)}, bf16[2,8,32,512]{3,2,1,0:T(8,128)(2,1)S(1)}, u32[]{:S(2)}, u32[]{:S(2)}) %collective-permute-start.20) | collective-permute-done | bytes 524320 | tf_op jit(solution)/shard_map/ppermute | solution.py:46
  44.6 7.2 %collective-permute-done.3.a3 = bf16[2,8,32,512]{3,2,1,0:T(8,128)(2,1)} collective-permute-done((bf16[2,8,32,512]{3,2,1,0:T(8,128)(2,1)}, bf16[2,8,32,512]{3,2,1,0:T(8,128)(2,1)}, u32[]{:S(2)}, u32[]{:S(2)}) %collective-permute-start.3) | collective-permute-done | bytes 524320 | tf_op jit(solution)/shard_map/ppermute | solution.py:46
  53.9 12.0 %partial.4 = (s16[528,512]{1,0:T(8,128)(2,1)S(1)}, s16[528,512]{1,0:T(8,128)(2,1)S(1)}, f32[16,32,512]{2,1,0:T(8,128)S(1)}, f32[16,32,512]{2,1,0:T(8,128)S(1)}) custom-call(s32[32]{0:T(128)S(1)} %get-tuple-element.54.blk, s32[32]{0:T(128)S(1)} %get-tuple-element.53.prow, s32[8]{0:T(128)S(1)} %stack.38.pos, ...), custom_call_target="tpu_custom_call" | custom-call | flops 4294967296 | bytes 25165824 | tf_op jit(solution)/shard_map/partial/pallas_call | solution.py:159
  65.9 3.2 %collective-permute-start.30 = (bf16[2,8,32,512]{3,2,1,0:T(8,128)(2,1)S(1)}, bf16[2,8,32,512]{3,2,1,0:T(8,128)(2,1)S(1)}, u32[]{:S(2)}, u32[]{:S(2)}) collective-permute-start(bf16[2,8,32,512]{3,2,1,0:T(8,128)(2,1)S(1)} %constant_dynamic-update-slice_fusion.6.a0), channel_id=1, source_target_pairs={{0,6},{1,3},{2,0},{3,5},{4,2},{5,7},{6,4},{7,1},{8,14},{9,11},{10,... | collective-permute-start | bytes 1572872 | tf_op jit(solution)/shard_map/ppermute | solution.py:46
  71.0 12.8 %partial.5 = (s16[528,512]{1,0:T(8,128)(2,1)}, s16[528,512]{1,0:T(8,128)(2,1)}, f32[16,32,512]{2,1,0:T(8,128)S(1)}, f32[16,32,512]{2,1,0:T(8,128)S(1)}) custom-call(s32[32]{0:T(128)S(1)} %get-tuple-element.54.blk, s32[32]{0:T(128)S(1)} %get-tuple-element.53.prow, s32[8]{0:T(128)S(1)} %stack.38.pos, ...), custom_call_target="tpu_custom_call" | custom-call | flops 4294967296 | bytes 25165824 | tf_op jit(solution)/shard_map/partial/pallas_call | solution.py:159
  86.1 12.0 %partial.6 = (s16[528,512]{1,0:T(8,128)(2,1)}, s16[528,512]{1,0:T(8,128)(2,1)S(1)}, f32[16,32,512]{2,1,0:T(8,128)S(1)}, f32[16,32,512]{2,1,0:T(8,128)S(1)}) custom-call(s32[32]{0:T(128)S(1)} %get-tuple-element.54.blk, s32[32]{0:T(128)S(1)} %get-tuple-element.53.prow, s32[8]{0:T(128)S(1)} %stack.38.pos, ...), custom_call_target="tpu_custom_call" | custom-call | flops 4294967296 | bytes 25165824 | tf_op jit(solution)/shard_map/partial/pallas_call | solution.py:159
  98.1 3.3 %collective-permute-start.16 = (s16[528,512]{1,0:T(8,128)(2,1)}, s16[528,512]{1,0:T(8,128)(2,1)S(1)}, u32[]{:S(2)}, u32[]{:S(2)}) collective-permute-start(s16[528,512]{1,0:T(8,128)(2,1)} %get-tuple-element.38), channel_id=1, source_target_pairs={{0,96},{1,33},{2,98},{3,35},{4,100},{5,37},{6,102},{7,39},{8,104},... | collective-permute-start | bytes 1622024 | tf_op jit(solution)/shard_map/ppermute | solution.py:46
  103.2 12.4 %partial.7 = (s16[528,512]{1,0:T(8,128)(2,1)}, s16[528,512]{1,0:T(8,128)(2,1)S(1)}, f32[16,32,512]{2,1,0:T(8,128)S(1)}, f32[16,32,512]{2,1,0:T(8,128)S(1)}) custom-call(s32[32]{0:T(128)S(1)} %get-tuple-element.54.blk, s32[32]{0:T(128)S(1)} %get-tuple-element.53.prow, s32[8]{0:T(128)S(1)} %stack.38.pos, ...), custom_call_target="tpu_custom_call" | custom-call | flops 4294967296 | bytes 25165824 | tf_op jit(solution)/shard_map/partial/pallas_call | solution.py:159
  119.7 2.5 %collective-permute-start.15 = (s16[528,512]{1,0:T(8,128)(2,1)}, s16[528,512]{1,0:T(8,128)(2,1)S(1)}, u32[]{:S(2)}, u32[]{:S(2)}) collective-permute-start(s16[528,512]{1,0:T(8,128)(2,1)} %relay.5), channel_id=1, source_target_pairs={{0,32},{1,97},{2,34},{3,99},{4,36},{5,101},{6,38},{7,103},{8,40},{... | collective-permute-start | bytes 1622024 | tf_op jit(solution)/shard_map/ppermute | solution.py:46
  123.8 5.2 %collective-permute-done.32.came_ref = s16[528,512]{1,0:T(8,128)(2,1)S(1)} collective-permute-done((s16[528,512]{1,0:T(8,128)(2,1)}, s16[528,512]{1,0:T(8,128)(2,1)S(1)}, u32[]{:S(2)}, u32[]{:S(2)}) %collective-permute-start.32) | collective-permute-done | bytes 540704 | tf_op jit(solution)/shard_map/ppermute | solution.py:46
  129.4 11.2 %collective-permute-done.6.came_ref = s16[528,512]{1,0:T(8,128)(2,1)S(1)} collective-permute-done((s16[528,512]{1,0:T(8,128)(2,1)S(1)}, s16[528,512]{1,0:T(8,128)(2,1)S(1)}, u32[]{:S(2)}, u32[]{:S(2)}) %collective-permute-start.6) | collective-permute-done | bytes 540704 | tf_op jit(solution)/shard_map/ppermute | solution.py:46
  141.1 8.6 %collective-permute-done.15.came_ref = s16[528,512]{1,0:T(8,128)(2,1)S(1)} collective-permute-done((s16[528,512]{1,0:T(8,128)(2,1)}, s16[528,512]{1,0:T(8,128)(2,1)S(1)}, u32[]{:S(2)}, u32[]{:S(2)}) %collective-permute-start.15) | collective-permute-done | bytes 540704 | tf_op jit(solution)/shard_map/ppermute | solution.py:46
  153.2 2.3 %collective-permute-done.24.came_ref = s16[528,512]{1,0:T(8,128)(2,1)S(1)} collective-permute-done((s16[528,512]{1,0:T(8,128)(2,1)S(1)}, s16[528,512]{1,0:T(8,128)(2,1)S(1)}, u32[]{:S(2)}, u32[]{:S(2)}) %collective-permute-start.24) | collective-permute-done | bytes 540704 | tf_op jit(solution)/shard_map/ppermute | solution.py:46
  158.4 2.9 %collective-permute-done.33.came_ref = s16[528,512]{1,0:T(8,128)(2,1)S(1)} collective-permute-done((s16[528,512]{1,0:T(8,128)(2,1)S(1)}, s16[528,512]{1,0:T(8,128)(2,1)S(1)}, u32[]{:S(2)}, u32[]{:S(2)}) %collective-permute-start.33) | collective-permute-done | bytes 540704 | tf_op jit(solution)/shard_map/ppermute | solution.py:46
  168.5 2.8 %collective-permute-done.27.other_ref = s16[272,512]{1,0:T(8,128)(2,1)S(1)} collective-permute-done((s16[272,512]{1,0:T(8,128)(2,1)}, s16[272,512]{1,0:T(8,128)(2,1)S(1)}, u32[]{:S(2)}, u32[]{:S(2)}) %collective-permute-start.27) | collective-permute-done | bytes 278560 | tf_op jit(solution)/shard_map/ppermute | solution.py:46
  171.6 5.1 %collective-permute-done.36.other_ref = s16[272,512]{1,0:T(8,128)(2,1)S(1)} collective-permute-done((s16[272,512]{1,0:T(8,128)(2,1)}, s16[272,512]{1,0:T(8,128)(2,1)S(1)}, u32[]{:S(2)}, u32[]{:S(2)}) %collective-permute-start.36) | collective-permute-done | bytes 278560 | tf_op jit(solution)/shard_map/ppermute | solution.py:46
  177.4 24.9 %all_to_all.5 = bf16[8,16,8,512]{3,1,2,0:T(8,128)(2,1)S(1)} all-to-all(bf16[8,16,8,512]{3,1,2,0:T(8,128)(2,1)S(1)} %copy.31), channel_id=1, replica_groups={{0,1,2,3,4,5,6,7},{8,9,10,11,12,13,14,15},{16,17,18,19,20,21,22,23},{24..., dimensions={0} | all-to-all | bytes 2097152 | tf_op jit(solution)/shard_map/all_to_all | solution.py:251
  (106 shorter events, 47.7 us)
Async XLA Ops:
  0.0 53.7 %collective-permute-start.4 = (bf16[32,512,256]{2,1,0:T(8,128)(2,1)}, bf16[32,512,256]{2,1,0:T(8,128)(2,1)}, u32[]{:S(2)}, u32[]{:S(2)}) collective-permute-start(bf16[32,512,256]{2,1,0:T(8,128)(2,1)} %rest_3_.7), channel_id=1, source_target_pairs={{0,1},{1,0},{2,3},{3,2},{4,5},{5,4},{6,7},{7,6},{8,9},{9,8},{10,11... | collective-permute-start | bytes 25165832 | tf_op jit(solution)/shard_map/ppermute | solution.py:46
  6.3 18.1 %collective-permute-start.19 = (bf16[1,8,32,512]{3,2,1,0:T(8,128)(2,1)S(1)}, bf16[1,8,32,512]{3,2,1,0:T(8,128)(2,1)S(1)}, u32[]{:S(2)}, u32[]{:S(2)}) collective-permute-start(bf16[1,8,32,512]{3,2,1,0:T(8,128)(2,1)S(1)} %squeeze.15), channel_id=1, source_target_pairs={{0,8},{1,9},{2,10},{3,11},{4,12},{5,13},{6,14},{7,15},{8,0},{9,1},... | collective-permute-start | bytes 786440 | tf_op jit(solution)/shard_map/ppermute | solution.py:46
  9.6 20.1 %collective-permute-start.28 = (bf16[1,8,32,512]{3,2,1,0:T(8,128)(2,1)S(1)}, bf16[1,8,32,512]{3,2,1,0:T(8,128)(2,1)S(1)}, u32[]{:S(2)}, u32[]{:S(2)}) collective-permute-start(bf16[1,8,32,512]{3,2,1,0:T(8,128)(2,1)S(1)} %squeeze.16), channel_id=1, source_target_pairs={{0,8},{1,9},{2,10},{3,11},{4,12},{5,13},{6,14},{7,15},{8,0},{9,1},... | collective-permute-start | bytes 786440 | tf_op jit(solution)/shard_map/ppermute | solution.py:46
  13.2 18.1 %collective-permute-start.1 = (bf16[2,8,32,512]{3,2,1,0:T(8,128)(2,1)S(1)}, bf16[2,8,32,512]{3,2,1,0:T(8,128)(2,1)}, u32[]{:S(2)}, u32[]{:S(2)}) collective-permute-start(bf16[2,8,32,512]{3,2,1,0:T(8,128)(2,1)S(1)} %constant_dynamic-update-slice_fusion.a0), channel_id=1, source_target_pairs={{0,2},{1,7},{2,4},{3,1},{4,6},{5,3},{6,0},{7,5},{8,10},{9,15},{10,... | collective-permute-start | bytes 1572872 | tf_op jit(solution)/shard_map/ppermute | solution.py:46
  18.8 15.3 %collective-permute-start.2 = (bf16[2,8,32,512]{3,2,1,0:T(8,128)(2,1)S(1)}, bf16[2,8,32,512]{3,2,1,0:T(8,128)(2,1)}, u32[]{:S(2)}, u32[]{:S(2)}) collective-permute-start(bf16[2,8,32,512]{3,2,1,0:T(8,128)(2,1)S(1)} %constant_dynamic-update-slice_fusion.a0), channel_id=1, source_target_pairs={{0,6},{1,3},{2,0},{3,5},{4,2},{5,7},{6,4},{7,1},{8,14},{9,11},{10,... | collective-permute-start | bytes 1572872 | tf_op jit(solution)/shard_map/ppermute | solution.py:46
  31.3 20.6 %collective-permute-start.3 = (bf16[2,8,32,512]{3,2,1,0:T(8,128)(2,1)}, bf16[2,8,32,512]{3,2,1,0:T(8,128)(2,1)}, u32[]{:S(2)}, u32[]{:S(2)}) collective-permute-start(bf16[2,8,32,512]{3,2,1,0:T(8,128)(2,1)} %collective-permute-done.1.a1), channel_id=1, source_target_pairs={{0,2},{1,7},{2,4},{3,1},{4,6},{5,3},{6,0},{7,5},{8,10},{9,15},{10,... | collective-permute-start | bytes 1572872 | tf_op jit(solution)/shard_map/ppermute | solution.py:46
  34.1 31.8 %collective-permute-start.12 = (bf16[2,8,32,512]{3,2,1,0:T(8,128)(2,1)S(1)}, bf16[2,8,32,512]{3,2,1,0:T(8,128)(2,1)}, u32[]{:S(2)}, u32[]{:S(2)}) collective-permute-start(bf16[2,8,32,512]{3,2,1,0:T(8,128)(2,1)S(1)} %constant_dynamic-update-slice_fusion.2.a0), channel_id=1, source_target_pairs={{0,6},{1,3},{2,0},{3,5},{4,2},{5,7},{6,4},{7,1},{8,14},{9,11},{10,... | collective-permute-start | bytes 1572872 | tf_op jit(solution)/shard_map/ppermute | solution.py:46
  35.8 33.3 %collective-permute-start.29 = (bf16[2,8,32,512]{3,2,1,0:T(8,128)(2,1)S(1)}, bf16[2,8,32,512]{3,2,1,0:T(8,128)(2,1)}, u32[]{:S(2)}, u32[]{:S(2)}) collective-permute-start(bf16[2,8,32,512]{3,2,1,0:T(8,128)(2,1)S(1)} %constant_dynamic-update-slice_fusion.6.a0), channel_id=1, source_target_pairs={{0,2},{1,7},{2,4},{3,1},{4,6},{5,3},{6,0},{7,5},{8,10},{9,15},{10,... | collective-permute-start | bytes 1572872 | tf_op jit(solution)/shard_map/ppermute | solution.py:46
  43.0 26.1 %collective-permute-start.13 = (bf16[2,8,32,512]{3,2,1,0:T(8,128)(2,1)S(1)}, bf16[2,8,32,512]{3,2,1,0:T(8,128)(2,1)}, u32[]{:S(2)}, u32[]{:S(2)}) collective-permute-start(bf16[2,8,32,512]{3,2,1,0:T(8,128)(2,1)S(1)} %collective-permute-done.11.a1), channel_id=1, source_target_pairs={{0,2},{1,7},{2,4},{3,1},{4,6},{5,3},{6,0},{7,5},{8,10},{9,15},{10,... | collective-permute-start | bytes 1572872 | tf_op jit(solution)/shard_map/ppermute | solution.py:46
  51.9 32.0 %collective-permute-start.21 = (bf16[2,8,32,512]{3,2,1,0:T(8,128)(2,1)S(1)}, bf16[2,8,32,512]{3,2,1,0:T(8,128)(2,1)S(1)}, u32[]{:S(2)}, u32[]{:S(2)}) collective-permute-start(bf16[2,8,32,512]{3,2,1,0:T(8,128)(2,1)S(1)} %constant_dynamic-update-slice_fusion.4.a0), channel_id=1, source_target_pairs={{0,6},{1,3},{2,0},{3,5},{4,2},{5,7},{6,4},{7,1},{8,14},{9,11},{10,... | collective-permute-start | bytes 1572872 | tf_op jit(solution)/shard_map/ppermute | solution.py:46
  53.7 32.3 %collective-permute-start.22 = (bf16[2,8,32,512]{3,2,1,0:T(8,128)(2,1)S(1)}, bf16[2,8,32,512]{3,2,1,0:T(8,128)(2,1)S(1)}, u32[]{:S(2)}, u32[]{:S(2)}) collective-permute-start(bf16[2,8,32,512]{3,2,1,0:T(8,128)(2,1)S(1)} %collective-permute-done.20.a1), channel_id=1, source_target_pairs={{0,2},{1,7},{2,4},{3,1},{4,6},{5,3},{6,0},{7,5},{8,10},{9,15},{10,... | collective-permute-start | bytes 1572872 | tf_op jit(solution)/shard_map/ppermute | solution.py:46
  65.9 32.2 %collective-permute-start.30 = (bf16[2,8,32,512]{3,2,1,0:T(8,128)(2,1)S(1)}, bf16[2,8,32,512]{3,2,1,0:T(8,128)(2,1)S(1)}, u32[]{:S(2)}, u32[]{:S(2)}) collective-permute-start(bf16[2,8,32,512]{3,2,1,0:T(8,128)(2,1)S(1)} %constant_dynamic-update-slice_fusion.6.a0), channel_id=1, source_target_pairs={{0,6},{1,3},{2,0},{3,5},{4,2},{5,7},{6,4},{7,1},{8,14},{9,11},{10,... | collective-permute-start | bytes 1572872 | tf_op jit(solution)/shard_map/ppermute | solution.py:46
  69.1 32.3 %collective-permute-start.31 = (bf16[2,8,32,512]{3,2,1,0:T(8,128)(2,1)}, bf16[2,8,32,512]{3,2,1,0:T(8,128)(2,1)S(1)}, u32[]{:S(2)}, u32[]{:S(2)}) collective-permute-start(bf16[2,8,32,512]{3,2,1,0:T(8,128)(2,1)} %collective-permute-done.29.a1), channel_id=1, source_target_pairs={{0,2},{1,7},{2,4},{3,1},{4,6},{5,3},{6,0},{7,5},{8,10},{9,15},{10,... | collective-permute-start | bytes 1572872 | tf_op jit(solution)/shard_map/ppermute | solution.py:46
  69.1 46.6 %collective-permute-start.5 = (s16[528,512]{1,0:T(8,128)(2,1)S(1)}, s16[528,512]{1,0:T(8,128)(2,1)S(1)}, u32[]{:S(2)}, u32[]{:S(2)}) collective-permute-start(s16[528,512]{1,0:T(8,128)(2,1)S(1)} %get-tuple-element.31), channel_id=1, source_target_pairs={{0,32},{1,97},{2,34},{3,99},{4,36},{5,101},{6,38},{7,103},{8,40},{... | collective-permute-start | bytes 1622024 | tf_op jit(solution)/shard_map/ppermute | solution.py:46
  83.9 35.8 %collective-permute-start.7 = (s16[528,512]{1,0:T(8,128)(2,1)S(1)}, s16[528,512]{1,0:T(8,128)(2,1)S(1)}, u32[]{:S(2)}, u32[]{:S(2)}) collective-permute-start(s16[528,512]{1,0:T(8,128)(2,1)S(1)} %get-tuple-element.32), channel_id=1, source_target_pairs={{0,96},{1,33},{2,98},{3,35},{4,100},{5,37},{6,102},{7,39},{8,104},... | collective-permute-start | bytes 1622024 | tf_op jit(solution)/shard_map/ppermute | solution.py:46
  86.1 30.7 %collective-permute-start.14 = (s16[528,512]{1,0:T(8,128)(2,1)}, s16[528,512]{1,0:T(8,128)(2,1)S(1)}, u32[]{:S(2)}, u32[]{:S(2)}) collective-permute-start(s16[528,512]{1,0:T(8,128)(2,1)} %get-tuple-element.37), channel_id=1, source_target_pairs={{0,32},{1,97},{2,34},{3,99},{4,36},{5,101},{6,38},{7,103},{8,40},{... | collective-permute-start | bytes 1622024 | tf_op jit(solution)/shard_map/ppermute | solution.py:46
  98.1 24.0 %collective-permute-start.16 = (s16[528,512]{1,0:T(8,128)(2,1)}, s16[528,512]{1,0:T(8,128)(2,1)S(1)}, u32[]{:S(2)}, u32[]{:S(2)}) collective-permute-start(s16[528,512]{1,0:T(8,128)(2,1)} %get-tuple-element.38), channel_id=1, source_target_pairs={{0,96},{1,33},{2,98},{3,35},{4,100},{5,37},{6,102},{7,39},{8,104},... | collective-permute-start | bytes 1622024 | tf_op jit(solution)/shard_map/ppermute | solution.py:46
  102.2 20.7 %collective-permute-start.23 = (s16[528,512]{1,0:T(8,128)(2,1)}, s16[528,512]{1,0:T(8,128)(2,1)S(1)}, u32[]{:S(2)}, u32[]{:S(2)}) collective-permute-start(s16[528,512]{1,0:T(8,128)(2,1)} %get-tuple-element.43), channel_id=1, source_target_pairs={{0,32},{1,97},{2,34},{3,99},{4,36},{5,101},{6,38},{7,103},{8,40},{... | collective-permute-start | bytes 1622024 | tf_op jit(solution)/shard_map/ppermute | solution.py:46
  116.8 23.8 %collective-permute-start.6 = (s16[528,512]{1,0:T(8,128)(2,1)S(1)}, s16[528,512]{1,0:T(8,128)(2,1)S(1)}, u32[]{:S(2)}, u32[]{:S(2)}) collective-permute-start(s16[528,512]{1,0:T(8,128)(2,1)S(1)} %relay.4), channel_id=1, source_target_pairs={{0,32},{1,97},{2,34},{3,99},{4,36},{5,101},{6,38},{7,103},{8,40},{... | collective-permute-start | bytes 1622024 | tf_op jit(solution)/shard_map/ppermute | solution.py:46
  119.7 30.0 %collective-permute-start.15 = (s16[528,512]{1,0:T(8,128)(2,1)}, s16[528,512]{1,0:T(8,128)(2,1)S(1)}, u32[]{:S(2)}, u32[]{:S(2)}) collective-permute-start(s16[528,512]{1,0:T(8,128)(2,1)} %relay.5), channel_id=1, source_target_pairs={{0,32},{1,97},{2,34},{3,99},{4,36},{5,101},{6,38},{7,103},{8,40},{... | collective-permute-start | bytes 1622024 | tf_op jit(solution)/shard_map/ppermute | solution.py:46
  122.1 28.8 %collective-permute-start.25 = (s16[528,512]{1,0:T(8,128)(2,1)S(1)}, s16[528,512]{1,0:T(8,128)(2,1)S(1)}, u32[]{:S(2)}, u32[]{:S(2)}) collective-permute-start(s16[528,512]{1,0:T(8,128)(2,1)S(1)} %get-tuple-element.44), channel_id=1, source_target_pairs={{0,96},{1,33},{2,98},{3,35},{4,100},{5,37},{6,102},{7,39},{8,104},... | collective-permute-start | bytes 1622024 | tf_op jit(solution)/shard_map/ppermute | solution.py:46
  122.9 29.6 %collective-permute-start.34 = (s16[528,512]{1,0:T(8,128)(2,1)S(1)}, s16[528,512]{1,0:T(8,128)(2,1)S(1)}, u32[]{:S(2)}, u32[]{:S(2)}) collective-permute-start(s16[528,512]{1,0:T(8,128)(2,1)S(1)} %get-tuple-element.50), channel_id=1, source_target_pairs={{0,96},{1,33},{2,98},{3,35},{4,100},{5,37},{6,102},{7,39},{8,104},... | collective-permute-start | bytes 1622024 | tf_op jit(solution)/shard_map/ppermute | solution.py:46
  129.0 26.5 %collective-permute-start.24 = (s16[528,512]{1,0:T(8,128)(2,1)S(1)}, s16[528,512]{1,0:T(8,128)(2,1)S(1)}, u32[]{:S(2)}, u32[]{:S(2)}) collective-permute-start(s16[528,512]{1,0:T(8,128)(2,1)S(1)} %relay.6), channel_id=1, source_target_pairs={{0,32},{1,97},{2,34},{3,99},{4,36},{5,101},{6,38},{7,103},{8,40},{... | collective-permute-start | bytes 1622024 | tf_op jit(solution)/shard_map/ppermute | solution.py:46
  140.5 20.7 %collective-permute-start.33 = (s16[528,512]{1,0:T(8,128)(2,1)S(1)}, s16[528,512]{1,0:T(8,128)(2,1)S(1)}, u32[]{:S(2)}, u32[]{:S(2)}) collective-permute-start(s16[528,512]{1,0:T(8,128)(2,1)S(1)} %relay.7), channel_id=1, source_target_pairs={{0,32},{1,97},{2,34},{3,99},{4,36},{5,101},{6,38},{7,103},{8,40},{... | collective-permute-start | bytes 1622024 | tf_op jit(solution)/shard_map/ppermute | solution.py:46
  (17 other events, 184.3 us)

commit v2 on v1

v2 whole, which is shorter than its diff:
```python
import functools

import jax
import jax.numpy as jnp
from jax import lax
from jax.experimental import pallas as pl
from jax.experimental.pallas import tpu as pltpu
from jax.sharding import PartitionSpec as P

PIECES = (4, 4, 4, 4)
ORDER = (
    ("stage", 0),
    ("join", 1),
    ("multiply", 0),
    ("forward", 1),
    ("join", 2),
    ("multiply", 1),
    ("forward", 2),
    ("join", 3),
    ("relay", 0),
    ("multiply", 2),
    ("forward", 3),
    ("relay", 1),
    ("multiply", 3),
    ("collect", (0, 1)),
    ("relay", 2),
    ("finish", (0, 1)),
    ("relay", 3),
    ("collect", (2, 3)),
    ("finish", (2, 3)),
)
STEP = 256.0
TOP = 32700.0


def tail(groups):
    return (groups + 15) // 16 * 16


def table(target):
    pairs = []
    for z in range(4):
        for xl in range(2):
            for xh in range(2):
                for y in range(4):
                    for k in range(2):
                        src = (z * 2 + xl) * 16 + xh * 8 + y * 2 + k
                        z2, xl2, xh2, y2, k2 = target(z, xl, xh, y, k)
                        dst = ((z2 % 4) * 2 + xl2) * 16 + xh2 * 8 + (y2 % 4) * 2 + k2
                        pairs.append((src, dst))
    return pairs


def way(k):
    return 1 - 2 * k


CORE = table(lambda z, xl, xh, y, k: (z, xl, xh, y, 1 - k))
X_HI = table(lambda z, xl, xh, y, k: (z, xl, 1 - xh, y, k))
Y_FORE = table(lambda z, xl, xh, y, k: (z, xl, xh, y + way(k), k))
Y_BACK = table(lambda z, xl, xh, y, k: (z, xl, xh, y - way(k), k))
Z_FORE = table(lambda z, xl, xh, y, k: (z + way(k), xl, xh, y, k))
Z_BACK = table(lambda z, xl, xh, y, k: (z - way(k), xl, xh, y, k))
X_SAME = [table(lambda z, xl, xh, y, k, b=b: (z, xl, k, y, xh ^ b)) for b in range(2)]
X_OTHER = [table(lambda z, xl, xh, y, k, b=b: (z, 1 - xl, k, y, xh ^ b)) for b in range(2)]
Y_SHIFT = [table(lambda z, xl, xh, y, k, a=a: (z, xl, xh, y + a, k)) for a in range(4)]


def move(array, pairs):
    return lax.ppermute(array, ("row", "col"), pairs)


def encode(values):
    top = jnp.max(jnp.abs(values), axis=0, keepdims=True)
    code = jnp.ceil(jnp.log2(jnp.maximum(top, 1e-30)) * STEP) + 1.0
    scaled = jnp.round(values * (jnp.exp2(code * (-1.0 / STEP)) * TOP))
    return scaled.astype(jnp.int32).astype(jnp.int16), code


def scales(message_ref, groups):
    codes = message_ref[message_ref.shape[0] - tail(groups) :, :]
    return jnp.exp2(codes.astype(jnp.int32).astype(jnp.float32) * (1.0 / STEP)) * (1.0 / TOP)


def decode(message_ref, scale, group, start, rows):
    held = message_ref[start : start + rows, :]
    return held.astype(jnp.int32).astype(jnp.float32) * scale[group : group + 1, :]


def put_codes(message_ref, codes):
    rows, width = message_ref.shape
    more = tail(len(codes)) - len(codes)
    block = jnp.concatenate(codes + [jnp.zeros((1, width), jnp.float32)] * more, axis=0)
    message_ref[rows - tail(len(codes)) :, :] = block.astype(jnp.int32).astype(jnp.int16)


def stage_kernel(where, own_ref, came_ref, *rest):
    out_ref, sems = rest[-2:]
    half = own_ref.shape[2]
    core = where[2]
    copies = []
    for n, (ref, side) in enumerate(((own_ref, core), (came_ref, 1 - core))):
        at = pl.ds(pl.multiple_of(side * half, half), half)
        copies.append(pltpu.make_async_copy(ref, out_ref.at[:, :, at], sems.at[n]))
    for copy in copies:
        copy.start()
    for copy in copies:
        copy.wait()


def partial_kernel(blk, prow, pos, a0, a1, a2, a3, v_ref, *rest):
    far_ref, back_ref, own_ref, next_ref, held, far_codes, back_codes = rest[-7:]
    q = pl.program_id(0)
    rows = a0.shape[2]
    total = None
    for j in range(4):
        tile = prow[q * 4 + j]
        left = jnp.concatenate([a[s, tile] for a in (a0, a1, a2, a3) for s in range(2)], axis=0)
        term = jnp.dot(left, v_ref[blk[q * 4 + j]], preferred_element_type=jnp.float32)
        total = term if total is None else total + term
    for s in range(8):
        held[pos[s]] = total[s * rows : (s + 1) * rows]
    own_ref[...] = held[0:2]
    next_ref[...] = held[2:4]
    for g in range(2):
        at = pl.ds(pl.multiple_of((q * 2 + g) * rows, rows), rows)
        for ref, codes, slot in ((far_ref, far_codes, 4), (back_ref, back_codes, 6)):
            message, code = encode(held[slot + g])
            ref[at, :] = message
            codes[pl.ds(q * 2 + g, 1), :] = code

    @pl.when(q == pl.num_programs(0) - 1)
    def _():
        for ref, codes in ((far_ref, far_codes), (back_ref, back_codes)):
            last = ref.shape[0] - codes.shape[0]
            ref[last:, :] = codes[...].astype(jnp.int32).astype(jnp.int16)


def join_kernel(own_ref, came_ref, *rest):
    rest[-1][0] = own_ref[0]
    rest[-1][1] = came_ref[0]


def copy_kernel(in_ref, *rest):
    rest[-1][...] = in_ref[...]


def relay_kernel(next_ref, came_ref, *rest):
    out_ref = rest[-1]
    groups, rows, _ = next_ref.shape
    scale = scales(came_ref, groups)
    codes = []
    for g in range(groups):
        total = next_ref[g] + decode(came_ref, scale, g, g * rows, rows)
        out_ref[g * rows : (g + 1) * rows, :], code = encode(total)
        codes.append(code)
    put_codes(out_ref, codes)


def collect_kernel(count, x_hi, *refs):
    pieces, outs = [refs[3 * i : 3 * i + 3] for i in range(count)], refs[-4:]
    codes, at, flip = ([], []), 0, x_hi[0] == 1
    for own_ref, came_ref, back_ref in pieces:
        groups, rows, _ = own_ref.shape
        came_scale, back_scale = scales(came_ref, groups), scales(back_ref, groups)
        half = rows // 2
        for g in range(groups):
            total = own_ref[g] + decode(came_ref, came_scale, g, g * rows, rows)
            total = total + decode(back_ref, back_scale, g, g * rows, rows)
            message, code = encode(total)
            first, second = message[:half].astype(jnp.int32), message[half:].astype(jnp.int32)
            near = slice(at, at + half)
            outs[2 * (g % 2)][near, :] = jnp.where(flip, second, first).astype(jnp.int16)
            outs[2 * (g % 2) + 1][near, :] = jnp.where(flip, first, second).astype(jnp.int16)
            codes[g % 2].append(code)
            at += half * (g % 2)
    for k in range(4):
        put_codes(outs[k], codes[k // 2])


def finish_kernel(pers, where, *refs):
    sums, out_ref = refs[:4], refs[-1]
    y, core = where[1], where[2]
    _, _, tiles, width2 = out_ref.shape
    width = width2 // 2
    groups = tiles * len(pers)
    scale = [scales(ref, groups) for ref in sums]
    start = base = 0
    for n, per in enumerate(pers):
        rows = 4 * per
        parts = []
        for b in range(2):
            stack = []
            for q in range(tiles):
                g, near = n * tiles + q, start + q * rows
                total = decode(sums[b], scale[b], g, near, rows) + decode(sums[2 + b], scale[2 + b], g, near, rows)
                stack.append(total)
            parts.append(jnp.swapaxes(jnp.stack(stack, axis=0), 0, 1))
        first = jnp.where(core == 0, parts[0], parts[1]).astype(out_ref.dtype)
        second = jnp.where(core == 0, parts[1], parts[0]).astype(out_ref.dtype)
        for to_y in range(4):
            slot = lax.rem(to_y - y + 4, 4)
            out_ref[slot, base : base + per, :, :width] = first[to_y * per : (to_y + 1) * per]
            out_ref[slot, base : base + per, :, width:] = second[to_y * per : (to_y + 1) * per]
        start += tiles * rows
        base += per


def place_kernel(count, where, *refs):
    parts, out_ref = refs[:count], refs[-1]
    base = 0
    for n in range(0, len(parts), 4):
        per = parts[n].shape[0]
        width = parts[n].shape[-1] // 2
        for a in range(4):
            from_y = lax.rem(where[1] - a + 4, 4)
            held = parts[n + a][...]
            for x in range(2):
                at = pl.ds(pl.multiple_of((x * 4 + from_y) * width, width), width)
                out_ref[base : base + per, :, at] = held[:, :, x * width : (x + 1) * width]
        base += per


LIMIT = 14 * 2**20


def stage(where, own, came):
    blocks, depth, half = own.shape
    return pl.pallas_call(
        stage_kernel,
        out_shape=pltpu.VMEM((blocks, depth, 2 * half), own.dtype),
        in_specs=[pl.BlockSpec(memory_space=pltpu.SMEM)] + [pl.BlockSpec(memory_space=pl.ANY)] * 2,
        out_specs=pl.BlockSpec(memory_space=pltpu.VMEM),
        scratch_shapes=[pltpu.SemaphoreType.DMA((2,))],
        compiler_params=pltpu.CompilerParams(vmem_limit_bytes=LIMIT),
        cost_estimate=pl.CostEstimate(flops=0, bytes_accessed=16 * 2**20, transcendentals=0),
        name="stage",
    )(where, pltpu.with_memory_space_constraint(own, pltpu.HBM), pltpu.with_memory_space_constraint(came, pltpu.HBM))


def partial(blk, prow, pos, gathered, staged):
    _, tiles, rows, depth = gathered[0].shape
    width = staged.shape[2]
    groups = 2 * tiles

    def whole(shape):
        return pl.BlockSpec(shape, lambda q, *_: (0,) * len(shape))

    message = jax.ShapeDtypeStruct((groups * rows + tail(groups), width), jnp.int16)
    kept = jax.ShapeDtypeStruct((groups, rows, width), jnp.float32)
    flops = 2 * 8 * rows * 4 * depth * width * tiles
    return pl.pallas_call(
        partial_kernel,
        grid_spec=pltpu.PrefetchScalarGridSpec(
            num_scalar_prefetch=3,
            grid=(tiles,),
            in_specs=[whole(gathered[0].shape)] * 4
            + [pl.BlockSpec(memory_space=pltpu.VMEM)],
            out_specs=[whole(message.shape)] * 2 + [pl.BlockSpec((2, rows, width), lambda q, *_: (q, 0, 0))] * 2,
            scratch_shapes=[
                pltpu.VMEM((8, rows, width), jnp.float32),
                pltpu.VMEM((tail(groups), width), jnp.float32),
                pltpu.VMEM((tail(groups), width), jnp.float32),
            ],
        ),
        out_shape=[message, message, kept, kept],
        compiler_params=pltpu.CompilerParams(vmem_limit_bytes=LIMIT),
        cost_estimate=pl.CostEstimate(flops=flops, bytes_accessed=24 * 2**20, transcendentals=0),
        name="partial",
    )(blk, prow, pos, *gathered, pltpu.with_memory_space_constraint(staged, pltpu.VMEM))


def simple(kernel, outs, args, name, scalars=0):
    vmem = pl.BlockSpec(memory_space=pltpu.VMEM)
    smem = pl.BlockSpec(memory_space=pltpu.SMEM)
    return pl.pallas_call(
        kernel,
        out_shape=outs,
        in_specs=[smem] * scalars + [vmem] * (len(args) - scalars),
        out_specs=jax.tree.map(lambda _: vmem, outs),
        compiler_params=pltpu.CompilerParams(vmem_limit_bytes=LIMIT),
        cost_estimate=pl.CostEstimate(flops=2**22, bytes_accessed=2**22, transcendentals=0),
        name=name,
    )(*args)


def later(array, *others):
    return lax.optimization_barrier((array, *others))[0]


def on_device(amplitudes, integrals, blocks):
    _, tiles, depth = amplitudes.shape
    width = 2 * integrals.shape[2]
    row, col = lax.axis_index("row"), lax.axis_index("col")
    z, x_lo = row // 2, row % 2
    x_hi, y, core = col // 8, (col // 2) % 4, col % 2
    turn = 1 - 2 * core
    where = jnp.stack([x_hi, y, core]).astype(jnp.int32)

    number = jnp.arange(32, dtype=jnp.int32)
    key = blocks[:, 1] * 32 + number
    rank = jnp.sum((key[None, :] < key[:, None]).astype(jnp.int32), axis=1)
    hit = (rank[None, :] == number[:, None]).astype(jnp.int32)
    blk = jnp.sum(hit * number[None, :], axis=1)
    prow = jnp.sum(hit * blocks[:, 0][None, :], axis=1)

    slots = []
    for shift in (0, -turn, turn, 2):
        for flip in (0, 1):
            from_y = (y + shift + 4) % 4
            from_x = x_hi ^ flip
            to_z = 2 * from_x + from_y // 2
            ahead = ((to_z - z) * turn + 8) % 4
            slots.append(ahead * 2 + ((from_y % 2) ^ x_lo))
    pos = jnp.stack(slots).astype(jnp.int32)

    last = []

    def run(kernel, outs, args, name, scalars=0, after=()):
        args = list(args)
        args[scalars] = later(args[scalars], *last[-1:], *after)
        out = simple(kernel, outs, args, name, scalars)
        last.append(jax.tree.leaves(out)[0])
        return out

    shards = amplitudes.reshape(4, 2, 16, tiles, depth).transpose(3, 1, 0, 2, 4)
    first = PIECES[0]
    own = [shards[:, :, :, :first].reshape(1, tiles, 8 * first, depth)]
    came = [move(own[0], X_HI)]
    v_other = move(integrals, CORE)
    at, rest = first, []
    for per in PIECES[1:]:
        rest.append(shards[:, :, :, at : at + per].reshape(1, tiles, 8 * per, depth))
        at += per
    own += rest
    gathered = []

    def join(p):
        per = PIECES[p]
        shape = jax.ShapeDtypeStruct((2, tiles, 8 * per, depth), jnp.bfloat16)
        before = gathered[-1][1:3] if gathered else ()
        a0 = run(join_kernel, shape, (own[p], came[p]), "join", after=before)
        a1, a2 = move(a0, Y_FORE), move(a0, Y_BACK)
        gathered.append([a0, a1, a2, None])

    def forward(p):
        a1 = later(gathered[p][1], last[-1])
        gathered[p][3] = move(a1, Y_FORE)

    sums, ends, placed, staged = [], {}, [], []

    def multiply(p):
        a0, a1, a2, a3 = gathered[p]
        far, back, kept, nxt = partial(blk, prow, pos, (later(a0, last[-1]), a1, a2, a3), staged[0])
        last.append(far)
        sums.append((kept, nxt, move(far, Z_FORE), move(back, Z_BACK)))

    def relay(p):
        kept, nxt, far, back = sums[p]
        message = jax.ShapeDtypeStruct((16 * 8 * PIECES[p] + 16, width), jnp.int16)
        out = run(relay_kernel, message, (nxt, far), "relay", after=(back,))
        ends[p] = (kept, move(out, Z_FORE), back)

    def collect(members):
        groups = tiles * len(members)
        rows = tiles * 4 * sum(PIECES[p] for p in members)
        small = jax.ShapeDtypeStruct((rows + tail(groups), width), jnp.int16)
        args = [array for p in members for array in ends[p]]
        kernel = functools.partial(collect_kernel, len(members))
        out = run(kernel, [small] * 4, (where[:1], *args), "collect", scalars=1)
        return [move(m, t) for m, t in zip(out, X_SAME + X_OTHER)]

    def finish(members, out):
        pers = tuple(PIECES[p] for p in members)
        shape = jax.ShapeDtypeStruct((4, sum(pers), tiles, 2 * width), jnp.bfloat16)
        done = run(functools.partial(finish_kernel, pers), shape, (where, *out), "finish", scalars=1)
        placed.extend([done[0]] + [move(done[a], Y_SHIFT[a]) for a in range(1, 4)])

    join(0)
    forward(0)
    moved = run(copy_kernel, jax.ShapeDtypeStruct((1, tiles, 8 * (16 - first), depth), jnp.bfloat16),
                (jnp.concatenate(rest, axis=2),), "rest")
    moved = move(moved, X_HI)
    at = 0
    for per in PIECES[1:]:
        came.append(moved[:, :, at : at + 8 * per])
        at += 8 * per
    pending = {}
    for step in ORDER:
        name, p = step[0], step[1]
        if name == "join":
            join(p)
        elif name == "stage":
            staged.append(stage(later(where, last[-1]), integrals, v_other))
        elif name == "forward":
            forward(p)
        elif name == "multiply":
            multiply(p)
        elif name == "relay":
            relay(p)
        elif name == "collect":
            pending[p] = collect(p)
        else:
            finish(p, pending[p])
    return simple(
        functools.partial(place_kernel, len(placed)),
        jax.ShapeDtypeStruct((16, tiles, 8 * width), jnp.bfloat16),
        (where, *placed),
        "place",
        scalars=1,
    )


def solution(mesh):
    return jax.shard_map(
        on_device,
        mesh=mesh,
        in_specs=(P("col", None, "row"), P(None, "row", "col"), P()),
        out_specs=P(("row", "col"), None, None),
        check_vma=False,
    )
```

time: 206 us -> 184 us (0.89)
  blocking collectives: 24.9 us -> 0 us
  starting transfers between devices: 49.1 us -> 63.3 us
  Pallas kernels: 56.2 us -> 44.6 us
  waiting for transfers between devices: 64.2 us -> 70.9 us
  local copies, waits for them, and re-layouts: 8.87 us -> 3.66 us
    all_to_all x1 -> x0, blocking collectives: 24.9 us -> none  [on_device(): lax.all_to_all(done, 'col', 0, 0, axis_index_groups=GROUPS, tiled=True)]
    pallas_call x4, Pallas kernels: 49.2 us -> 30.1 us  [partial(): pl.pallas_call(partial_kernel, grid_spec=pltpu.PrefetchScalarGridSpec(num...]
    ppermute x37 -> x41, starting transfers between devices: 49.1 us -> 63.3 us  [move(): return lax.ppermute(array, ('row', 'col'), pairs)]
    ppermute x37 -> x41, waiting for transfers between devices: 64.2 us -> 70.9 us  [move(): return lax.ppermute(array, ('row', 'col'), pairs)]
    pallas_call x0 -> x1, Pallas kernels: none -> 6.33 us  [stage(): pl.pallas_call(stage_kernel, out_shape=pltpu.VMEM((blocks, depth, 2 * hal...]
    pallas_call x12 -> x14, Pallas kernels: 6.94 us -> 8.19 us  [simple(): pl.pallas_call(kernel, out_shape=outs, in_specs=[smem] * scalars + [vmem]...]
  transfers between devices with their start and end apart: 37 -> 41, of which waited for: 13 -> 15; matrix products, arithmetic and copies ran while one was open for 3% -> 2% of each run, Pallas kernels for 27% -> 23%
where the time goes in v2:
time: 184 us; the launch traced here: 183 us
  waiting for transfers between devices  70.9 us (39%)
  starting transfers between devices  63.3 us (34%)
  Pallas kernels  44.6 us (24%)
  local copies, waits for them, and re-layouts  3.66 us (2%)
    ppermute x41, waiting for transfers between devices, move(): return lax.ppermute(array, ('row', 'col'), pairs)  70.9 us
    ppermute x41, starting transfers between devices, move(): return lax.ppermute(array, ('row', 'col'), pairs)  63.3 us
    pallas_call x4, Pallas kernels, partial(): pl.pallas_call(partial_kernel, grid_spec=pltpu.PrefetchScalarGridSpec(num...  30.1 us
    pallas_call x14, Pallas kernels, simple(): pl.pallas_call(kernel, out_shape=outs, in_specs=[smem] * scalars + [vmem]...  8.19 us
    pallas_call x1, Pallas kernels, stage(): pl.pallas_call(stage_kernel, out_shape=pltpu.VMEM((blocks, depth, 2 * hal...  6.33 us
  transfers between devices with their start and end apart: 41, of which 15 were waited for; matrix products, arithmetic and copies ran while one was open for 2% of the time, Pallas kernels for 23%

profile of v2, /device:TPU:0, one launch (start us, length us, event | category | flops | bytes accessed | tf_op | source)
XLA Modules:
  0.0 183.3 jit_solution(6331785601645270457)
XLA Ops:
  2.2 3.2 %collective-permute-start = (bf16[1,8,32,512]{3,2,1,0:T(8,128)(2,1)S(1)}, bf16[1,8,32,512]{3,2,1,0:T(8,128)(2,1)S(1)}, u32[]{:S(2)}, u32[]{:S(2)}) collective-permute-start(bf16[1,8,32,512]{3,2,1,0:T(8,128)(2,1)S(1)} %reshape.30.own_ref), channel_id=1, source_target_pairs={{0,8},{1,9},{2,10},{3,11},{4,12},{5,13},{6,14},{7,15},{8,0},{9,1},... | collective-permute-start | bytes 786440 | tf_op jit(solution)/shard_map/ppermute | solution.py:70
  5.6 6.8 %collective-permute-done.came_ref = bf16[1,8,32,512]{3,2,1,0:T(8,128)(2,1)S(1)} collective-permute-done((bf16[1,8,32,512]{3,2,1,0:T(8,128)(2,1)S(1)}, bf16[1,8,32,512]{3,2,1,0:T(8,128)(2,1)S(1)}, u32[]{:S(2)}, u32[]{:S(2)}) %collective-permute-start) | collective-permute-done | bytes 262176 | tf_op jit(solution)/shard_map/ppermute | solution.py:70
  12.6 3.2 %collective-permute-start.3 = (bf16[1,8,96,512]{3,2,1,0:T(8,128)(2,1)S(1)}, bf16[1,8,96,512]{3,2,1,0:T(8,128)(2,1)}, u32[]{:S(2)}, u32[]{:S(2)}) collective-permute-start(bf16[1,8,96,512]{3,2,1,0:T(8,128)(2,1)S(1)} %rest.1), channel_id=1, source_target_pairs={{0,8},{1,9},{2,10},{3,11},{4,12},{5,13},{6,14},{7,15},{8,0},{9,1},... | collective-permute-start | bytes 2359304 | tf_op jit(solution)/shard_map/ppermute | solution.py:70
  19.0 11.5 %collective-permute-done.1.a1 = bf16[2,8,32,512]{3,2,1,0:T(8,128)(2,1)S(1)} collective-permute-done((bf16[2,8,32,512]{3,2,1,0:T(8,128)(2,1)S(1)}, bf16[2,8,32,512]{3,2,1,0:T(8,128)(2,1)S(1)}, u32[]{:S(2)}, u32[]{:S(2)}) %collective-permute-start.1) | collective-permute-done | bytes 524320 | tf_op jit(solution)/shard_map/ppermute | solution.py:70
  38.3 6.3 %stage.1.v_ref = bf16[32,512,512]{2,1,0:T(8,128)(2,1)S(1)} custom-call(s32[3]{0:T(128)S(1)} %pad_add_fusion.where, bf16[32,512,256]{2,1,0:T(8,128)(2,1)} %own_ref.1, bf16[32,512,256]{2,1,0:T(8,128)(2,1)} %collective-permute-done.5.came_ref), custom_call_target="tpu_custom_call" | custom-call | bytes 16777216 | tf_op jit(solution)/shard_map/stage/pallas_call | solution.py:229
  44.7 8.1 %partial.4 = (s16[528,512]{1,0:T(8,128)(2,1)S(1)}, s16[528,512]{1,0:T(8,128)(2,1)S(1)}, f32[16,32,512]{2,1,0:T(8,128)S(1)}, f32[16,32,512]{2,1,0:T(8,128)S(1)}) custom-call(s32[32]{0:T(128)S(1)} %get-tuple-element.96.blk, s32[32]{0:T(128)S(1)} %get-tuple-element.95.prow, s32[8]{0:T(128)S(1)} %stack.51.pos, bf16[2,8,32,512]{3,2,1,0:T(8,128)(2,1)S(1)} %join.4.a0, ...), custom_call_target="tpu_custom_call" | custom-call | flops 4294967296 | bytes 25165824 | tf_op jit(solution)/shard_map/partial/pallas_call | solution.py:252
  60.6 8.5 %collective-permute-done.8.a3 = bf16[2,8,32,512]{3,2,1,0:T(8,128)(2,1)S(1)} collective-permute-done((bf16[2,8,32,512]{3,2,1,0:T(8,128)(2,1)}, bf16[2,8,32,512]{3,2,1,0:T(8,128)(2,1)S(1)}, u32[]{:S(2)}, u32[]{:S(2)}) %collective-permute-start.8) | collective-permute-done | bytes 524320 | tf_op jit(solution)/shard_map/ppermute | solution.py:70
  69.0 8.1 %partial.5 = (s16[528,512]{1,0:T(8,128)(2,1)S(1)}, s16[528,512]{1,0:T(8,128)(2,1)S(1)}, f32[16,32,512]{2,1,0:T(8,128)S(1)}, f32[16,32,512]{2,1,0:T(8,128)S(1)}) custom-call(s32[32]{0:T(128)S(1)} %get-tuple-element.96.blk, s32[32]{0:T(128)S(1)} %get-tuple-element.95.prow, s32[8]{0:T(128)S(1)} %stack.51.pos, bf16[2,8,32,512]{3,2,1,0:T(8,128)(2,1)S(1)} %join.5.a0, ...), custom_call_target="tpu_custom_call" | custom-call | flops 4294967296 | bytes 25165824 | tf_op jit(solution)/shard_map/partial/pallas_call | solution.py:252
  79.9 2.7 %collective-permute-start.17 = (bf16[2,8,32,512]{3,2,1,0:T(8,128)(2,1)S(1)}, bf16[2,8,32,512]{3,2,1,0:T(8,128)(2,1)S(1)}, u32[]{:S(2)}, u32[]{:S(2)}) collective-permute-start(bf16[2,8,32,512]{3,2,1,0:T(8,128)(2,1)S(1)} %join.7.a0), channel_id=1, source_target_pairs={{0,6},{1,3},{2,0},{3,5},{4,2},{5,7},{6,4},{7,1},{8,14},{9,11},{10,... | collective-permute-start | bytes 1572872 | tf_op jit(solution)/shard_map/ppermute | solution.py:70
  82.6 2.2 %collective-permute-start.14 = (s16[528,512]{1,0:T(8,128)(2,1)S(1)}, s16[528,512]{1,0:T(8,128)(2,1)S(1)}, u32[]{:S(2)}, u32[]{:S(2)}) collective-permute-start(s16[528,512]{1,0:T(8,128)(2,1)S(1)} %get-tuple-element.69), channel_id=1, source_target_pairs={{0,96},{1,33},{2,98},{3,35},{4,100},{5,37},{6,102},{7,39},{8,104},... | collective-permute-start | bytes 1622024 | tf_op jit(solution)/shard_map/ppermute | solution.py:70
  85.2 7.7 %collective-permute-done.13.a3 = bf16[2,8,32,512]{3,2,1,0:T(8,128)(2,1)S(1)} collective-permute-done((bf16[2,8,32,512]{3,2,1,0:T(8,128)(2,1)S(1)}, bf16[2,8,32,512]{3,2,1,0:T(8,128)(2,1)S(1)}, u32[]{:S(2)}, u32[]{:S(2)}) %collective-permute-start.13) | collective-permute-done | bytes 524320 | tf_op jit(solution)/shard_map/ppermute | solution.py:70
  92.9 7.0 %partial.6 = (s16[528,512]{1,0:T(8,128)(2,1)S(1)}, s16[528,512]{1,0:T(8,128)(2,1)S(1)}, f32[16,32,512]{2,1,0:T(8,128)S(1)}, f32[16,32,512]{2,1,0:T(8,128)S(1)}) custom-call(s32[32]{0:T(128)S(1)} %get-tuple-element.96.blk, s32[32]{0:T(128)S(1)} %get-tuple-element.95.prow, s32[8]{0:T(128)S(1)} %stack.51.pos, bf16[2,8,32,512]{3,2,1,0:T(8,128)(2,1)S(1)} %join.6.a0, ...), custom_call_target="tpu_custom_call" | custom-call | flops 4294967296 | bytes 25165824 | tf_op jit(solution)/shard_map/partial/pallas_call | solution.py:252
  104.9 5.5 %collective-permute-done.18.a3 = bf16[2,8,32,512]{3,2,1,0:T(8,128)(2,1)S(1)} collective-permute-done((bf16[2,8,32,512]{3,2,1,0:T(8,128)(2,1)S(1)}, bf16[2,8,32,512]{3,2,1,0:T(8,128)(2,1)S(1)}, u32[]{:S(2)}, u32[]{:S(2)}) %collective-permute-start.18) | collective-permute-done | bytes 524320 | tf_op jit(solution)/shard_map/ppermute | solution.py:70
  110.4 7.0 %partial.7 = (s16[528,512]{1,0:T(8,128)(2,1)S(1)}, s16[528,512]{1,0:T(8,128)(2,1)S(1)}, f32[16,32,512]{2,1,0:T(8,128)S(1)}, f32[16,32,512]{2,1,0:T(8,128)S(1)}) custom-call(s32[32]{0:T(128)S(1)} %get-tuple-element.96.blk, s32[32]{0:T(128)S(1)} %get-tuple-element.95.prow, s32[8]{0:T(128)S(1)} %stack.51.pos, bf16[2,8,32,512]{3,2,1,0:T(8,128)(2,1)S(1)} %join.7.a0, ...), custom_call_target="tpu_custom_call" | custom-call | flops 4294967296 | bytes 25165824 | tf_op jit(solution)/shard_map/partial/pallas_call | solution.py:252
  117.4 2.3 %collective-permute-done.20.refs_4_ = s16[528,512]{1,0:T(8,128)(2,1)S(1)} collective-permute-done((s16[528,512]{1,0:T(8,128)(2,1)S(1)}, s16[528,512]{1,0:T(8,128)(2,1)S(1)}, u32[]{:S(2)}, u32[]{:S(2)}) %collective-permute-start.20) | collective-permute-done | bytes 540704 | tf_op jit(solution)/shard_map/ppermute | solution.py:70
  123.8 5.0 %collective-permute-start.24 = (s16[272,512]{1,0:T(8,128)(2,1)S(1)}, s16[272,512]{1,0:T(8,128)(2,1)S(1)}, u32[]{:S(2)}, u32[]{:S(2)}) collective-permute-start(s16[272,512]{1,0:T(8,128)(2,1)S(1)} %get-tuple-element.81), channel_id=1, source_target_pairs={{0,1},{1,9},{2,3},{3,11},{4,5},{5,13},{6,7},{7,15},{8,0},{9,8},{10... | collective-permute-start | bytes 835592 | tf_op jit(solution)/shard_map/ppermute | solution.py:70
  129.4 4.3 %collective-permute-start.26 = (s16[272,512]{1,0:T(8,128)(2,1)S(1)}, s16[272,512]{1,0:T(8,128)(2,1)S(1)}, u32[]{:S(2)}, u32[]{:S(2)}) collective-permute-start(s16[272,512]{1,0:T(8,128)(2,1)S(1)} %get-tuple-element.83), channel_id=1, source_target_pairs={{0,17},{1,25},{2,19},{3,27},{4,21},{5,29},{6,23},{7,31},{8,16},{9,... | collective-permute-start | bytes 835592 | tf_op jit(solution)/shard_map/ppermute | solution.py:70
  136.1 2.4 %collective-permute-start.32 = (s16[528,512]{1,0:T(8,128)(2,1)S(1)}, s16[528,512]{1,0:T(8,128)(2,1)S(1)}, u32[]{:S(2)}, u32[]{:S(2)}) collective-permute-start(s16[528,512]{1,0:T(8,128)(2,1)S(1)} %relay.6), channel_id=1, source_target_pairs={{0,32},{1,97},{2,34},{3,99},{4,36},{5,101},{6,38},{7,103},{8,40},{... | collective-permute-start | bytes 1622024 | tf_op jit(solution)/shard_map/ppermute | solution.py:70
  138.6 3.1 %collective-permute-done.26.refs_3_ = s16[272,512]{1,0:T(8,128)(2,1)S(1)} collective-permute-done((s16[272,512]{1,0:T(8,128)(2,1)S(1)}, s16[272,512]{1,0:T(8,128)(2,1)S(1)}, u32[]{:S(2)}, u32[]{:S(2)}) %collective-permute-start.26) | collective-permute-done | bytes 278560 | tf_op jit(solution)/shard_map/ppermute | solution.py:70
  146.7 7.2 %collective-permute-done.33.refs_4_ = s16[528,512]{1,0:T(8,128)(2,1)S(1)} collective-permute-done((s16[528,512]{1,0:T(8,128)(2,1)S(1)}, s16[528,512]{1,0:T(8,128)(2,1)S(1)}, u32[]{:S(2)}, u32[]{:S(2)}) %collective-permute-start.33) | collective-permute-done | bytes 540704 | tf_op jit(solution)/shard_map/ppermute | solution.py:70
  159.2 2.9 %collective-permute-start.28 = (bf16[8,8,1024]{2,1,0:T(8,128)(2,1)S(1)}, bf16[8,8,1024]{2,1,0:T(8,128)(2,1)S(1)}, u32[]{:S(2)}, u32[]{:S(2)}) collective-permute-start(bf16[8,8,1024]{2,1,0:T(8,128)(2,1)S(1)} %get-tuple-element.109), channel_id=1, source_target_pairs={{0,4},{1,5},{2,6},{3,7},{4,0},{5,1},{6,2},{7,3},{8,12},{9,13},{10,... | collective-permute-start | bytes 393224 | tf_op jit(solution)/shard_map/ppermute | solution.py:70
  162.2 7.7 %collective-permute-done.35.refs_1_ = s16[272,512]{1,0:T(8,128)(2,1)S(1)} collective-permute-done((s16[272,512]{1,0:T(8,128)(2,1)S(1)}, s16[272,512]{1,0:T(8,128)(2,1)S(1)}, u32[]{:S(2)}, u32[]{:S(2)}) %collective-permute-start.35) | collective-permute-done | bytes 278560 | tf_op jit(solution)/shard_map/ppermute | solution.py:70
  173.1 3.1 %collective-permute-start.39 = (bf16[8,8,1024]{2,1,0:T(8,128)(2,1)S(1)}, bf16[8,8,1024]{2,1,0:T(8,128)(2,1)S(1)}, u32[]{:S(2)}, u32[]{:S(2)}) collective-permute-start(bf16[8,8,1024]{2,1,0:T(8,128)(2,1)S(1)} %get-tuple-element.105), channel_id=1, source_target_pairs={{0,4},{1,5},{2,6},{3,7},{4,0},{5,1},{6,2},{7,3},{8,12},{9,13},{10,... | collective-permute-start | bytes 393224 | tf_op jit(solution)/shard_map/ppermute | solution.py:70
  176.3 4.7 %collective-permute-done.38.refs_5_ = bf16[8,8,1024]{2,1,0:T(8,128)(2,1)S(1)} collective-permute-done((bf16[8,8,1024]{2,1,0:T(8,128)(2,1)S(1)}, bf16[8,8,1024]{2,1,0:T(8,128)(2,1)S(1)}, u32[]{:S(2)}, u32[]{:S(2)}) %collective-permute-start.38) | collective-permute-done | bytes 131104 | tf_op jit(solution)/shard_map/ppermute | solution.py:70
  (95 shorter events, 52.4 us)
Async XLA Ops:
  0.0 38.3 %collective-permute-start.5 = (bf16[32,512,256]{2,1,0:T(8,128)(2,1)}, bf16[32,512,256]{2,1,0:T(8,128)(2,1)}, u32[]{:S(2)}, u32[]{:S(2)}) collective-permute-start(bf16[32,512,256]{2,1,0:T(8,128)(2,1)} %own_ref.1), channel_id=1, source_target_pairs={{0,1},{1,0},{2,3},{3,2},{4,5},{5,4},{6,7},{7,6},{8,9},{9,8},{10,11... | collective-permute-start | bytes 25165832 | tf_op jit(solution)/shard_map/ppermute | solution.py:70
  12.6 20.9 %collective-permute-start.3 = (bf16[1,8,96,512]{3,2,1,0:T(8,128)(2,1)S(1)}, bf16[1,8,96,512]{3,2,1,0:T(8,128)(2,1)}, u32[]{:S(2)}, u32[]{:S(2)}) collective-permute-start(bf16[1,8,96,512]{3,2,1,0:T(8,128)(2,1)S(1)} %rest.1), channel_id=1, source_target_pairs={{0,8},{1,9},{2,10},{3,11},{4,12},{5,13},{6,14},{7,15},{8,0},{9,1},... | collective-permute-start | bytes 2359304 | tf_op jit(solution)/shard_map/ppermute | solution.py:70
  15.7 14.8 %collective-permute-start.1 = (bf16[2,8,32,512]{3,2,1,0:T(8,128)(2,1)S(1)}, bf16[2,8,32,512]{3,2,1,0:T(8,128)(2,1)S(1)}, u32[]{:S(2)}, u32[]{:S(2)}) collective-permute-start(bf16[2,8,32,512]{3,2,1,0:T(8,128)(2,1)S(1)} %join.4.a0), channel_id=1, source_target_pairs={{0,2},{1,7},{2,4},{3,1},{4,6},{5,3},{6,0},{7,5},{8,10},{9,15},{10,... | collective-permute-start | bytes 1572872 | tf_op jit(solution)/shard_map/ppermute | solution.py:70
  17.3 15.1 %collective-permute-start.2 = (bf16[2,8,32,512]{3,2,1,0:T(8,128)(2,1)S(1)}, bf16[2,8,32,512]{3,2,1,0:T(8,128)(2,1)S(1)}, u32[]{:S(2)}, u32[]{:S(2)}) collective-permute-start(bf16[2,8,32,512]{3,2,1,0:T(8,128)(2,1)S(1)} %join.4.a0), channel_id=1, source_target_pairs={{0,6},{1,3},{2,0},{3,5},{4,2},{5,7},{6,4},{7,1},{8,14},{9,11},{10,... | collective-permute-start | bytes 1572872 | tf_op jit(solution)/shard_map/ppermute | solution.py:70
  34.6 18.1 %collective-permute-start.6 = (bf16[2,8,32,512]{3,2,1,0:T(8,128)(2,1)S(1)}, bf16[2,8,32,512]{3,2,1,0:T(8,128)(2,1)}, u32[]{:S(2)}, u32[]{:S(2)}) collective-permute-start(bf16[2,8,32,512]{3,2,1,0:T(8,128)(2,1)S(1)} %join.5.a0), channel_id=1, source_target_pairs={{0,2},{1,7},{2,4},{3,1},{4,6},{5,3},{6,0},{7,5},{8,10},{9,15},{10,... | collective-permute-start | bytes 1572872 | tf_op jit(solution)/shard_map/ppermute | solution.py:70
  36.6 16.6 %collective-permute-start.7 = (bf16[2,8,32,512]{3,2,1,0:T(8,128)(2,1)S(1)}, bf16[2,8,32,512]{3,2,1,0:T(8,128)(2,1)S(1)}, u32[]{:S(2)}, u32[]{:S(2)}) collective-permute-start(bf16[2,8,32,512]{3,2,1,0:T(8,128)(2,1)S(1)} %join.5.a0), channel_id=1, source_target_pairs={{0,6},{1,3},{2,0},{3,5},{4,2},{5,7},{6,4},{7,1},{8,14},{9,11},{10,... | collective-permute-start | bytes 1572872 | tf_op jit(solution)/shard_map/ppermute | solution.py:70
  52.8 16.3 %collective-permute-start.8 = (bf16[2,8,32,512]{3,2,1,0:T(8,128)(2,1)}, bf16[2,8,32,512]{3,2,1,0:T(8,128)(2,1)S(1)}, u32[]{:S(2)}, u32[]{:S(2)}) collective-permute-start(bf16[2,8,32,512]{3,2,1,0:T(8,128)(2,1)} %collective-permute-done.6.a1), channel_id=1, source_target_pairs={{0,2},{1,7},{2,4},{3,1},{4,6},{5,3},{6,0},{7,5},{8,10},{9,15},{10,... | collective-permute-start | bytes 1572872 | tf_op jit(solution)/shard_map/ppermute | solution.py:70
  53.2 23.9 %collective-permute-start.9 = (bf16[2,8,32,512]{3,2,1,0:T(8,128)(2,1)S(1)}, bf16[2,8,32,512]{3,2,1,0:T(8,128)(2,1)S(1)}, u32[]{:S(2)}, u32[]{:S(2)}) collective-permute-start(bf16[2,8,32,512]{3,2,1,0:T(8,128)(2,1)S(1)} %join.6.a0), channel_id=1, source_target_pairs={{0,2},{1,7},{2,4},{3,1},{4,6},{5,3},{6,0},{7,5},{8,10},{9,15},{10,... | collective-permute-start | bytes 1572872 | tf_op jit(solution)/shard_map/ppermute | solution.py:70
  54.9 22.3 %collective-permute-start.10 = (bf16[2,8,32,512]{3,2,1,0:T(8,128)(2,1)S(1)}, bf16[2,8,32,512]{3,2,1,0:T(8,128)(2,1)S(1)}, u32[]{:S(2)}, u32[]{:S(2)}) collective-permute-start(bf16[2,8,32,512]{3,2,1,0:T(8,128)(2,1)S(1)} %join.6.a0), channel_id=1, source_target_pairs={{0,6},{1,3},{2,0},{3,5},{4,2},{5,7},{6,4},{7,1},{8,14},{9,11},{10,... | collective-permute-start | bytes 1572872 | tf_op jit(solution)/shard_map/ppermute | solution.py:70
  56.5 26.1 %collective-permute-start.12 = (s16[528,512]{1,0:T(8,128)(2,1)S(1)}, s16[528,512]{1,0:T(8,128)(2,1)S(1)}, u32[]{:S(2)}, u32[]{:S(2)}) collective-permute-start(s16[528,512]{1,0:T(8,128)(2,1)S(1)} %get-tuple-element.56), channel_id=1, source_target_pairs={{0,32},{1,97},{2,34},{3,99},{4,36},{5,101},{6,38},{7,103},{8,40},{... | collective-permute-start | bytes 1622024 | tf_op jit(solution)/shard_map/ppermute | solution.py:70
  58.4 21.5 %collective-permute-start.11 = (s16[528,512]{1,0:T(8,128)(2,1)S(1)}, s16[528,512]{1,0:T(8,128)(2,1)S(1)}, u32[]{:S(2)}, u32[]{:S(2)}) collective-permute-start(s16[528,512]{1,0:T(8,128)(2,1)S(1)} %get-tuple-element.64), channel_id=1, source_target_pairs={{0,96},{1,33},{2,98},{3,35},{4,100},{5,37},{6,102},{7,39},{8,104},... | collective-permute-start | bytes 1622024 | tf_op jit(solution)/shard_map/ppermute | solution.py:70
  77.1 15.8 %collective-permute-start.13 = (bf16[2,8,32,512]{3,2,1,0:T(8,128)(2,1)S(1)}, bf16[2,8,32,512]{3,2,1,0:T(8,128)(2,1)S(1)}, u32[]{:S(2)}, u32[]{:S(2)}) collective-permute-start(bf16[2,8,32,512]{3,2,1,0:T(8,128)(2,1)S(1)} %collective-permute-done.9.a1), channel_id=1, source_target_pairs={{0,2},{1,7},{2,4},{3,1},{4,6},{5,3},{6,0},{7,5},{8,10},{9,15},{10,... | collective-permute-start | bytes 1572872 | tf_op jit(solution)/shard_map/ppermute | solution.py:70
  77.3 22.7 %collective-permute-start.16 = (bf16[2,8,32,512]{3,2,1,0:T(8,128)(2,1)S(1)}, bf16[2,8,32,512]{3,2,1,0:T(8,128)(2,1)S(1)}, u32[]{:S(2)}, u32[]{:S(2)}) collective-permute-start(bf16[2,8,32,512]{3,2,1,0:T(8,128)(2,1)S(1)} %join.7.a0), channel_id=1, source_target_pairs={{0,2},{1,7},{2,4},{3,1},{4,6},{5,3},{6,0},{7,5},{8,10},{9,15},{10,... | collective-permute-start | bytes 1572872 | tf_op jit(solution)/shard_map/ppermute | solution.py:70
  78.0 22.1 %collective-permute-start.15 = (s16[528,512]{1,0:T(8,128)(2,1)S(1)}, s16[528,512]{1,0:T(8,128)(2,1)S(1)}, u32[]{:S(2)}, u32[]{:S(2)}) collective-permute-start(s16[528,512]{1,0:T(8,128)(2,1)S(1)} %get-tuple-element.60), channel_id=1, source_target_pairs={{0,32},{1,97},{2,34},{3,99},{4,36},{5,101},{6,38},{7,103},{8,40},{... | collective-permute-start | bytes 1622024 | tf_op jit(solution)/shard_map/ppermute | solution.py:70
  79.9 23.5 %collective-permute-start.17 = (bf16[2,8,32,512]{3,2,1,0:T(8,128)(2,1)S(1)}, bf16[2,8,32,512]{3,2,1,0:T(8,128)(2,1)S(1)}, u32[]{:S(2)}, u32[]{:S(2)}) collective-permute-start(bf16[2,8,32,512]{3,2,1,0:T(8,128)(2,1)S(1)} %join.7.a0), channel_id=1, source_target_pairs={{0,6},{1,3},{2,0},{3,5},{4,2},{5,7},{6,4},{7,1},{8,14},{9,11},{10,... | collective-permute-start | bytes 1572872 | tf_op jit(solution)/shard_map/ppermute | solution.py:70
  82.6 17.5 %collective-permute-start.14 = (s16[528,512]{1,0:T(8,128)(2,1)S(1)}, s16[528,512]{1,0:T(8,128)(2,1)S(1)}, u32[]{:S(2)}, u32[]{:S(2)}) collective-permute-start(s16[528,512]{1,0:T(8,128)(2,1)S(1)} %get-tuple-element.69), channel_id=1, source_target_pairs={{0,96},{1,33},{2,98},{3,35},{4,100},{5,37},{6,102},{7,39},{8,104},... | collective-permute-start | bytes 1622024 | tf_op jit(solution)/shard_map/ppermute | solution.py:70
  100.0 17.4 %collective-permute-start.19 = (s16[528,512]{1,0:T(8,128)(2,1)S(1)}, s16[528,512]{1,0:T(8,128)(2,1)S(1)}, u32[]{:S(2)}, u32[]{:S(2)}) collective-permute-start(s16[528,512]{1,0:T(8,128)(2,1)S(1)} %relay.4), channel_id=1, source_target_pairs={{0,32},{1,97},{2,34},{3,99},{4,36},{5,101},{6,38},{7,103},{8,40},{... | collective-permute-start | bytes 1622024 | tf_op jit(solution)/shard_map/ppermute | solution.py:70
  100.5 19.2 %collective-permute-start.20 = (s16[528,512]{1,0:T(8,128)(2,1)S(1)}, s16[528,512]{1,0:T(8,128)(2,1)S(1)}, u32[]{:S(2)}, u32[]{:S(2)}) collective-permute-start(s16[528,512]{1,0:T(8,128)(2,1)S(1)} %relay.5), channel_id=1, source_target_pairs={{0,32},{1,97},{2,34},{3,99},{4,36},{5,101},{6,38},{7,103},{8,40},{... | collective-permute-start | bytes 1622024 | tf_op jit(solution)/shard_map/ppermute | solution.py:70
  101.6 27.2 %collective-permute-start.23 = (s16[528,512]{1,0:T(8,128)(2,1)S(1)}, s16[528,512]{1,0:T(8,128)(2,1)S(1)}, u32[]{:S(2)}, u32[]{:S(2)}) collective-permute-start(s16[528,512]{1,0:T(8,128)(2,1)S(1)} %get-tuple-element.68), channel_id=1, source_target_pairs={{0,32},{1,97},{2,34},{3,99},{4,36},{5,101},{6,38},{7,103},{8,40},{... | collective-permute-start | bytes 1622024 | tf_op jit(solution)/shard_map/ppermute | solution.py:70
  103.4 20.4 %collective-permute-start.22 = (s16[528,512]{1,0:T(8,128)(2,1)S(1)}, s16[528,512]{1,0:T(8,128)(2,1)S(1)}, u32[]{:S(2)}, u32[]{:S(2)}) collective-permute-start(s16[528,512]{1,0:T(8,128)(2,1)S(1)} %get-tuple-element.78), channel_id=1, source_target_pairs={{0,96},{1,33},{2,98},{3,35},{4,100},{5,37},{6,102},{7,39},{8,104},... | collective-permute-start | bytes 1622024 | tf_op jit(solution)/shard_map/ppermute | solution.py:70
  121.7 21.1 %collective-permute-start.30 = (s16[528,512]{1,0:T(8,128)(2,1)S(1)}, s16[528,512]{1,0:T(8,128)(2,1)S(1)}, u32[]{:S(2)}, u32[]{:S(2)}) collective-permute-start(s16[528,512]{1,0:T(8,128)(2,1)S(1)} %get-tuple-element.86), channel_id=1, source_target_pairs={{0,96},{1,33},{2,98},{3,35},{4,100},{5,37},{6,102},{7,39},{8,104},... | collective-permute-start | bytes 1622024 | tf_op jit(solution)/shard_map/ppermute | solution.py:70
  122.5 20.2 %collective-permute-start.31 = (s16[528,512]{1,0:T(8,128)(2,1)S(1)}, s16[528,512]{1,0:T(8,128)(2,1)S(1)}, u32[]{:S(2)}, u32[]{:S(2)}) collective-permute-start(s16[528,512]{1,0:T(8,128)(2,1)S(1)} %get-tuple-element.73), channel_id=1, source_target_pairs={{0,32},{1,97},{2,34},{3,99},{4,36},{5,101},{6,38},{7,103},{8,40},{... | collective-permute-start | bytes 1622024 | tf_op jit(solution)/shard_map/ppermute | solution.py:70
  159.1 17.1 %collective-permute-start.27 = (bf16[8,8,1024]{2,1,0:T(8,128)(2,1)S(1)}, bf16[8,8,1024]{2,1,0:T(8,128)(2,1)S(1)}, u32[]{:S(2)}, u32[]{:S(2)}) collective-permute-start(bf16[8,8,1024]{2,1,0:T(8,128)(2,1)S(1)} %get-tuple-element.110), channel_id=1, source_target_pairs={{0,2},{1,3},{2,4},{3,5},{4,6},{5,7},{6,0},{7,1},{8,10},{9,11},{10,... | collective-permute-start | bytes 393224 | tf_op jit(solution)/shard_map/ppermute | solution.py:70
  159.2 17.1 %collective-permute-start.28 = (bf16[8,8,1024]{2,1,0:T(8,128)(2,1)S(1)}, bf16[8,8,1024]{2,1,0:T(8,128)(2,1)S(1)}, u32[]{:S(2)}, u32[]{:S(2)}) collective-permute-start(bf16[8,8,1024]{2,1,0:T(8,128)(2,1)S(1)} %get-tuple-element.109), channel_id=1, source_target_pairs={{0,4},{1,5},{2,6},{3,7},{4,0},{5,1},{6,2},{7,3},{8,12},{9,13},{10,... | collective-permute-start | bytes 393224 | tf_op jit(solution)/shard_map/ppermute | solution.py:70
  (18 other events, 187.0 us)

commit v3 on v2

--- a/solution.py
+++ b/solution.py
@@ -9,20 +9,22 @@
 
 PIECES = (4, 4, 4, 4)
 ORDER = (
+    ("join", 1),
+    ("fetch", (2, 3)),
+    ("turn", 0),
     ("stage", 0),
-    ("join", 1),
-    ("multiply", 0),
     ("forward", 1),
     ("join", 2),
     ("multiply", 1),
     ("forward", 2),
     ("join", 3),
+    ("multiply", 0),
+    ("relay", 1),
     ("relay", 0),
     ("multiply", 2),
     ("forward", 3),
-    ("relay", 1),
+    ("collect", (0, 1)),
     ("multiply", 3),
-    ("collect", (0, 1)),
     ("relay", 2),
     ("finish", (0, 1)),
     ("relay", 3),
@@ -108,14 +110,15 @@
         copy.wait()
 
 
-def partial_kernel(blk, prow, pos, a0, a1, a2, a3, v_ref, *rest):
+def partial_kernel(blk, prow, pos, *rest):
     far_ref, back_ref, own_ref, next_ref, held, far_codes, back_codes = rest[-7:]
+    *shards, v_ref = rest[:-7]
     q = pl.program_id(0)
-    rows = a0.shape[2]
+    rows = shards[0].shape[2]
     total = None
     for j in range(4):
         tile = prow[q * 4 + j]
-        left = jnp.concatenate([a[s, tile] for a in (a0, a1, a2, a3) for s in range(2)], axis=0)
+        left = jnp.concatenate([a[s, tile] for a in shards for s in range(a.shape[0])], axis=0)
         term = jnp.dot(left, v_ref[blk[q * 4 + j]], preferred_element_type=jnp.float32)
         total = term if total is None else total + term
     for s in range(8):
@@ -136,9 +139,9 @@
             ref[last:, :] = codes[...].astype(jnp.int32).astype(jnp.int16)
 
 
-def join_kernel(own_ref, came_ref, *rest):
-    rest[-1][0] = own_ref[0]
-    rest[-1][1] = came_ref[0]
+def join_kernel(*refs):
+    for n, ref in enumerate(refs[:-1]):
+        refs[-1][n] = ref[0]
 
 
 def copy_kernel(in_ref, *rest):
@@ -221,7 +224,7 @@
         base += per
 
 
-LIMIT = 14 * 2**20
+LIMIT = 10 * 2**20
 
 
 def stage(where, own, came):
@@ -247,14 +250,14 @@
         return pl.BlockSpec(shape, lambda q, *_: (0,) * len(shape))
 
     message = jax.ShapeDtypeStruct((groups * rows + tail(groups), width), jnp.int16)
-    kept = jax.ShapeDtypeStruct((groups, rows, width), jnp.float32)
+    kept = pltpu.HBM((groups, rows, width), jnp.float32)
     flops = 2 * 8 * rows * 4 * depth * width * tiles
     return pl.pallas_call(
         partial_kernel,
         grid_spec=pltpu.PrefetchScalarGridSpec(
             num_scalar_prefetch=3,
             grid=(tiles,),
-            in_specs=[whole(gathered[0].shape)] * 4
+            in_specs=[whole(a.shape) for a in gathered]
             + [pl.BlockSpec(memory_space=pltpu.VMEM)],
             out_specs=[whole(message.shape)] * 2 + [pl.BlockSpec((2, rows, width), lambda q, *_: (q, 0, 0))] * 2,
             scratch_shapes=[
@@ -313,6 +316,7 @@
             ahead = ((to_z - z) * turn + 8) % 4
             slots.append(ahead * 2 + ((from_y % 2) ^ x_lo))
     pos = jnp.stack(slots).astype(jnp.int32)
+    pos_first = jnp.stack(slots[0::2] + slots[1::2]).astype(jnp.int32)
 
     last = []
 
@@ -324,36 +328,47 @@
         return out
 
     shards = amplitudes.reshape(4, 2, 16, tiles, depth).transpose(3, 1, 0, 2, 4)
-    first = PIECES[0]
-    own = [shards[:, :, :, :first].reshape(1, tiles, 8 * first, depth)]
-    came = [move(own[0], X_HI)]
+    own, at = [], 0
+    for per in PIECES:
+        own.append(shards[:, :, :, at : at + per].reshape(1, tiles, 8 * per, depth))
+        at += per
+    came = {1: move(own[1], X_HI)}
     v_other = move(integrals, CORE)
-    at, rest = first, []
-    for per in PIECES[1:]:
-        rest.append(shards[:, :, :, at : at + per].reshape(1, tiles, 8 * per, depth))
-        at += per
-    own += rest
-    gathered = []
+    gathered = {}
+
+    def send(p, a0):
+        gathered[p] = [a0, move(a0, Y_FORE), move(a0, Y_BACK), None]
+
+    def forward(p):
+        a1 = later(gathered[p][1], *last[-1:])
+        gathered[p][3] = move(a1, Y_FORE)
+
+    def fetch(members):
+        rows = [8 * PIECES[p] for p in members]
+        shape = jax.ShapeDtypeStruct((1, tiles, sum(rows), depth), jnp.bfloat16)
+        block = jnp.concatenate([own[p] for p in members], axis=2)
+        moved = move(run(copy_kernel, shape, (block,), "rest", after=(came[1],)), X_HI)
+        at = 0
+        for p, n in zip(members, rows):
+            came[p] = moved[:, :, at : at + n]
+            at += n
 
     def join(p):
-        per = PIECES[p]
-        shape = jax.ShapeDtypeStruct((2, tiles, 8 * per, depth), jnp.bfloat16)
-        before = gathered[-1][1:3] if gathered else ()
-        a0 = run(join_kernel, shape, (own[p], came[p]), "join", after=before)
-        a1, a2 = move(a0, Y_FORE), move(a0, Y_BACK)
-        gathered.append([a0, a1, a2, None])
-
-    def forward(p):
-        a1 = later(gathered[p][1], last[-1])
-        gathered[p][3] = move(a1, Y_FORE)
-
-    sums, ends, placed, staged = [], {}, [], []
+        shape = jax.ShapeDtypeStruct((2, tiles, 8 * PIECES[p], depth), jnp.bfloat16)
+        send(p, run(join_kernel, shape, (own[p], came[p]), "join", after=gathered[p - 1][1:3]))
+
+    def turn_first():
+        shape = jax.ShapeDtypeStruct((4, tiles, 8 * PIECES[0], depth), jnp.bfloat16)
+        held = run(join_kernel, shape, tuple(gathered[0]), "join")
+        gathered[0] = (held, move(held, X_HI))
+
+    sums, ends, placed, staged = {}, {}, [], []
 
     def multiply(p):
-        a0, a1, a2, a3 = gathered[p]
-        far, back, kept, nxt = partial(blk, prow, pos, (later(a0, last[-1]), a1, a2, a3), staged[0])
+        held = (later(gathered[p][0], last[-1]), *gathered[p][1:])
+        far, back, kept, nxt = partial(blk, prow, pos if p else pos_first, held, staged[0])
         last.append(far)
-        sums.append((kept, nxt, move(far, Z_FORE), move(back, Z_BACK)))
+        sums[p] = (kept, nxt, move(far, Z_FORE), move(back, Z_BACK))
 
     def relay(p):
         kept, nxt, far, back = sums[p]
@@ -376,15 +391,8 @@
         done = run(functools.partial(finish_kernel, pers), shape, (where, *out), "finish", scalars=1)
         placed.extend([done[0]] + [move(done[a], Y_SHIFT[a]) for a in range(1, 4)])
 
-    join(0)
+    send(0, own[0])
     forward(0)
-    moved = run(copy_kernel, jax.ShapeDtypeStruct((1, tiles, 8 * (16 - first), depth), jnp.bfloat16),
-                (jnp.concatenate(rest, axis=2),), "rest")
-    moved = move(moved, X_HI)
-    at = 0
-    for per in PIECES[1:]:
-        came.append(moved[:, :, at : at + 8 * per])
-        at += 8 * per
     pending = {}
     for step in ORDER:
         name, p = step[0], step[1]
@@ -394,6 +402,10 @@
             staged.append(stage(later(where, last[-1]), integrals, v_other))
         elif name == "forward":
             forward(p)
+        elif name == "fetch":
+            fetch(p)
+        elif name == "turn":
+            turn_first()
         elif name == "multiply":
             multiply(p)
         elif name == "relay":

time: 184 us -> 177 us (0.962)
  starting transfers between devices: 63.3 us -> 49.3 us
  local copies, waits for them, and re-layouts: 3.66 us -> 10 us
  Pallas kernels: 44.6 us -> 50.2 us
  waiting for transfers between devices: 70.9 us -> 65.9 us
    ppermute x41 -> x42, starting transfers between devices: 63.3 us -> 49.3 us  [move(): return lax.ppermute(array, ('row', 'col'), pairs)]
    unnamed x2 -> x30, local copies, waits for them, and re-layouts: 0.01 us -> 6.39 us
    ppermute x41 -> x42, waiting for transfers between devices: 70.9 us -> 65.9 us  [move(): return lax.ppermute(array, ('row', 'col'), pairs)]
    pallas_call x4, Pallas kernels: 30.1 us -> 34.9 us  [partial(): pl.pallas_call(partial_kernel, grid_spec=pltpu.PrefetchScalarGridSpec(num...]
  transfers between devices with their start and end apart: 41 -> 42, of which waited for: 15 -> 19; matrix products, arithmetic and copies ran while one was open for 2% -> 2% of each run, Pallas kernels for 23% -> 27%
where the time goes in v3:
time: 177 us; the launch traced here: 176 us
  waiting for transfers between devices  65.9 us (37%)
  Pallas kernels  50.2 us (28%)
  starting transfers between devices  49.3 us (28%)
  local copies, waits for them, and re-layouts  10 us (6%)
    ppermute x42, waiting for transfers between devices, move(): return lax.ppermute(array, ('row', 'col'), pairs)  65.9 us
    ppermute x42, starting transfers between devices, move(): return lax.ppermute(array, ('row', 'col'), pairs)  49.3 us
    pallas_call x4, Pallas kernels, partial(): pl.pallas_call(partial_kernel, grid_spec=pltpu.PrefetchScalarGridSpec(num...  34.9 us
    pallas_call x14, Pallas kernels, simple(): pl.pallas_call(kernel, out_shape=outs, in_specs=[smem] * scalars + [vmem]...  8.99 us
    unnamed x30, local copies, waits for them, and re-layouts  6.39 us
    pallas_call x1, Pallas kernels, stage(): pl.pallas_call(stage_kernel, out_shape=pltpu.VMEM((blocks, depth, 2 * hal...  6.33 us
  transfers between devices with their start and end apart: 42, of which 19 were waited for; matrix products, arithmetic and copies ran while one was open for 2% of the time, Pallas kernels for 27%

profile of v3, /device:TPU:0, one launch (start us, length us, event | category | flops | bytes accessed | tf_op | source)
XLA Modules:
  0.0 176.4 jit_solution(11255150124767243312)
XLA Ops:
  5.6 3.2 %collective-permute-start.2 = (bf16[1,8,32,512]{3,2,1,0:T(8,128)(2,1)S(1)}, bf16[1,8,32,512]{3,2,1,0:T(8,128)(2,1)S(1)}, u32[]{:S(2)}, u32[]{:S(2)}) collective-permute-start(bf16[1,8,32,512]{3,2,1,0:T(8,128)(2,1)S(1)} %reshape.33.refs_0_), channel_id=1, source_target_pairs={{0,8},{1,9},{2,10},{3,11},{4,12},{5,13},{6,14},{7,15},{8,0},{9,1},... | collective-permute-start | bytes 786440 | tf_op jit(solution)/shard_map/ppermute | solution.py:72
  12.6 2.8 %collective-permute-done.2.refs_1_ = bf16[1,8,32,512]{3,2,1,0:T(8,128)(2,1)S(1)} collective-permute-done((bf16[1,8,32,512]{3,2,1,0:T(8,128)(2,1)S(1)}, bf16[1,8,32,512]{3,2,1,0:T(8,128)(2,1)S(1)}, u32[]{:S(2)}, u32[]{:S(2)}) %collective-permute-start.2) | collective-permute-done | bytes 262176 | tf_op jit(solution)/shard_map/ppermute | solution.py:72
  15.9 3.0 %collective-permute-start.5 = (bf16[2,8,32,512]{3,2,1,0:T(8,128)(2,1)S(1)}, bf16[2,8,32,512]{3,2,1,0:T(8,128)(2,1)S(1)}, u32[]{:S(2)}, u32[]{:S(2)}) collective-permute-start(bf16[2,8,32,512]{3,2,1,0:T(8,128)(2,1)S(1)} %join.4.rest_0_), channel_id=1, source_target_pairs={{0,6},{1,3},{2,0},{3,5},{4,2},{5,7},{6,4},{7,1},{8,14},{9,11},{10,... | collective-permute-start | bytes 1572872 | tf_op jit(solution)/shard_map/ppermute | solution.py:72
  19.7 3.0 %collective-permute-start.6 = (bf16[1,8,64,512]{3,2,1,0:T(8,128)(2,1)}, bf16[1,8,64,512]{3,2,1,0:T(8,128)(2,1)}, u32[]{:S(2)}, u32[]{:S(2)}) collective-permute-start(bf16[1,8,64,512]{3,2,1,0:T(8,128)(2,1)} %rest.1), channel_id=1, source_target_pairs={{0,8},{1,9},{2,10},{3,11},{4,12},{5,13},{6,14},{7,15},{8,0},{9,1},... | collective-permute-start | bytes 1572872 | tf_op jit(solution)/shard_map/ppermute | solution.py:72
  25.4 4.5 %collective-permute-done.4.rest_1_ = bf16[2,8,32,512]{3,2,1,0:T(8,128)(2,1)S(1)} collective-permute-done((bf16[2,8,32,512]{3,2,1,0:T(8,128)(2,1)S(1)}, bf16[2,8,32,512]{3,2,1,0:T(8,128)(2,1)S(1)}, u32[]{:S(2)}, u32[]{:S(2)}) %collective-permute-start.4) | collective-permute-done | bytes 524320 | tf_op jit(solution)/shard_map/ppermute | solution.py:72
  31.0 5.4 %collective-permute-done.6 = bf16[1,8,64,512]{3,2,1,0:T(8,128)(2,1)} collective-permute-done((bf16[1,8,64,512]{3,2,1,0:T(8,128)(2,1)}, bf16[1,8,64,512]{3,2,1,0:T(8,128)(2,1)}, u32[]{:S(2)}, u32[]{:S(2)}) %collective-permute-start.6) | collective-permute-done | bytes 524320 | tf_op jit(solution)/shard_map/ppermute | solution.py:72
  37.6 3.2 %collective-permute-start.10 = (bf16[2,8,32,512]{3,2,1,0:T(8,128)(2,1)S(1)}, bf16[2,8,32,512]{3,2,1,0:T(8,128)(2,1)}, u32[]{:S(2)}, u32[]{:S(2)}) collective-permute-start(bf16[2,8,32,512]{3,2,1,0:T(8,128)(2,1)S(1)} %join.6.rest_0_), channel_id=1, source_target_pairs={{0,6},{1,3},{2,0},{3,5},{4,2},{5,7},{6,4},{7,1},{8,14},{9,11},{10,... | collective-permute-start | bytes 1572872 | tf_op jit(solution)/shard_map/ppermute | solution.py:72
  41.1 6.3 %stage.1.rest_4_.rest_2_ = bf16[32,512,512]{2,1,0:T(8,128)(2,1)S(1)} custom-call(s32[3]{0:T(128)S(1)} %pad_add_fusion.where, bf16[32,512,256]{2,1,0:T(8,128)(2,1)} %own_ref.1, bf16[32,512,256]{2,1,0:T(8,128)(2,1)} %collective-permute-done.8.came_ref), custom_call_target="tpu_custom_call" | custom-call | bytes 16777216 | tf_op jit(solution)/shard_map/stage/pallas_call | solution.py:232
  47.5 8.9 %partial.4 = (s16[528,512]{1,0:T(8,128)(2,1)S(1)}, s16[528,512]{1,0:T(8,128)(2,1)S(1)}, f32[16,32,512]{2,1,0:T(8,128)}, f32[16,32,512]{2,1,0:T(8,128)}) custom-call(s32[32]{0:T(128)S(1)} %get-tuple-element.96.blk, s32[32]{0:T(128)S(1)} %get-tuple-element.95.prow, s32[8]{0:T(128)S(1)} %stack.63.pos, bf16[2,8,32,512]{3,2,1,0:T(8,128)(2,1)S(1)} %join.4.rest_0_, ...), custom_call_target="tpu_custom_call" | custom-call | flops 4294967296 | bytes 25165824 | tf_op jit(solution)/shard_map/partial/pallas_call | solution.py:255
  60.6 9.1 %partial.5 = (s16[528,512]{1,0:T(8,128)(2,1)S(1)}, s16[528,512]{1,0:T(8,128)(2,1)S(1)}, f32[16,32,512]{2,1,0:T(8,128)}, f32[16,32,512]{2,1,0:T(8,128)}) custom-call(s32[32]{0:T(128)S(1)} %get-tuple-element.96.blk, s32[32]{0:T(128)S(1)} %get-tuple-element.95.prow, s32[8]{0:T(128)S(1)} %stack.62.pos, bf16[4,8,32,512]{3,2,1,0:T(8,128)(2,1)S(1)} %join.5.rest_0_, ...), custom_call_target="tpu_custom_call" | custom-call | flops 4294967296 | bytes 25165824 | tf_op jit(solution)/shard_map/partial/pallas_call | solution.py:255
  75.4 6.1 %collective-permute-done.14.refs_2_ = s16[528,512]{1,0:T(8,128)(2,1)S(1)} collective-permute-done((s16[528,512]{1,0:T(8,128)(2,1)S(1)}, s16[528,512]{1,0:T(8,128)(2,1)S(1)}, u32[]{:S(2)}, u32[]{:S(2)}) %collective-permute-start.14) | collective-permute-done | bytes 540704 | tf_op jit(solution)/shard_map/ppermute | solution.py:72
  81.6 3.2 %collective-permute-done.15.came_ref = s16[528,512]{1,0:T(8,128)(2,1)S(1)} collective-permute-done((s16[528,512]{1,0:T(8,128)(2,1)S(1)}, s16[528,512]{1,0:T(8,128)(2,1)S(1)}, u32[]{:S(2)}, u32[]{:S(2)}) %collective-permute-start.15) | collective-permute-done | bytes 540704 | tf_op jit(solution)/shard_map/ppermute | solution.py:72
  87.6 9.1 %partial.6 = (s16[528,512]{1,0:T(8,128)(2,1)S(1)}, s16[528,512]{1,0:T(8,128)(2,1)S(1)}, f32[16,32,512]{2,1,0:T(8,128)}, f32[16,32,512]{2,1,0:T(8,128)}) custom-call(s32[32]{0:T(128)S(1)} %get-tuple-element.96.blk, s32[32]{0:T(128)S(1)} %get-tuple-element.95.prow, s32[8]{0:T(128)S(1)} %stack.63.pos, bf16[2,8,32,512]{3,2,1,0:T(8,128)(2,1)S(1)} %join.6.rest_0_, ...), custom_call_target="tpu_custom_call" | custom-call | flops 4294967296 | bytes 25165824 | tf_op jit(solution)/shard_map/partial/pallas_call | solution.py:255
  100.0 3.0 %collective-permute-done.18.refs_4_ = s16[528,512]{1,0:T(8,128)(2,1)S(1)} collective-permute-done((s16[528,512]{1,0:T(8,128)(2,1)S(1)}, s16[528,512]{1,0:T(8,128)(2,1)S(1)}, u32[]{:S(2)}, u32[]{:S(2)}) %collective-permute-start.18) | collective-permute-done | bytes 540704 | tf_op jit(solution)/shard_map/ppermute | solution.py:72
  107.1 7.8 %partial.7 = (s16[528,512]{1,0:T(8,128)(2,1)S(1)}, s16[528,512]{1,0:T(8,128)(2,1)S(1)}, f32[16,32,512]{2,1,0:T(8,128)}, f32[16,32,512]{2,1,0:T(8,128)}) custom-call(s32[32]{0:T(128)S(1)} %get-tuple-element.96.blk, s32[32]{0:T(128)S(1)} %get-tuple-element.95.prow, s32[8]{0:T(128)S(1)} %stack.63.pos, bf16[2,8,32,512]{3,2,1,0:T(8,128)(2,1)S(1)} %join.7.rest_0_, ...), custom_call_target="tpu_custom_call" | custom-call | flops 4294967296 | bytes 25165824 | tf_op jit(solution)/shard_map/partial/pallas_call | solution.py:255
  117.3 2.7 %collective-permute-start.25 = (s16[272,512]{1,0:T(8,128)(2,1)S(1)}, s16[272,512]{1,0:T(8,128)(2,1)S(1)}, u32[]{:S(2)}, u32[]{:S(2)}) collective-permute-start(s16[272,512]{1,0:T(8,128)(2,1)S(1)} %get-tuple-element.81), channel_id=1, source_target_pairs={{0,1},{1,9},{2,3},{3,11},{4,5},{5,13},{6,7},{7,15},{8,0},{9,8},{10... | collective-permute-start | bytes 835592 | tf_op jit(solution)/shard_map/ppermute | solution.py:72
  121.1 7.1 %collective-permute-done.25.refs_1_ = s16[272,512]{1,0:T(8,128)(2,1)S(1)} collective-permute-done((s16[272,512]{1,0:T(8,128)(2,1)S(1)}, s16[272,512]{1,0:T(8,128)(2,1)S(1)}, u32[]{:S(2)}, u32[]{:S(2)}) %collective-permute-start.25) | collective-permute-done | bytes 278560 | tf_op jit(solution)/shard_map/ppermute | solution.py:72
  129.3 3.0 %collective-permute-done.27.refs_3_ = s16[272,512]{1,0:T(8,128)(2,1)S(1)} collective-permute-done((s16[272,512]{1,0:T(8,128)(2,1)S(1)}, s16[272,512]{1,0:T(8,128)(2,1)S(1)}, u32[]{:S(2)}, u32[]{:S(2)}) %collective-permute-start.27) | collective-permute-done | bytes 278560 | tf_op jit(solution)/shard_map/ppermute | solution.py:72
  135.6 3.1 %collective-permute-done.33.refs_1_ = s16[528,512]{1,0:T(8,128)(2,1)S(1)} collective-permute-done((s16[528,512]{1,0:T(8,128)(2,1)S(1)}, s16[528,512]{1,0:T(8,128)(2,1)S(1)}, u32[]{:S(2)}, u32[]{:S(2)}) %collective-permute-start.33) | collective-permute-done | bytes 540704 | tf_op jit(solution)/shard_map/ppermute | solution.py:72
  138.7 7.0 %collective-permute-done.34.refs_4_ = s16[528,512]{1,0:T(8,128)(2,1)S(1)} collective-permute-done((s16[528,512]{1,0:T(8,128)(2,1)S(1)}, s16[528,512]{1,0:T(8,128)(2,1)S(1)}, u32[]{:S(2)}, u32[]{:S(2)}) %collective-permute-start.34) | collective-permute-done | bytes 540704 | tf_op jit(solution)/shard_map/ppermute | solution.py:72
  152.3 2.5 %collective-permute-start.29 = (bf16[8,8,1024]{2,1,0:T(8,128)(2,1)S(1)}, bf16[8,8,1024]{2,1,0:T(8,128)(2,1)S(1)}, u32[]{:S(2)}, u32[]{:S(2)}) collective-permute-start(bf16[8,8,1024]{2,1,0:T(8,128)(2,1)S(1)} %get-tuple-element.106), channel_id=1, source_target_pairs={{0,4},{1,5},{2,6},{3,7},{4,0},{5,1},{6,2},{7,3},{8,12},{9,13},{10,... | collective-permute-start | bytes 393224 | tf_op jit(solution)/shard_map/ppermute | solution.py:72
  154.8 8.0 %collective-permute-done.36.refs_1_ = s16[272,512]{1,0:T(8,128)(2,1)S(1)} collective-permute-done((s16[272,512]{1,0:T(8,128)(2,1)S(1)}, s16[272,512]{1,0:T(8,128)(2,1)S(1)}, u32[]{:S(2)}, u32[]{:S(2)}) %collective-permute-start.36) | collective-permute-done | bytes 278560 | tf_op jit(solution)/shard_map/ppermute | solution.py:72
  166.0 3.1 %collective-permute-start.40 = (bf16[8,8,1024]{2,1,0:T(8,128)(2,1)S(1)}, bf16[8,8,1024]{2,1,0:T(8,128)(2,1)S(1)}, u32[]{:S(2)}, u32[]{:S(2)}) collective-permute-start(bf16[8,8,1024]{2,1,0:T(8,128)(2,1)S(1)} %get-tuple-element.102), channel_id=1, source_target_pairs={{0,4},{1,5},{2,6},{3,7},{4,0},{5,1},{6,2},{7,3},{8,12},{9,13},{10,... | collective-permute-start | bytes 393224 | tf_op jit(solution)/shard_map/ppermute | solution.py:72
  169.3 4.9 %collective-permute-done.39.refs_5_ = bf16[8,8,1024]{2,1,0:T(8,128)(2,1)S(1)} collective-permute-done((bf16[8,8,1024]{2,1,0:T(8,128)(2,1)S(1)}, bf16[8,8,1024]{2,1,0:T(8,128)(2,1)S(1)}, u32[]{:S(2)}, u32[]{:S(2)}) %collective-permute-start.39) | collective-permute-done | bytes 131104 | tf_op jit(solution)/shard_map/ppermute | solution.py:72
  (126 shorter events, 55.9 us)
Async XLA Ops:
  0.0 41.1 %collective-permute-start.8 = (bf16[32,512,256]{2,1,0:T(8,128)(2,1)}, bf16[32,512,256]{2,1,0:T(8,128)(2,1)}, u32[]{:S(2)}, u32[]{:S(2)}) collective-permute-start(bf16[32,512,256]{2,1,0:T(8,128)(2,1)} %own_ref.1), channel_id=1, source_target_pairs={{0,1},{1,0},{2,3},{3,2},{4,5},{5,4},{6,7},{7,6},{8,9},{9,8},{10,11... | collective-permute-start | bytes 25165832 | tf_op jit(solution)/shard_map/ppermute | solution.py:72
  15.5 14.4 %collective-permute-start.4 = (bf16[2,8,32,512]{3,2,1,0:T(8,128)(2,1)S(1)}, bf16[2,8,32,512]{3,2,1,0:T(8,128)(2,1)S(1)}, u32[]{:S(2)}, u32[]{:S(2)}) collective-permute-start(bf16[2,8,32,512]{3,2,1,0:T(8,128)(2,1)S(1)} %join.4.rest_0_), channel_id=1, source_target_pairs={{0,2},{1,7},{2,4},{3,1},{4,6},{5,3},{6,0},{7,5},{8,10},{9,15},{10,... | collective-permute-start | bytes 1572872 | tf_op jit(solution)/shard_map/ppermute | solution.py:72
  15.9 14.4 %collective-permute-start.5 = (bf16[2,8,32,512]{3,2,1,0:T(8,128)(2,1)S(1)}, bf16[2,8,32,512]{3,2,1,0:T(8,128)(2,1)S(1)}, u32[]{:S(2)}, u32[]{:S(2)}) collective-permute-start(bf16[2,8,32,512]{3,2,1,0:T(8,128)(2,1)S(1)} %join.4.rest_0_), channel_id=1, source_target_pairs={{0,6},{1,3},{2,0},{3,5},{4,2},{5,7},{6,4},{7,1},{8,14},{9,11},{10,... | collective-permute-start | bytes 1572872 | tf_op jit(solution)/shard_map/ppermute | solution.py:72
  19.7 16.7 %collective-permute-start.6 = (bf16[1,8,64,512]{3,2,1,0:T(8,128)(2,1)}, bf16[1,8,64,512]{3,2,1,0:T(8,128)(2,1)}, u32[]{:S(2)}, u32[]{:S(2)}) collective-permute-start(bf16[1,8,64,512]{3,2,1,0:T(8,128)(2,1)} %rest.1), channel_id=1, source_target_pairs={{0,8},{1,9},{2,10},{3,11},{4,12},{5,13},{6,14},{7,15},{8,0},{9,1},... | collective-permute-start | bytes 1572872 | tf_op jit(solution)/shard_map/ppermute | solution.py:72
  24.8 35.8 %collective-permute-start.11 = (bf16[4,8,32,512]{3,2,1,0:T(8,128)(2,1)S(1)}, bf16[4,8,32,512]{3,2,1,0:T(8,128)(2,1)}, u32[]{:S(2)}, u32[]{:S(2)}) collective-permute-start(bf16[4,8,32,512]{3,2,1,0:T(8,128)(2,1)S(1)} %join.5.rest_0_), channel_id=1, source_target_pairs={{0,8},{1,9},{2,10},{3,11},{4,12},{5,13},{6,14},{7,15},{8,0},{9,1},... | collective-permute-start | bytes 3145736 | tf_op jit(solution)/shard_map/ppermute | solution.py:72
  29.9 17.6 %collective-permute-start.7 = (bf16[2,8,32,512]{3,2,1,0:T(8,128)(2,1)S(1)}, bf16[2,8,32,512]{3,2,1,0:T(8,128)(2,1)}, u32[]{:S(2)}, u32[]{:S(2)}) collective-permute-start(bf16[2,8,32,512]{3,2,1,0:T(8,128)(2,1)S(1)} %collective-permute-done.4.rest_1_), channel_id=1, source_target_pairs={{0,2},{1,7},{2,4},{3,1},{4,6},{5,3},{6,0},{7,5},{8,10},{9,15},{10,... | collective-permute-start | bytes 1572872 | tf_op jit(solution)/shard_map/ppermute | solution.py:72
  37.5 20.8 %collective-permute-start.9 = (bf16[2,8,32,512]{3,2,1,0:T(8,128)(2,1)S(1)}, bf16[2,8,32,512]{3,2,1,0:T(8,128)(2,1)}, u32[]{:S(2)}, u32[]{:S(2)}) collective-permute-start(bf16[2,8,32,512]{3,2,1,0:T(8,128)(2,1)S(1)} %join.6.rest_0_), channel_id=1, source_target_pairs={{0,2},{1,7},{2,4},{3,1},{4,6},{5,3},{6,0},{7,5},{8,10},{9,15},{10,... | collective-permute-start | bytes 1572872 | tf_op jit(solution)/shard_map/ppermute | solution.py:72
  37.6 20.7 %collective-permute-start.10 = (bf16[2,8,32,512]{3,2,1,0:T(8,128)(2,1)S(1)}, bf16[2,8,32,512]{3,2,1,0:T(8,128)(2,1)}, u32[]{:S(2)}, u32[]{:S(2)}) collective-permute-start(bf16[2,8,32,512]{3,2,1,0:T(8,128)(2,1)S(1)} %join.6.rest_0_), channel_id=1, source_target_pairs={{0,6},{1,3},{2,0},{3,5},{4,2},{5,7},{6,4},{7,1},{8,14},{9,11},{10,... | collective-permute-start | bytes 1572872 | tf_op jit(solution)/shard_map/ppermute | solution.py:72
  56.4 17.1 %collective-permute-start.13 = (s16[528,512]{1,0:T(8,128)(2,1)S(1)}, s16[528,512]{1,0:T(8,128)(2,1)S(1)}, u32[]{:S(2)}, u32[]{:S(2)}) collective-permute-start(s16[528,512]{1,0:T(8,128)(2,1)S(1)} %get-tuple-element.57), channel_id=1, source_target_pairs={{0,32},{1,97},{2,34},{3,99},{4,36},{5,101},{6,38},{7,103},{8,40},{... | collective-permute-start | bytes 1622024 | tf_op jit(solution)/shard_map/ppermute | solution.py:72
  58.4 13.3 %collective-permute-start.12 = (s16[528,512]{1,0:T(8,128)(2,1)S(1)}, s16[528,512]{1,0:T(8,128)(2,1)S(1)}, u32[]{:S(2)}, u32[]{:S(2)}) collective-permute-start(s16[528,512]{1,0:T(8,128)(2,1)S(1)} %get-tuple-element.64), channel_id=1, source_target_pairs={{0,96},{1,33},{2,98},{3,35},{4,100},{5,37},{6,102},{7,39},{8,104},... | collective-permute-start | bytes 1622024 | tf_op jit(solution)/shard_map/ppermute | solution.py:72
  71.7 15.9 %collective-permute-start.16 = (bf16[2,8,32,512]{3,2,1,0:T(8,128)(2,1)}, bf16[2,8,32,512]{3,2,1,0:T(8,128)(2,1)S(1)}, u32[]{:S(2)}, u32[]{:S(2)}) collective-permute-start(bf16[2,8,32,512]{3,2,1,0:T(8,128)(2,1)} %collective-permute-done.9.rest_1_), channel_id=1, source_target_pairs={{0,2},{1,7},{2,4},{3,1},{4,6},{5,3},{6,0},{7,5},{8,10},{9,15},{10,... | collective-permute-start | bytes 1572872 | tf_op jit(solution)/shard_map/ppermute | solution.py:72
  71.7 25.0 %collective-permute-start.20 = (bf16[2,8,32,512]{3,2,1,0:T(8,128)(2,1)S(1)}, bf16[2,8,32,512]{3,2,1,0:T(8,128)(2,1)S(1)}, u32[]{:S(2)}, u32[]{:S(2)}) collective-permute-start(bf16[2,8,32,512]{3,2,1,0:T(8,128)(2,1)S(1)} %join.7.rest_0_), channel_id=1, source_target_pairs={{0,2},{1,7},{2,4},{3,1},{4,6},{5,3},{6,0},{7,5},{8,10},{9,15},{10,... | collective-permute-start | bytes 1572872 | tf_op jit(solution)/shard_map/ppermute | solution.py:72
  73.5 31.7 %collective-permute-start.21 = (bf16[2,8,32,512]{3,2,1,0:T(8,128)(2,1)S(1)}, bf16[2,8,32,512]{3,2,1,0:T(8,128)(2,1)S(1)}, u32[]{:S(2)}, u32[]{:S(2)}) collective-permute-start(bf16[2,8,32,512]{3,2,1,0:T(8,128)(2,1)S(1)} %join.7.rest_0_), channel_id=1, source_target_pairs={{0,6},{1,3},{2,0},{3,5},{4,2},{5,7},{6,4},{7,1},{8,14},{9,11},{10,... | collective-permute-start | bytes 1572872 | tf_op jit(solution)/shard_map/ppermute | solution.py:72
  86.5 16.5 %collective-permute-start.18 = (s16[528,512]{1,0:T(8,128)(2,1)S(1)}, s16[528,512]{1,0:T(8,128)(2,1)S(1)}, u32[]{:S(2)}, u32[]{:S(2)}) collective-permute-start(s16[528,512]{1,0:T(8,128)(2,1)S(1)} %relay.4), channel_id=1, source_target_pairs={{0,32},{1,97},{2,34},{3,99},{4,36},{5,101},{6,38},{7,103},{8,40},{... | collective-permute-start | bytes 1622024 | tf_op jit(solution)/shard_map/ppermute | solution.py:72
  96.7 23.3 %collective-permute-start.24 = (s16[528,512]{1,0:T(8,128)(2,1)S(1)}, s16[528,512]{1,0:T(8,128)(2,1)S(1)}, u32[]{:S(2)}, u32[]{:S(2)}) collective-permute-start(s16[528,512]{1,0:T(8,128)(2,1)S(1)} %get-tuple-element.70), channel_id=1, source_target_pairs={{0,32},{1,97},{2,34},{3,99},{4,36},{5,101},{6,38},{7,103},{8,40},{... | collective-permute-start | bytes 1622024 | tf_op jit(solution)/shard_map/ppermute | solution.py:72
  97.6 19.7 %collective-permute-start.23 = (s16[528,512]{1,0:T(8,128)(2,1)S(1)}, s16[528,512]{1,0:T(8,128)(2,1)S(1)}, u32[]{:S(2)}, u32[]{:S(2)}) collective-permute-start(s16[528,512]{1,0:T(8,128)(2,1)S(1)} %get-tuple-element.78), channel_id=1, source_target_pairs={{0,96},{1,33},{2,98},{3,35},{4,100},{5,37},{6,102},{7,39},{8,104},... | collective-permute-start | bytes 1622024 | tf_op jit(solution)/shard_map/ppermute | solution.py:72
  104.3 16.3 %collective-permute-start.19 = (s16[272,512]{1,0:T(8,128)(2,1)S(1)}, s16[272,512]{1,0:T(8,128)(2,1)S(1)}, u32[]{:S(2)}, u32[]{:S(2)}) collective-permute-start(s16[272,512]{1,0:T(8,128)(2,1)S(1)} %get-tuple-element.73), channel_id=1, source_target_pairs={{0,0},{1,8},{2,2},{3,10},{4,4},{5,12},{6,6},{7,14},{8,1},{9,9},{10... | collective-permute-start | bytes 835592 | tf_op jit(solution)/shard_map/ppermute | solution.py:72
  114.9 18.5 %collective-permute-start.31 = (s16[528,512]{1,0:T(8,128)(2,1)S(1)}, s16[528,512]{1,0:T(8,128)(2,1)S(1)}, u32[]{:S(2)}, u32[]{:S(2)}) collective-permute-start(s16[528,512]{1,0:T(8,128)(2,1)S(1)} %get-tuple-element.86), channel_id=1, source_target_pairs={{0,96},{1,33},{2,98},{3,35},{4,100},{5,37},{6,102},{7,39},{8,104},... | collective-permute-start | bytes 1622024 | tf_op jit(solution)/shard_map/ppermute | solution.py:72
  117.3 16.1 %collective-permute-start.32 = (s16[528,512]{1,0:T(8,128)(2,1)S(1)}, s16[528,512]{1,0:T(8,128)(2,1)S(1)}, u32[]{:S(2)}, u32[]{:S(2)}) collective-permute-start(s16[528,512]{1,0:T(8,128)(2,1)S(1)} %get-tuple-element.77), channel_id=1, source_target_pairs={{0,32},{1,97},{2,34},{3,99},{4,36},{5,101},{6,38},{7,103},{8,40},{... | collective-permute-start | bytes 1622024 | tf_op jit(solution)/shard_map/ppermute | solution.py:72
  148.9 13.9 %collective-permute-start.36 = (s16[272,512]{1,0:T(8,128)(2,1)S(1)}, s16[272,512]{1,0:T(8,128)(2,1)S(1)}, u32[]{:S(2)}, u32[]{:S(2)}) collective-permute-start(s16[272,512]{1,0:T(8,128)(2,1)S(1)} %get-tuple-element.92), channel_id=1, source_target_pairs={{0,1},{1,9},{2,3},{3,11},{4,5},{5,13},{6,7},{7,15},{8,0},{9,8},{10... | collective-permute-start | bytes 835592 | tf_op jit(solution)/shard_map/ppermute | solution.py:72
  150.4 14.2 %collective-permute-start.37 = (s16[272,512]{1,0:T(8,128)(2,1)S(1)}, s16[272,512]{1,0:T(8,128)(2,1)S(1)}, u32[]{:S(2)}, u32[]{:S(2)}) collective-permute-start(s16[272,512]{1,0:T(8,128)(2,1)S(1)} %get-tuple-element.93), channel_id=1, source_target_pairs={{0,16},{1,24},{2,18},{3,26},{4,20},{5,28},{6,22},{7,30},{8,17},{9,... | collective-permute-start | bytes 835592 | tf_op jit(solution)/shard_map/ppermute | solution.py:72
  150.7 14.1 %collective-permute-start.38 = (s16[272,512]{1,0:T(8,128)(2,1)S(1)}, s16[272,512]{1,0:T(8,128)(2,1)S(1)}, u32[]{:S(2)}, u32[]{:S(2)}) collective-permute-start(s16[272,512]{1,0:T(8,128)(2,1)S(1)} %get-tuple-element.94), channel_id=1, source_target_pairs={{0,17},{1,25},{2,19},{3,27},{4,21},{5,29},{6,23},{7,31},{8,16},{9,... | collective-permute-start | bytes 835592 | tf_op jit(solution)/shard_map/ppermute | solution.py:72
  152.2 16.9 %collective-permute-start.28 = (bf16[8,8,1024]{2,1,0:T(8,128)(2,1)S(1)}, bf16[8,8,1024]{2,1,0:T(8,128)(2,1)S(1)}, u32[]{:S(2)}, u32[]{:S(2)}) collective-permute-start(bf16[8,8,1024]{2,1,0:T(8,128)(2,1)S(1)} %get-tuple-element.107), channel_id=1, source_target_pairs={{0,2},{1,3},{2,4},{3,5},{4,6},{5,7},{6,0},{7,1},{8,10},{9,11},{10,... | collective-permute-start | bytes 393224 | tf_op jit(solution)/shard_map/ppermute | solution.py:72
  152.3 17.0 %collective-permute-start.29 = (bf16[8,8,1024]{2,1,0:T(8,128)(2,1)S(1)}, bf16[8,8,1024]{2,1,0:T(8,128)(2,1)S(1)}, u32[]{:S(2)}, u32[]{:S(2)}) collective-permute-start(bf16[8,8,1024]{2,1,0:T(8,128)(2,1)S(1)} %get-tuple-element.106), channel_id=1, source_target_pairs={{0,4},{1,5},{2,6},{3,7},{4,0},{5,1},{6,2},{7,3},{8,12},{9,13},{10,... | collective-permute-start | bytes 393224 | tf_op jit(solution)/shard_map/ppermute | solution.py:72
  (33 other events, 335.8 us)

commit v4 on v3

--- a/solution.py
+++ b/solution.py
@@ -21,8 +21,8 @@
     ("multiply", 0),
     ("relay", 1),
     ("relay", 0),
+    ("forward", 3),
     ("multiply", 2),
-    ("forward", 3),
     ("collect", (0, 1)),
     ("multiply", 3),
     ("relay", 2),
@@ -250,7 +250,7 @@
         return pl.BlockSpec(shape, lambda q, *_: (0,) * len(shape))
 
     message = jax.ShapeDtypeStruct((groups * rows + tail(groups), width), jnp.int16)
-    kept = pltpu.HBM((groups, rows, width), jnp.float32)
+    kept = jax.ShapeDtypeStruct((groups, rows, width), jnp.float32)
     flops = 2 * 8 * rows * 4 * depth * width * tiles
     return pl.pallas_call(
         partial_kernel,

time: 177 us -> 171 us (0.966)
  local copies, waits for them, and re-layouts: 10 us -> 6.34 us
  Pallas kernels: 50.2 us -> 46.9 us
    unnamed x30 -> x14, local copies, waits for them, and re-layouts: 6.39 us -> 2.7 us
    pallas_call x4, Pallas kernels: 34.9 us -> 31.6 us  [partial(): pl.pallas_call(partial_kernel, grid_spec=pltpu.PrefetchScalarGridSpec(num...]
  transfers between devices with their start and end apart: 42 -> 42, of which waited for: 19 -> 18; matrix products, arithmetic and copies ran while one was open for 2% -> 2% of each run, Pallas kernels for 27% -> 26%
where the time goes in v4:
time: 171 us
  waiting for transfers between devices  65.4 us (38%)
  starting transfers between devices  51 us (30%)
  Pallas kernels  46.9 us (27%)
  local copies, waits for them, and re-layouts  6.34 us (4%)
    ppermute x42, waiting for transfers between devices, move(): return lax.ppermute(array, ('row', 'col'), pairs)  65.4 us
    ppermute x42, starting transfers between devices, move(): return lax.ppermute(array, ('row', 'col'), pairs)  51 us
    pallas_call x4, Pallas kernels, partial(): pl.pallas_call(partial_kernel, grid_spec=pltpu.PrefetchScalarGridSpec(num...  31.6 us
    pallas_call x14, Pallas kernels, simple(): pl.pallas_call(kernel, out_shape=outs, in_specs=[smem] * scalars + [vmem]...  8.98 us
    pallas_call x1, Pallas kernels, stage(): pl.pallas_call(stage_kernel, out_shape=pltpu.VMEM((blocks, depth, 2 * hal...  6.33 us
  transfers between devices with their start and end apart: 42, of which 18 were waited for; matrix products, arithmetic and copies ran while one was open for 2% of the time, Pallas kernels for 26%

profile of v4, /device:TPU:0, one launch (start us, length us, event | category | flops | bytes accessed | tf_op | source)
XLA Modules:
  0.0 170.6 jit_solution(7809377070120788732)
XLA Ops:
  5.6 3.2 %collective-permute-start.2 = (bf16[1,8,32,512]{3,2,1,0:T(8,128)(2,1)S(1)}, bf16[1,8,32,512]{3,2,1,0:T(8,128)(2,1)S(1)}, u32[]{:S(2)}, u32[]{:S(2)}) collective-permute-start(bf16[1,8,32,512]{3,2,1,0:T(8,128)(2,1)S(1)} %reshape.33.refs_0_), channel_id=1, source_target_pairs={{0,8},{1,9},{2,10},{3,11},{4,12},{5,13},{6,14},{7,15},{8,0},{9,1},... | collective-permute-start | bytes 786440 | tf_op jit(solution)/shard_map/ppermute | solution.py:72
  12.6 2.8 %collective-permute-done.2.refs_1_ = bf16[1,8,32,512]{3,2,1,0:T(8,128)(2,1)S(1)} collective-permute-done((bf16[1,8,32,512]{3,2,1,0:T(8,128)(2,1)S(1)}, bf16[1,8,32,512]{3,2,1,0:T(8,128)(2,1)S(1)}, u32[]{:S(2)}, u32[]{:S(2)}) %collective-permute-start.2) | collective-permute-done | bytes 262176 | tf_op jit(solution)/shard_map/ppermute | solution.py:72
  15.9 3.0 %collective-permute-start.5 = (bf16[2,8,32,512]{3,2,1,0:T(8,128)(2,1)S(1)}, bf16[2,8,32,512]{3,2,1,0:T(8,128)(2,1)S(1)}, u32[]{:S(2)}, u32[]{:S(2)}) collective-permute-start(bf16[2,8,32,512]{3,2,1,0:T(8,128)(2,1)S(1)} %join.4.rest_0_), channel_id=1, source_target_pairs={{0,6},{1,3},{2,0},{3,5},{4,2},{5,7},{6,4},{7,1},{8,14},{9,11},{10,... | collective-permute-start | bytes 1572872 | tf_op jit(solution)/shard_map/ppermute | solution.py:72
  19.7 3.0 %collective-permute-start.6 = (bf16[1,8,64,512]{3,2,1,0:T(8,128)(2,1)}, bf16[1,8,64,512]{3,2,1,0:T(8,128)(2,1)}, u32[]{:S(2)}, u32[]{:S(2)}) collective-permute-start(bf16[1,8,64,512]{3,2,1,0:T(8,128)(2,1)} %rest.1), channel_id=1, source_target_pairs={{0,8},{1,9},{2,10},{3,11},{4,12},{5,13},{6,14},{7,15},{8,0},{9,1},... | collective-permute-start | bytes 1572872 | tf_op jit(solution)/shard_map/ppermute | solution.py:72
  25.3 4.5 %collective-permute-done.4.rest_1_ = bf16[2,8,32,512]{3,2,1,0:T(8,128)(2,1)S(1)} collective-permute-done((bf16[2,8,32,512]{3,2,1,0:T(8,128)(2,1)S(1)}, bf16[2,8,32,512]{3,2,1,0:T(8,128)(2,1)S(1)}, u32[]{:S(2)}, u32[]{:S(2)}) %collective-permute-start.4) | collective-permute-done | bytes 524320 | tf_op jit(solution)/shard_map/ppermute | solution.py:72
  31.0 5.3 %collective-permute-done.6 = bf16[1,8,64,512]{3,2,1,0:T(8,128)(2,1)} collective-permute-done((bf16[1,8,64,512]{3,2,1,0:T(8,128)(2,1)}, bf16[1,8,64,512]{3,2,1,0:T(8,128)(2,1)}, u32[]{:S(2)}, u32[]{:S(2)}) %collective-permute-start.6) | collective-permute-done | bytes 524320 | tf_op jit(solution)/shard_map/ppermute | solution.py:72
  37.6 3.2 %collective-permute-start.10 = (bf16[2,8,32,512]{3,2,1,0:T(8,128)(2,1)S(1)}, bf16[2,8,32,512]{3,2,1,0:T(8,128)(2,1)}, u32[]{:S(2)}, u32[]{:S(2)}) collective-permute-start(bf16[2,8,32,512]{3,2,1,0:T(8,128)(2,1)S(1)} %join.6.rest_0_), channel_id=1, source_target_pairs={{0,6},{1,3},{2,0},{3,5},{4,2},{5,7},{6,4},{7,1},{8,14},{9,11},{10,... | collective-permute-start | bytes 1572872 | tf_op jit(solution)/shard_map/ppermute | solution.py:72
  41.1 6.3 %stage.1.rest_4_.rest_2_ = bf16[32,512,512]{2,1,0:T(8,128)(2,1)S(1)} custom-call(s32[3]{0:T(128)S(1)} %pad_add_fusion.where, bf16[32,512,256]{2,1,0:T(8,128)(2,1)} %own_ref.1, bf16[32,512,256]{2,1,0:T(8,128)(2,1)} %collective-permute-done.8.came_ref), custom_call_target="tpu_custom_call" | custom-call | bytes 16777216 | tf_op jit(solution)/shard_map/stage/pallas_call | solution.py:232
  47.5 8.1 %partial.4 = (s16[528,512]{1,0:T(8,128)(2,1)S(1)}, s16[528,512]{1,0:T(8,128)(2,1)S(1)}, f32[16,32,512]{2,1,0:T(8,128)S(1)}, f32[16,32,512]{2,1,0:T(8,128)S(1)}) custom-call(s32[32]{0:T(128)S(1)} %get-tuple-element.96.blk, s32[32]{0:T(128)S(1)} %get-tuple-element.95.prow, s32[8]{0:T(128)S(1)} %stack.63.pos, bf16[2,8,32,512]{3,2,1,0:T(8,128)(2,1)S(1)} %join.4.rest_0_, ...), custom_call_target="tpu_custom_call" | custom-call | flops 4294967296 | bytes 25165824 | tf_op jit(solution)/shard_map/partial/pallas_call | solution.py:255
  59.8 8.2 %partial.5 = (s16[528,512]{1,0:T(8,128)(2,1)S(1)}, s16[528,512]{1,0:T(8,128)(2,1)S(1)}, f32[16,32,512]{2,1,0:T(8,128)S(1)}, f32[16,32,512]{2,1,0:T(8,128)S(1)}) custom-call(s32[32]{0:T(128)S(1)} %get-tuple-element.96.blk, s32[32]{0:T(128)S(1)} %get-tuple-element.95.prow, s32[8]{0:T(128)S(1)} %stack.62.pos, bf16[4,8,32,512]{3,2,1,0:T(8,128)(2,1)S(1)} %join.5.rest_0_, ...), custom_call_target="tpu_custom_call" | custom-call | flops 4294967296 | bytes 25165824 | tf_op jit(solution)/shard_map/partial/pallas_call | solution.py:255
  73.1 7.3 %collective-permute-done.14.refs_2_ = s16[528,512]{1,0:T(8,128)(2,1)S(1)} collective-permute-done((s16[528,512]{1,0:T(8,128)(2,1)S(1)}, s16[528,512]{1,0:T(8,128)(2,1)S(1)}, u32[]{:S(2)}, u32[]{:S(2)}) %collective-permute-start.14) | collective-permute-done | bytes 540704 | tf_op jit(solution)/shard_map/ppermute | solution.py:72
  80.5 3.5 %collective-permute-done.15.came_ref = s16[528,512]{1,0:T(8,128)(2,1)S(1)} collective-permute-done((s16[528,512]{1,0:T(8,128)(2,1)S(1)}, s16[528,512]{1,0:T(8,128)(2,1)S(1)}, u32[]{:S(2)}, u32[]{:S(2)}) %collective-permute-start.15) | collective-permute-done | bytes 540704 | tf_op jit(solution)/shard_map/ppermute | solution.py:72
  84.6 2.9 %collective-permute-start.21 = (bf16[2,8,32,512]{3,2,1,0:T(8,128)(2,1)S(1)}, bf16[2,8,32,512]{3,2,1,0:T(8,128)(2,1)S(1)}, u32[]{:S(2)}, u32[]{:S(2)}) collective-permute-start(bf16[2,8,32,512]{3,2,1,0:T(8,128)(2,1)S(1)} %join.7.rest_0_), channel_id=1, source_target_pairs={{0,6},{1,3},{2,0},{3,5},{4,2},{5,7},{6,4},{7,1},{8,14},{9,11},{10,... | collective-permute-start | bytes 1572872 | tf_op jit(solution)/shard_map/ppermute | solution.py:72
  87.5 8.2 %partial.6 = (s16[528,512]{1,0:T(8,128)(2,1)S(1)}, s16[528,512]{1,0:T(8,128)(2,1)S(1)}, f32[16,32,512]{2,1,0:T(8,128)S(1)}, f32[16,32,512]{2,1,0:T(8,128)S(1)}) custom-call(s32[32]{0:T(128)S(1)} %get-tuple-element.96.blk, s32[32]{0:T(128)S(1)} %get-tuple-element.95.prow, s32[8]{0:T(128)S(1)} %stack.63.pos, bf16[2,8,32,512]{3,2,1,0:T(8,128)(2,1)S(1)} %join.6.rest_0_, ...), custom_call_target="tpu_custom_call" | custom-call | flops 4294967296 | bytes 25165824 | tf_op jit(solution)/shard_map/partial/pallas_call | solution.py:255
  99.1 2.5 %collective-permute-done.18.refs_4_ = s16[528,512]{1,0:T(8,128)(2,1)S(1)} collective-permute-done((s16[528,512]{1,0:T(8,128)(2,1)S(1)}, s16[528,512]{1,0:T(8,128)(2,1)S(1)}, u32[]{:S(2)}, u32[]{:S(2)}) %collective-permute-start.18) | collective-permute-done | bytes 540704 | tf_op jit(solution)/shard_map/ppermute | solution.py:72
  103.5 7.0 %partial.7 = (s16[528,512]{1,0:T(8,128)(2,1)S(1)}, s16[528,512]{1,0:T(8,128)(2,1)S(1)}, f32[16,32,512]{2,1,0:T(8,128)S(1)}, f32[16,32,512]{2,1,0:T(8,128)S(1)}) custom-call(s32[32]{0:T(128)S(1)} %get-tuple-element.96.blk, s32[32]{0:T(128)S(1)} %get-tuple-element.95.prow, s32[8]{0:T(128)S(1)} %stack.63.pos, bf16[2,8,32,512]{3,2,1,0:T(8,128)(2,1)S(1)} %join.7.rest_0_, ...), custom_call_target="tpu_custom_call" | custom-call | flops 4294967296 | bytes 25165824 | tf_op jit(solution)/shard_map/partial/pallas_call | solution.py:255
  112.6 5.1 %collective-permute-start.25 = (s16[272,512]{1,0:T(8,128)(2,1)S(1)}, s16[272,512]{1,0:T(8,128)(2,1)S(1)}, u32[]{:S(2)}, u32[]{:S(2)}) collective-permute-start(s16[272,512]{1,0:T(8,128)(2,1)S(1)} %get-tuple-element.81), channel_id=1, source_target_pairs={{0,1},{1,9},{2,3},{3,11},{4,5},{5,13},{6,7},{7,15},{8,0},{9,8},{10... | collective-permute-start | bytes 835592 | tf_op jit(solution)/shard_map/ppermute | solution.py:72
  118.6 5.2 %collective-permute-done.25.refs_1_ = s16[272,512]{1,0:T(8,128)(2,1)S(1)} collective-permute-done((s16[272,512]{1,0:T(8,128)(2,1)S(1)}, s16[272,512]{1,0:T(8,128)(2,1)S(1)}, u32[]{:S(2)}, u32[]{:S(2)}) %collective-permute-start.25) | collective-permute-done | bytes 278560 | tf_op jit(solution)/shard_map/ppermute | solution.py:72
  125.1 3.9 %collective-permute-done.27.refs_3_ = s16[272,512]{1,0:T(8,128)(2,1)S(1)} collective-permute-done((s16[272,512]{1,0:T(8,128)(2,1)S(1)}, s16[272,512]{1,0:T(8,128)(2,1)S(1)}, u32[]{:S(2)}, u32[]{:S(2)}) %collective-permute-start.27) | collective-permute-done | bytes 278560 | tf_op jit(solution)/shard_map/ppermute | solution.py:72
  130.6 3.8 %collective-permute-done.33.refs_1_ = s16[528,512]{1,0:T(8,128)(2,1)S(1)} collective-permute-done((s16[528,512]{1,0:T(8,128)(2,1)S(1)}, s16[528,512]{1,0:T(8,128)(2,1)S(1)}, u32[]{:S(2)}, u32[]{:S(2)}) %collective-permute-start.33) | collective-permute-done | bytes 540704 | tf_op jit(solution)/shard_map/ppermute | solution.py:72
  134.4 6.7 %collective-permute-done.34.refs_4_ = s16[528,512]{1,0:T(8,128)(2,1)S(1)} collective-permute-done((s16[528,512]{1,0:T(8,128)(2,1)S(1)}, s16[528,512]{1,0:T(8,128)(2,1)S(1)}, u32[]{:S(2)}, u32[]{:S(2)}) %collective-permute-start.34) | collective-permute-done | bytes 540704 | tf_op jit(solution)/shard_map/ppermute | solution.py:72
  148.9 7.6 %collective-permute-done.36.refs_1_ = s16[272,512]{1,0:T(8,128)(2,1)S(1)} collective-permute-done((s16[272,512]{1,0:T(8,128)(2,1)S(1)}, s16[272,512]{1,0:T(8,128)(2,1)S(1)}, u32[]{:S(2)}, u32[]{:S(2)}) %collective-permute-start.36) | collective-permute-done | bytes 278560 | tf_op jit(solution)/shard_map/ppermute | solution.py:72
  159.8 3.0 %collective-permute-start.40 = (bf16[8,8,1024]{2,1,0:T(8,128)(2,1)S(1)}, bf16[8,8,1024]{2,1,0:T(8,128)(2,1)S(1)}, u32[]{:S(2)}, u32[]{:S(2)}) collective-permute-start(bf16[8,8,1024]{2,1,0:T(8,128)(2,1)S(1)} %get-tuple-element.102), channel_id=1, source_target_pairs={{0,4},{1,5},{2,6},{3,7},{4,0},{5,1},{6,2},{7,3},{8,12},{9,13},{10,... | collective-permute-start | bytes 393224 | tf_op jit(solution)/shard_map/ppermute | solution.py:72
  163.1 5.3 %collective-permute-done.39.refs_5_ = bf16[8,8,1024]{2,1,0:T(8,128)(2,1)S(1)} collective-permute-done((bf16[8,8,1024]{2,1,0:T(8,128)(2,1)S(1)}, bf16[8,8,1024]{2,1,0:T(8,128)(2,1)S(1)}, u32[]{:S(2)}, u32[]{:S(2)}) %collective-permute-start.39) | collective-permute-done | bytes 131104 | tf_op jit(solution)/shard_map/ppermute | solution.py:72
  (110 shorter events, 50.3 us)
Async XLA Ops:
  0.0 41.1 %collective-permute-start.8 = (bf16[32,512,256]{2,1,0:T(8,128)(2,1)}, bf16[32,512,256]{2,1,0:T(8,128)(2,1)}, u32[]{:S(2)}, u32[]{:S(2)}) collective-permute-start(bf16[32,512,256]{2,1,0:T(8,128)(2,1)} %own_ref.1), channel_id=1, source_target_pairs={{0,1},{1,0},{2,3},{3,2},{4,5},{5,4},{6,7},{7,6},{8,9},{9,8},{10,11... | collective-permute-start | bytes 25165832 | tf_op jit(solution)/shard_map/ppermute | solution.py:72
  15.5 14.4 %collective-permute-start.4 = (bf16[2,8,32,512]{3,2,1,0:T(8,128)(2,1)S(1)}, bf16[2,8,32,512]{3,2,1,0:T(8,128)(2,1)S(1)}, u32[]{:S(2)}, u32[]{:S(2)}) collective-permute-start(bf16[2,8,32,512]{3,2,1,0:T(8,128)(2,1)S(1)} %join.4.rest_0_), channel_id=1, source_target_pairs={{0,2},{1,7},{2,4},{3,1},{4,6},{5,3},{6,0},{7,5},{8,10},{9,15},{10,... | collective-permute-start | bytes 1572872 | tf_op jit(solution)/shard_map/ppermute | solution.py:72
  15.9 14.4 %collective-permute-start.5 = (bf16[2,8,32,512]{3,2,1,0:T(8,128)(2,1)S(1)}, bf16[2,8,32,512]{3,2,1,0:T(8,128)(2,1)S(1)}, u32[]{:S(2)}, u32[]{:S(2)}) collective-permute-start(bf16[2,8,32,512]{3,2,1,0:T(8,128)(2,1)S(1)} %join.4.rest_0_), channel_id=1, source_target_pairs={{0,6},{1,3},{2,0},{3,5},{4,2},{5,7},{6,4},{7,1},{8,14},{9,11},{10,... | collective-permute-start | bytes 1572872 | tf_op jit(solution)/shard_map/ppermute | solution.py:72
  19.7 16.7 %collective-permute-start.6 = (bf16[1,8,64,512]{3,2,1,0:T(8,128)(2,1)}, bf16[1,8,64,512]{3,2,1,0:T(8,128)(2,1)}, u32[]{:S(2)}, u32[]{:S(2)}) collective-permute-start(bf16[1,8,64,512]{3,2,1,0:T(8,128)(2,1)} %rest.1), channel_id=1, source_target_pairs={{0,8},{1,9},{2,10},{3,11},{4,12},{5,13},{6,14},{7,15},{8,0},{9,1},... | collective-permute-start | bytes 1572872 | tf_op jit(solution)/shard_map/ppermute | solution.py:72
  24.7 35.1 %collective-permute-start.11 = (bf16[4,8,32,512]{3,2,1,0:T(8,128)(2,1)S(1)}, bf16[4,8,32,512]{3,2,1,0:T(8,128)(2,1)}, u32[]{:S(2)}, u32[]{:S(2)}) collective-permute-start(bf16[4,8,32,512]{3,2,1,0:T(8,128)(2,1)S(1)} %join.5.rest_0_), channel_id=1, source_target_pairs={{0,8},{1,9},{2,10},{3,11},{4,12},{5,13},{6,14},{7,15},{8,0},{9,1},... | collective-permute-start | bytes 3145736 | tf_op jit(solution)/shard_map/ppermute | solution.py:72
  29.9 17.6 %collective-permute-start.7 = (bf16[2,8,32,512]{3,2,1,0:T(8,128)(2,1)S(1)}, bf16[2,8,32,512]{3,2,1,0:T(8,128)(2,1)}, u32[]{:S(2)}, u32[]{:S(2)}) collective-permute-start(bf16[2,8,32,512]{3,2,1,0:T(8,128)(2,1)S(1)} %collective-permute-done.4.rest_1_), channel_id=1, source_target_pairs={{0,2},{1,7},{2,4},{3,1},{4,6},{5,3},{6,0},{7,5},{8,10},{9,15},{10,... | collective-permute-start | bytes 1572872 | tf_op jit(solution)/shard_map/ppermute | solution.py:72
  37.5 20.1 %collective-permute-start.9 = (bf16[2,8,32,512]{3,2,1,0:T(8,128)(2,1)S(1)}, bf16[2,8,32,512]{3,2,1,0:T(8,128)(2,1)}, u32[]{:S(2)}, u32[]{:S(2)}) collective-permute-start(bf16[2,8,32,512]{3,2,1,0:T(8,128)(2,1)S(1)} %join.6.rest_0_), channel_id=1, source_target_pairs={{0,2},{1,7},{2,4},{3,1},{4,6},{5,3},{6,0},{7,5},{8,10},{9,15},{10,... | collective-permute-start | bytes 1572872 | tf_op jit(solution)/shard_map/ppermute | solution.py:72
  37.6 20.0 %collective-permute-start.10 = (bf16[2,8,32,512]{3,2,1,0:T(8,128)(2,1)S(1)}, bf16[2,8,32,512]{3,2,1,0:T(8,128)(2,1)}, u32[]{:S(2)}, u32[]{:S(2)}) collective-permute-start(bf16[2,8,32,512]{3,2,1,0:T(8,128)(2,1)S(1)} %join.6.rest_0_), channel_id=1, source_target_pairs={{0,6},{1,3},{2,0},{3,5},{4,2},{5,7},{6,4},{7,1},{8,14},{9,11},{10,... | collective-permute-start | bytes 1572872 | tf_op jit(solution)/shard_map/ppermute | solution.py:72
  55.6 17.1 %collective-permute-start.13 = (s16[528,512]{1,0:T(8,128)(2,1)S(1)}, s16[528,512]{1,0:T(8,128)(2,1)S(1)}, u32[]{:S(2)}, u32[]{:S(2)}) collective-permute-start(s16[528,512]{1,0:T(8,128)(2,1)S(1)} %get-tuple-element.57), channel_id=1, source_target_pairs={{0,32},{1,97},{2,34},{3,99},{4,36},{5,101},{6,38},{7,103},{8,40},{... | collective-permute-start | bytes 1622024 | tf_op jit(solution)/shard_map/ppermute | solution.py:72
  70.1 13.9 %collective-permute-start.15 = (s16[528,512]{1,0:T(8,128)(2,1)S(1)}, s16[528,512]{1,0:T(8,128)(2,1)S(1)}, u32[]{:S(2)}, u32[]{:S(2)}) collective-permute-start(s16[528,512]{1,0:T(8,128)(2,1)S(1)} %get-tuple-element.63), channel_id=1, source_target_pairs={{0,32},{1,97},{2,34},{3,99},{4,36},{5,101},{6,38},{7,103},{8,40},{... | collective-permute-start | bytes 1622024 | tf_op jit(solution)/shard_map/ppermute | solution.py:72
  70.2 17.3 %collective-permute-start.20 = (bf16[2,8,32,512]{3,2,1,0:T(8,128)(2,1)S(1)}, bf16[2,8,32,512]{3,2,1,0:T(8,128)(2,1)S(1)}, u32[]{:S(2)}, u32[]{:S(2)}) collective-permute-start(bf16[2,8,32,512]{3,2,1,0:T(8,128)(2,1)S(1)} %join.7.rest_0_), channel_id=1, source_target_pairs={{0,2},{1,7},{2,4},{3,1},{4,6},{5,3},{6,0},{7,5},{8,10},{9,15},{10,... | collective-permute-start | bytes 1572872 | tf_op jit(solution)/shard_map/ppermute | solution.py:72
  70.2 17.3 %collective-permute-start.16 = (bf16[2,8,32,512]{3,2,1,0:T(8,128)(2,1)}, bf16[2,8,32,512]{3,2,1,0:T(8,128)(2,1)S(1)}, u32[]{:S(2)}, u32[]{:S(2)}) collective-permute-start(bf16[2,8,32,512]{3,2,1,0:T(8,128)(2,1)} %collective-permute-done.9.rest_1_), channel_id=1, source_target_pairs={{0,2},{1,7},{2,4},{3,1},{4,6},{5,3},{6,0},{7,5},{8,10},{9,15},{10,... | collective-permute-start | bytes 1572872 | tf_op jit(solution)/shard_map/ppermute | solution.py:72
  84.5 17.0 %collective-permute-start.18 = (s16[528,512]{1,0:T(8,128)(2,1)S(1)}, s16[528,512]{1,0:T(8,128)(2,1)S(1)}, u32[]{:S(2)}, u32[]{:S(2)}) collective-permute-start(s16[528,512]{1,0:T(8,128)(2,1)S(1)} %relay.4), channel_id=1, source_target_pairs={{0,32},{1,97},{2,34},{3,99},{4,36},{5,101},{6,38},{7,103},{8,40},{... | collective-permute-start | bytes 1622024 | tf_op jit(solution)/shard_map/ppermute | solution.py:72
  84.6 18.9 %collective-permute-start.21 = (bf16[2,8,32,512]{3,2,1,0:T(8,128)(2,1)S(1)}, bf16[2,8,32,512]{3,2,1,0:T(8,128)(2,1)S(1)}, u32[]{:S(2)}, u32[]{:S(2)}) collective-permute-start(bf16[2,8,32,512]{3,2,1,0:T(8,128)(2,1)S(1)} %join.7.rest_0_), channel_id=1, source_target_pairs={{0,6},{1,3},{2,0},{3,5},{4,2},{5,7},{6,4},{7,1},{8,14},{9,11},{10,... | collective-permute-start | bytes 1572872 | tf_op jit(solution)/shard_map/ppermute | solution.py:72
  87.5 16.0 %collective-permute-start.22 = (bf16[2,8,32,512]{3,2,1,0:T(8,128)(2,1)S(1)}, bf16[2,8,32,512]{3,2,1,0:T(8,128)(2,1)S(1)}, u32[]{:S(2)}, u32[]{:S(2)}) collective-permute-start(bf16[2,8,32,512]{3,2,1,0:T(8,128)(2,1)S(1)} %collective-permute-done.20.rest_1_), channel_id=1, source_target_pairs={{0,2},{1,7},{2,4},{3,1},{4,6},{5,3},{6,0},{7,5},{8,10},{9,15},{10,... | collective-permute-start | bytes 1572872 | tf_op jit(solution)/shard_map/ppermute | solution.py:72
  95.7 21.9 %collective-permute-start.24 = (s16[528,512]{1,0:T(8,128)(2,1)S(1)}, s16[528,512]{1,0:T(8,128)(2,1)S(1)}, u32[]{:S(2)}, u32[]{:S(2)}) collective-permute-start(s16[528,512]{1,0:T(8,128)(2,1)S(1)} %get-tuple-element.70), channel_id=1, source_target_pairs={{0,32},{1,97},{2,34},{3,99},{4,36},{5,101},{6,38},{7,103},{8,40},{... | collective-permute-start | bytes 1622024 | tf_op jit(solution)/shard_map/ppermute | solution.py:72
  98.0 14.6 %collective-permute-start.23 = (s16[528,512]{1,0:T(8,128)(2,1)S(1)}, s16[528,512]{1,0:T(8,128)(2,1)S(1)}, u32[]{:S(2)}, u32[]{:S(2)}) collective-permute-start(s16[528,512]{1,0:T(8,128)(2,1)S(1)} %get-tuple-element.78), channel_id=1, source_target_pairs={{0,96},{1,33},{2,98},{3,35},{4,100},{5,37},{6,102},{7,39},{8,104},... | collective-permute-start | bytes 1622024 | tf_op jit(solution)/shard_map/ppermute | solution.py:72
  102.8 15.4 %collective-permute-start.19 = (s16[272,512]{1,0:T(8,128)(2,1)S(1)}, s16[272,512]{1,0:T(8,128)(2,1)S(1)}, u32[]{:S(2)}, u32[]{:S(2)}) collective-permute-start(s16[272,512]{1,0:T(8,128)(2,1)S(1)} %get-tuple-element.73), channel_id=1, source_target_pairs={{0,0},{1,8},{2,2},{3,10},{4,4},{5,12},{6,6},{7,14},{8,1},{9,9},{10... | collective-permute-start | bytes 835592 | tf_op jit(solution)/shard_map/ppermute | solution.py:72
  110.5 19.5 %collective-permute-start.31 = (s16[528,512]{1,0:T(8,128)(2,1)S(1)}, s16[528,512]{1,0:T(8,128)(2,1)S(1)}, u32[]{:S(2)}, u32[]{:S(2)}) collective-permute-start(s16[528,512]{1,0:T(8,128)(2,1)S(1)} %get-tuple-element.86), channel_id=1, source_target_pairs={{0,96},{1,33},{2,98},{3,35},{4,100},{5,37},{6,102},{7,39},{8,104},... | collective-permute-start | bytes 1622024 | tf_op jit(solution)/shard_map/ppermute | solution.py:72
  110.6 19.5 %collective-permute-start.32 = (s16[528,512]{1,0:T(8,128)(2,1)S(1)}, s16[528,512]{1,0:T(8,128)(2,1)S(1)}, u32[]{:S(2)}, u32[]{:S(2)}) collective-permute-start(s16[528,512]{1,0:T(8,128)(2,1)S(1)} %get-tuple-element.77), channel_id=1, source_target_pairs={{0,32},{1,97},{2,34},{3,99},{4,36},{5,101},{6,38},{7,103},{8,40},{... | collective-permute-start | bytes 1622024 | tf_op jit(solution)/shard_map/ppermute | solution.py:72
  144.3 13.9 %collective-permute-start.37 = (s16[272,512]{1,0:T(8,128)(2,1)S(1)}, s16[272,512]{1,0:T(8,128)(2,1)S(1)}, u32[]{:S(2)}, u32[]{:S(2)}) collective-permute-start(s16[272,512]{1,0:T(8,128)(2,1)S(1)} %get-tuple-element.93), channel_id=1, source_target_pairs={{0,16},{1,24},{2,18},{3,26},{4,20},{5,28},{6,22},{7,30},{8,17},{9,... | collective-permute-start | bytes 835592 | tf_op jit(solution)/shard_map/ppermute | solution.py:72
  144.9 13.7 %collective-permute-start.38 = (s16[272,512]{1,0:T(8,128)(2,1)S(1)}, s16[272,512]{1,0:T(8,128)(2,1)S(1)}, u32[]{:S(2)}, u32[]{:S(2)}) collective-permute-start(s16[272,512]{1,0:T(8,128)(2,1)S(1)} %get-tuple-element.94), channel_id=1, source_target_pairs={{0,17},{1,25},{2,19},{3,27},{4,21},{5,29},{6,23},{7,31},{8,16},{9,... | collective-permute-start | bytes 835592 | tf_op jit(solution)/shard_map/ppermute | solution.py:72
  146.4 16.4 %collective-permute-start.28 = (bf16[8,8,1024]{2,1,0:T(8,128)(2,1)S(1)}, bf16[8,8,1024]{2,1,0:T(8,128)(2,1)S(1)}, u32[]{:S(2)}, u32[]{:S(2)}) collective-permute-start(bf16[8,8,1024]{2,1,0:T(8,128)(2,1)S(1)} %get-tuple-element.107), channel_id=1, source_target_pairs={{0,2},{1,3},{2,4},{3,5},{4,6},{5,7},{6,0},{7,1},{8,10},{9,11},{10,... | collective-permute-start | bytes 393224 | tf_op jit(solution)/shard_map/ppermute | solution.py:72
  146.5 16.6 %collective-permute-start.29 = (bf16[8,8,1024]{2,1,0:T(8,128)(2,1)S(1)}, bf16[8,8,1024]{2,1,0:T(8,128)(2,1)S(1)}, u32[]{:S(2)}, u32[]{:S(2)}) collective-permute-start(bf16[8,8,1024]{2,1,0:T(8,128)(2,1)S(1)} %get-tuple-element.106), channel_id=1, source_target_pairs={{0,4},{1,5},{2,6},{3,7},{4,0},{5,1},{6,2},{7,3},{8,12},{9,13},{10,... | collective-permute-start | bytes 393224 | tf_op jit(solution)/shard_map/ppermute | solution.py:72
  (25 other events, 228.7 us)

commit v5 on v4

--- a/solution.py
+++ b/solution.py
@@ -20,8 +20,8 @@
     ("join", 3),
     ("multiply", 0),
     ("relay", 1),
+    ("forward", 3),
     ("relay", 0),
-    ("forward", 3),
     ("multiply", 2),
     ("collect", (0, 1)),
     ("multiply", 3),

time: 171 us -> 171 us (level)
  no operation moved by 1% of the time
where the time goes in v5:
time: 171 us
  waiting for transfers between devices  65.4 us (38%)
  starting transfers between devices  51 us (30%)
  Pallas kernels  46.9 us (27%)
  local copies, waits for them, and re-layouts  6.34 us (4%)
    ppermute x42, waiting for transfers between devices, move(): return lax.ppermute(array, ('row', 'col'), pairs)  65.4 us
    ppermute x42, starting transfers between devices, move(): return lax.ppermute(array, ('row', 'col'), pairs)  51 us
    pallas_call x4, Pallas kernels, partial(): pl.pallas_call(partial_kernel, grid_spec=pltpu.PrefetchScalarGridSpec(num...  31.6 us
    pallas_call x14, Pallas kernels, simple(): pl.pallas_call(kernel, out_shape=outs, in_specs=[smem] * scalars + [vmem]...  8.98 us
    pallas_call x1, Pallas kernels, stage(): pl.pallas_call(stage_kernel, out_shape=pltpu.VMEM((blocks, depth, 2 * hal...  6.33 us
  transfers between devices with their start and end apart: 42, of which 18 were waited for; matrix products, arithmetic and copies ran while one was open for 2% of the time, Pallas kernels for 26%

profile of v5, /device:TPU:0, one launch (start us, length us, event | category | flops | bytes accessed | tf_op | source)
XLA Modules:
  0.0 170.6 jit_solution(7809377070120788732)
XLA Ops:
  5.6 3.2 %collective-permute-start.2 = (bf16[1,8,32,512]{3,2,1,0:T(8,128)(2,1)S(1)}, bf16[1,8,32,512]{3,2,1,0:T(8,128)(2,1)S(1)}, u32[]{:S(2)}, u32[]{:S(2)}) collective-permute-start(bf16[1,8,32,512]{3,2,1,0:T(8,128)(2,1)S(1)} %reshape.33.refs_0_), channel_id=1, source_target_pairs={{0,8},{1,9},{2,10},{3,11},{4,12},{5,13},{6,14},{7,15},{8,0},{9,1},... | collective-permute-start | bytes 786440 | tf_op jit(solution)/shard_map/ppermute | solution.py:72
  12.6 2.8 %collective-permute-done.2.refs_1_ = bf16[1,8,32,512]{3,2,1,0:T(8,128)(2,1)S(1)} collective-permute-done((bf16[1,8,32,512]{3,2,1,0:T(8,128)(2,1)S(1)}, bf16[1,8,32,512]{3,2,1,0:T(8,128)(2,1)S(1)}, u32[]{:S(2)}, u32[]{:S(2)}) %collective-permute-start.2) | collective-permute-done | bytes 262176 | tf_op jit(solution)/shard_map/ppermute | solution.py:72
  15.9 3.0 %collective-permute-start.5 = (bf16[2,8,32,512]{3,2,1,0:T(8,128)(2,1)S(1)}, bf16[2,8,32,512]{3,2,1,0:T(8,128)(2,1)S(1)}, u32[]{:S(2)}, u32[]{:S(2)}) collective-permute-start(bf16[2,8,32,512]{3,2,1,0:T(8,128)(2,1)S(1)} %join.4.rest_0_), channel_id=1, source_target_pairs={{0,6},{1,3},{2,0},{3,5},{4,2},{5,7},{6,4},{7,1},{8,14},{9,11},{10,... | collective-permute-start | bytes 1572872 | tf_op jit(solution)/shard_map/ppermute | solution.py:72
  19.7 3.0 %collective-permute-start.6 = (bf16[1,8,64,512]{3,2,1,0:T(8,128)(2,1)}, bf16[1,8,64,512]{3,2,1,0:T(8,128)(2,1)}, u32[]{:S(2)}, u32[]{:S(2)}) collective-permute-start(bf16[1,8,64,512]{3,2,1,0:T(8,128)(2,1)} %rest.1), channel_id=1, source_target_pairs={{0,8},{1,9},{2,10},{3,11},{4,12},{5,13},{6,14},{7,15},{8,0},{9,1},... | collective-permute-start | bytes 1572872 | tf_op jit(solution)/shard_map/ppermute | solution.py:72
  25.3 4.5 %collective-permute-done.4.rest_1_ = bf16[2,8,32,512]{3,2,1,0:T(8,128)(2,1)S(1)} collective-permute-done((bf16[2,8,32,512]{3,2,1,0:T(8,128)(2,1)S(1)}, bf16[2,8,32,512]{3,2,1,0:T(8,128)(2,1)S(1)}, u32[]{:S(2)}, u32[]{:S(2)}) %collective-permute-start.4) | collective-permute-done | bytes 524320 | tf_op jit(solution)/shard_map/ppermute | solution.py:72
  31.0 5.3 %collective-permute-done.6 = bf16[1,8,64,512]{3,2,1,0:T(8,128)(2,1)} collective-permute-done((bf16[1,8,64,512]{3,2,1,0:T(8,128)(2,1)}, bf16[1,8,64,512]{3,2,1,0:T(8,128)(2,1)}, u32[]{:S(2)}, u32[]{:S(2)}) %collective-permute-start.6) | collective-permute-done | bytes 524320 | tf_op jit(solution)/shard_map/ppermute | solution.py:72
  37.6 3.2 %collective-permute-start.10 = (bf16[2,8,32,512]{3,2,1,0:T(8,128)(2,1)S(1)}, bf16[2,8,32,512]{3,2,1,0:T(8,128)(2,1)}, u32[]{:S(2)}, u32[]{:S(2)}) collective-permute-start(bf16[2,8,32,512]{3,2,1,0:T(8,128)(2,1)S(1)} %join.6.rest_0_), channel_id=1, source_target_pairs={{0,6},{1,3},{2,0},{3,5},{4,2},{5,7},{6,4},{7,1},{8,14},{9,11},{10,... | collective-permute-start | bytes 1572872 | tf_op jit(solution)/shard_map/ppermute | solution.py:72
  41.1 6.3 %stage.1.rest_4_.rest_2_ = bf16[32,512,512]{2,1,0:T(8,128)(2,1)S(1)} custom-call(s32[3]{0:T(128)S(1)} %pad_add_fusion.where, bf16[32,512,256]{2,1,0:T(8,128)(2,1)} %own_ref.1, bf16[32,512,256]{2,1,0:T(8,128)(2,1)} %collective-permute-done.8.came_ref), custom_call_target="tpu_custom_call" | custom-call | bytes 16777216 | tf_op jit(solution)/shard_map/stage/pallas_call | solution.py:232
  47.5 8.1 %partial.4 = (s16[528,512]{1,0:T(8,128)(2,1)S(1)}, s16[528,512]{1,0:T(8,128)(2,1)S(1)}, f32[16,32,512]{2,1,0:T(8,128)S(1)}, f32[16,32,512]{2,1,0:T(8,128)S(1)}) custom-call(s32[32]{0:T(128)S(1)} %get-tuple-element.96.blk, s32[32]{0:T(128)S(1)} %get-tuple-element.95.prow, s32[8]{0:T(128)S(1)} %stack.63.pos, bf16[2,8,32,512]{3,2,1,0:T(8,128)(2,1)S(1)} %join.4.rest_0_, ...), custom_call_target="tpu_custom_call" | custom-call | flops 4294967296 | bytes 25165824 | tf_op jit(solution)/shard_map/partial/pallas_call | solution.py:255
  59.8 8.2 %partial.5 = (s16[528,512]{1,0:T(8,128)(2,1)S(1)}, s16[528,512]{1,0:T(8,128)(2,1)S(1)}, f32[16,32,512]{2,1,0:T(8,128)S(1)}, f32[16,32,512]{2,1,0:T(8,128)S(1)}) custom-call(s32[32]{0:T(128)S(1)} %get-tuple-element.96.blk, s32[32]{0:T(128)S(1)} %get-tuple-element.95.prow, s32[8]{0:T(128)S(1)} %stack.62.pos, bf16[4,8,32,512]{3,2,1,0:T(8,128)(2,1)S(1)} %join.5.rest_0_, ...), custom_call_target="tpu_custom_call" | custom-call | flops 4294967296 | bytes 25165824 | tf_op jit(solution)/shard_map/partial/pallas_call | solution.py:255
  73.1 7.3 %collective-permute-done.14.refs_2_ = s16[528,512]{1,0:T(8,128)(2,1)S(1)} collective-permute-done((s16[528,512]{1,0:T(8,128)(2,1)S(1)}, s16[528,512]{1,0:T(8,128)(2,1)S(1)}, u32[]{:S(2)}, u32[]{:S(2)}) %collective-permute-start.14) | collective-permute-done | bytes 540704 | tf_op jit(solution)/shard_map/ppermute | solution.py:72
  80.5 3.5 %collective-permute-done.15.came_ref = s16[528,512]{1,0:T(8,128)(2,1)S(1)} collective-permute-done((s16[528,512]{1,0:T(8,128)(2,1)S(1)}, s16[528,512]{1,0:T(8,128)(2,1)S(1)}, u32[]{:S(2)}, u32[]{:S(2)}) %collective-permute-start.15) | collective-permute-done | bytes 540704 | tf_op jit(solution)/shard_map/ppermute | solution.py:72
  84.6 2.9 %collective-permute-start.21 = (bf16[2,8,32,512]{3,2,1,0:T(8,128)(2,1)S(1)}, bf16[2,8,32,512]{3,2,1,0:T(8,128)(2,1)S(1)}, u32[]{:S(2)}, u32[]{:S(2)}) collective-permute-start(bf16[2,8,32,512]{3,2,1,0:T(8,128)(2,1)S(1)} %join.7.rest_0_), channel_id=1, source_target_pairs={{0,6},{1,3},{2,0},{3,5},{4,2},{5,7},{6,4},{7,1},{8,14},{9,11},{10,... | collective-permute-start | bytes 1572872 | tf_op jit(solution)/shard_map/ppermute | solution.py:72
  87.5 8.2 %partial.6 = (s16[528,512]{1,0:T(8,128)(2,1)S(1)}, s16[528,512]{1,0:T(8,128)(2,1)S(1)}, f32[16,32,512]{2,1,0:T(8,128)S(1)}, f32[16,32,512]{2,1,0:T(8,128)S(1)}) custom-call(s32[32]{0:T(128)S(1)} %get-tuple-element.96.blk, s32[32]{0:T(128)S(1)} %get-tuple-element.95.prow, s32[8]{0:T(128)S(1)} %stack.63.pos, bf16[2,8,32,512]{3,2,1,0:T(8,128)(2,1)S(1)} %join.6.rest_0_, ...), custom_call_target="tpu_custom_call" | custom-call | flops 4294967296 | bytes 25165824 | tf_op jit(solution)/shard_map/partial/pallas_call | solution.py:255
  99.1 2.5 %collective-permute-done.18.refs_4_ = s16[528,512]{1,0:T(8,128)(2,1)S(1)} collective-permute-done((s16[528,512]{1,0:T(8,128)(2,1)S(1)}, s16[528,512]{1,0:T(8,128)(2,1)S(1)}, u32[]{:S(2)}, u32[]{:S(2)}) %collective-permute-start.18) | collective-permute-done | bytes 540704 | tf_op jit(solution)/shard_map/ppermute | solution.py:72
  103.5 7.0 %partial.7 = (s16[528,512]{1,0:T(8,128)(2,1)S(1)}, s16[528,512]{1,0:T(8,128)(2,1)S(1)}, f32[16,32,512]{2,1,0:T(8,128)S(1)}, f32[16,32,512]{2,1,0:T(8,128)S(1)}) custom-call(s32[32]{0:T(128)S(1)} %get-tuple-element.96.blk, s32[32]{0:T(128)S(1)} %get-tuple-element.95.prow, s32[8]{0:T(128)S(1)} %stack.63.pos, bf16[2,8,32,512]{3,2,1,0:T(8,128)(2,1)S(1)} %join.7.rest_0_, ...), custom_call_target="tpu_custom_call" | custom-call | flops 4294967296 | bytes 25165824 | tf_op jit(solution)/shard_map/partial/pallas_call | solution.py:255
  112.6 5.1 %collective-permute-start.25 = (s16[272,512]{1,0:T(8,128)(2,1)S(1)}, s16[272,512]{1,0:T(8,128)(2,1)S(1)}, u32[]{:S(2)}, u32[]{:S(2)}) collective-permute-start(s16[272,512]{1,0:T(8,128)(2,1)S(1)} %get-tuple-element.81), channel_id=1, source_target_pairs={{0,1},{1,9},{2,3},{3,11},{4,5},{5,13},{6,7},{7,15},{8,0},{9,8},{10... | collective-permute-start | bytes 835592 | tf_op jit(solution)/shard_map/ppermute | solution.py:72
  118.6 5.2 %collective-permute-done.25.refs_1_ = s16[272,512]{1,0:T(8,128)(2,1)S(1)} collective-permute-done((s16[272,512]{1,0:T(8,128)(2,1)S(1)}, s16[272,512]{1,0:T(8,128)(2,1)S(1)}, u32[]{:S(2)}, u32[]{:S(2)}) %collective-permute-start.25) | collective-permute-done | bytes 278560 | tf_op jit(solution)/shard_map/ppermute | solution.py:72
  125.1 3.9 %collective-permute-done.27.refs_3_ = s16[272,512]{1,0:T(8,128)(2,1)S(1)} collective-permute-done((s16[272,512]{1,0:T(8,128)(2,1)S(1)}, s16[272,512]{1,0:T(8,128)(2,1)S(1)}, u32[]{:S(2)}, u32[]{:S(2)}) %collective-permute-start.27) | collective-permute-done | bytes 278560 | tf_op jit(solution)/shard_map/ppermute | solution.py:72
  130.6 3.8 %collective-permute-done.33.refs_1_ = s16[528,512]{1,0:T(8,128)(2,1)S(1)} collective-permute-done((s16[528,512]{1,0:T(8,128)(2,1)S(1)}, s16[528,512]{1,0:T(8,128)(2,1)S(1)}, u32[]{:S(2)}, u32[]{:S(2)}) %collective-permute-start.33) | collective-permute-done | bytes 540704 | tf_op jit(solution)/shard_map/ppermute | solution.py:72
  134.4 6.7 %collective-permute-done.34.refs_4_ = s16[528,512]{1,0:T(8,128)(2,1)S(1)} collective-permute-done((s16[528,512]{1,0:T(8,128)(2,1)S(1)}, s16[528,512]{1,0:T(8,128)(2,1)S(1)}, u32[]{:S(2)}, u32[]{:S(2)}) %collective-permute-start.34) | collective-permute-done | bytes 540704 | tf_op jit(solution)/shard_map/ppermute | solution.py:72
  148.9 7.6 %collective-permute-done.36.refs_1_ = s16[272,512]{1,0:T(8,128)(2,1)S(1)} collective-permute-done((s16[272,512]{1,0:T(8,128)(2,1)S(1)}, s16[272,512]{1,0:T(8,128)(2,1)S(1)}, u32[]{:S(2)}, u32[]{:S(2)}) %collective-permute-start.36) | collective-permute-done | bytes 278560 | tf_op jit(solution)/shard_map/ppermute | solution.py:72
  159.8 3.0 %collective-permute-start.40 = (bf16[8,8,1024]{2,1,0:T(8,128)(2,1)S(1)}, bf16[8,8,1024]{2,1,0:T(8,128)(2,1)S(1)}, u32[]{:S(2)}, u32[]{:S(2)}) collective-permute-start(bf16[8,8,1024]{2,1,0:T(8,128)(2,1)S(1)} %get-tuple-element.102), channel_id=1, source_target_pairs={{0,4},{1,5},{2,6},{3,7},{4,0},{5,1},{6,2},{7,3},{8,12},{9,13},{10,... | collective-permute-start | bytes 393224 | tf_op jit(solution)/shard_map/ppermute | solution.py:72
  163.1 5.3 %collective-permute-done.39.refs_5_ = bf16[8,8,1024]{2,1,0:T(8,128)(2,1)S(1)} collective-permute-done((bf16[8,8,1024]{2,1,0:T(8,128)(2,1)S(1)}, bf16[8,8,1024]{2,1,0:T(8,128)(2,1)S(1)}, u32[]{:S(2)}, u32[]{:S(2)}) %collective-permute-start.39) | collective-permute-done | bytes 131104 | tf_op jit(solution)/shard_map/ppermute | solution.py:72
  (110 shorter events, 50.3 us)
Async XLA Ops:
  0.0 41.1 %collective-permute-start.8 = (bf16[32,512,256]{2,1,0:T(8,128)(2,1)}, bf16[32,512,256]{2,1,0:T(8,128)(2,1)}, u32[]{:S(2)}, u32[]{:S(2)}) collective-permute-start(bf16[32,512,256]{2,1,0:T(8,128)(2,1)} %own_ref.1), channel_id=1, source_target_pairs={{0,1},{1,0},{2,3},{3,2},{4,5},{5,4},{6,7},{7,6},{8,9},{9,8},{10,11... | collective-permute-start | bytes 25165832 | tf_op jit(solution)/shard_map/ppermute | solution.py:72
  15.5 14.4 %collective-permute-start.4 = (bf16[2,8,32,512]{3,2,1,0:T(8,128)(2,1)S(1)}, bf16[2,8,32,512]{3,2,1,0:T(8,128)(2,1)S(1)}, u32[]{:S(2)}, u32[]{:S(2)}) collective-permute-start(bf16[2,8,32,512]{3,2,1,0:T(8,128)(2,1)S(1)} %join.4.rest_0_), channel_id=1, source_target_pairs={{0,2},{1,7},{2,4},{3,1},{4,6},{5,3},{6,0},{7,5},{8,10},{9,15},{10,... | collective-permute-start | bytes 1572872 | tf_op jit(solution)/shard_map/ppermute | solution.py:72
  15.9 14.4 %collective-permute-start.5 = (bf16[2,8,32,512]{3,2,1,0:T(8,128)(2,1)S(1)}, bf16[2,8,32,512]{3,2,1,0:T(8,128)(2,1)S(1)}, u32[]{:S(2)}, u32[]{:S(2)}) collective-permute-start(bf16[2,8,32,512]{3,2,1,0:T(8,128)(2,1)S(1)} %join.4.rest_0_), channel_id=1, source_target_pairs={{0,6},{1,3},{2,0},{3,5},{4,2},{5,7},{6,4},{7,1},{8,14},{9,11},{10,... | collective-permute-start | bytes 1572872 | tf_op jit(solution)/shard_map/ppermute | solution.py:72
  19.7 16.7 %collective-permute-start.6 = (bf16[1,8,64,512]{3,2,1,0:T(8,128)(2,1)}, bf16[1,8,64,512]{3,2,1,0:T(8,128)(2,1)}, u32[]{:S(2)}, u32[]{:S(2)}) collective-permute-start(bf16[1,8,64,512]{3,2,1,0:T(8,128)(2,1)} %rest.1), channel_id=1, source_target_pairs={{0,8},{1,9},{2,10},{3,11},{4,12},{5,13},{6,14},{7,15},{8,0},{9,1},... | collective-permute-start | bytes 1572872 | tf_op jit(solution)/shard_map/ppermute | solution.py:72
  24.7 35.1 %collective-permute-start.11 = (bf16[4,8,32,512]{3,2,1,0:T(8,128)(2,1)S(1)}, bf16[4,8,32,512]{3,2,1,0:T(8,128)(2,1)}, u32[]{:S(2)}, u32[]{:S(2)}) collective-permute-start(bf16[4,8,32,512]{3,2,1,0:T(8,128)(2,1)S(1)} %join.5.rest_0_), channel_id=1, source_target_pairs={{0,8},{1,9},{2,10},{3,11},{4,12},{5,13},{6,14},{7,15},{8,0},{9,1},... | collective-permute-start | bytes 3145736 | tf_op jit(solution)/shard_map/ppermute | solution.py:72
  29.9 17.6 %collective-permute-start.7 = (bf16[2,8,32,512]{3,2,1,0:T(8,128)(2,1)S(1)}, bf16[2,8,32,512]{3,2,1,0:T(8,128)(2,1)}, u32[]{:S(2)}, u32[]{:S(2)}) collective-permute-start(bf16[2,8,32,512]{3,2,1,0:T(8,128)(2,1)S(1)} %collective-permute-done.4.rest_1_), channel_id=1, source_target_pairs={{0,2},{1,7},{2,4},{3,1},{4,6},{5,3},{6,0},{7,5},{8,10},{9,15},{10,... | collective-permute-start | bytes 1572872 | tf_op jit(solution)/shard_map/ppermute | solution.py:72
  37.5 20.1 %collective-permute-start.9 = (bf16[2,8,32,512]{3,2,1,0:T(8,128)(2,1)S(1)}, bf16[2,8,32,512]{3,2,1,0:T(8,128)(2,1)}, u32[]{:S(2)}, u32[]{:S(2)}) collective-permute-start(bf16[2,8,32,512]{3,2,1,0:T(8,128)(2,1)S(1)} %join.6.rest_0_), channel_id=1, source_target_pairs={{0,2},{1,7},{2,4},{3,1},{4,6},{5,3},{6,0},{7,5},{8,10},{9,15},{10,... | collective-permute-start | bytes 1572872 | tf_op jit(solution)/shard_map/ppermute | solution.py:72
  37.6 20.0 %collective-permute-start.10 = (bf16[2,8,32,512]{3,2,1,0:T(8,128)(2,1)S(1)}, bf16[2,8,32,512]{3,2,1,0:T(8,128)(2,1)}, u32[]{:S(2)}, u32[]{:S(2)}) collective-permute-start(bf16[2,8,32,512]{3,2,1,0:T(8,128)(2,1)S(1)} %join.6.rest_0_), channel_id=1, source_target_pairs={{0,6},{1,3},{2,0},{3,5},{4,2},{5,7},{6,4},{7,1},{8,14},{9,11},{10,... | collective-permute-start | bytes 1572872 | tf_op jit(solution)/shard_map/ppermute | solution.py:72
  55.6 17.1 %collective-permute-start.13 = (s16[528,512]{1,0:T(8,128)(2,1)S(1)}, s16[528,512]{1,0:T(8,128)(2,1)S(1)}, u32[]{:S(2)}, u32[]{:S(2)}) collective-permute-start(s16[528,512]{1,0:T(8,128)(2,1)S(1)} %get-tuple-element.57), channel_id=1, source_target_pairs={{0,32},{1,97},{2,34},{3,99},{4,36},{5,101},{6,38},{7,103},{8,40},{... | collective-permute-start | bytes 1622024 | tf_op jit(solution)/shard_map/ppermute | solution.py:72
  70.1 13.9 %collective-permute-start.15 = (s16[528,512]{1,0:T(8,128)(2,1)S(1)}, s16[528,512]{1,0:T(8,128)(2,1)S(1)}, u32[]{:S(2)}, u32[]{:S(2)}) collective-permute-start(s16[528,512]{1,0:T(8,128)(2,1)S(1)} %get-tuple-element.63), channel_id=1, source_target_pairs={{0,32},{1,97},{2,34},{3,99},{4,36},{5,101},{6,38},{7,103},{8,40},{... | collective-permute-start | bytes 1622024 | tf_op jit(solution)/shard_map/ppermute | solution.py:72
  70.2 17.3 %collective-permute-start.20 = (bf16[2,8,32,512]{3,2,1,0:T(8,128)(2,1)S(1)}, bf16[2,8,32,512]{3,2,1,0:T(8,128)(2,1)S(1)}, u32[]{:S(2)}, u32[]{:S(2)}) collective-permute-start(bf16[2,8,32,512]{3,2,1,0:T(8,128)(2,1)S(1)} %join.7.rest_0_), channel_id=1, source_target_pairs={{0,2},{1,7},{2,4},{3,1},{4,6},{5,3},{6,0},{7,5},{8,10},{9,15},{10,... | collective-permute-start | bytes 1572872 | tf_op jit(solution)/shard_map/ppermute | solution.py:72
  70.2 17.3 %collective-permute-start.16 = (bf16[2,8,32,512]{3,2,1,0:T(8,128)(2,1)}, bf16[2,8,32,512]{3,2,1,0:T(8,128)(2,1)S(1)}, u32[]{:S(2)}, u32[]{:S(2)}) collective-permute-start(bf16[2,8,32,512]{3,2,1,0:T(8,128)(2,1)} %collective-permute-done.9.rest_1_), channel_id=1, source_target_pairs={{0,2},{1,7},{2,4},{3,1},{4,6},{5,3},{6,0},{7,5},{8,10},{9,15},{10,... | collective-permute-start | bytes 1572872 | tf_op jit(solution)/shard_map/ppermute | solution.py:72
  84.5 17.0 %collective-permute-start.18 = (s16[528,512]{1,0:T(8,128)(2,1)S(1)}, s16[528,512]{1,0:T(8,128)(2,1)S(1)}, u32[]{:S(2)}, u32[]{:S(2)}) collective-permute-start(s16[528,512]{1,0:T(8,128)(2,1)S(1)} %relay.4), channel_id=1, source_target_pairs={{0,32},{1,97},{2,34},{3,99},{4,36},{5,101},{6,38},{7,103},{8,40},{... | collective-permute-start | bytes 1622024 | tf_op jit(solution)/shard_map/ppermute | solution.py:72
  84.6 18.9 %collective-permute-start.21 = (bf16[2,8,32,512]{3,2,1,0:T(8,128)(2,1)S(1)}, bf16[2,8,32,512]{3,2,1,0:T(8,128)(2,1)S(1)}, u32[]{:S(2)}, u32[]{:S(2)}) collective-permute-start(bf16[2,8,32,512]{3,2,1,0:T(8,128)(2,1)S(1)} %join.7.rest_0_), channel_id=1, source_target_pairs={{0,6},{1,3},{2,0},{3,5},{4,2},{5,7},{6,4},{7,1},{8,14},{9,11},{10,... | collective-permute-start | bytes 1572872 | tf_op jit(solution)/shard_map/ppermute | solution.py:72
  87.5 16.0 %collective-permute-start.22 = (bf16[2,8,32,512]{3,2,1,0:T(8,128)(2,1)S(1)}, bf16[2,8,32,512]{3,2,1,0:T(8,128)(2,1)S(1)}, u32[]{:S(2)}, u32[]{:S(2)}) collective-permute-start(bf16[2,8,32,512]{3,2,1,0:T(8,128)(2,1)S(1)} %collective-permute-done.20.rest_1_), channel_id=1, source_target_pairs={{0,2},{1,7},{2,4},{3,1},{4,6},{5,3},{6,0},{7,5},{8,10},{9,15},{10,... | collective-permute-start | bytes 1572872 | tf_op jit(solution)/shard_map/ppermute | solution.py:72
  95.7 21.9 %collective-permute-start.24 = (s16[528,512]{1,0:T(8,128)(2,1)S(1)}, s16[528,512]{1,0:T(8,128)(2,1)S(1)}, u32[]{:S(2)}, u32[]{:S(2)}) collective-permute-start(s16[528,512]{1,0:T(8,128)(2,1)S(1)} %get-tuple-element.70), channel_id=1, source_target_pairs={{0,32},{1,97},{2,34},{3,99},{4,36},{5,101},{6,38},{7,103},{8,40},{... | collective-permute-start | bytes 1622024 | tf_op jit(solution)/shard_map/ppermute | solution.py:72
  98.0 14.6 %collective-permute-start.23 = (s16[528,512]{1,0:T(8,128)(2,1)S(1)}, s16[528,512]{1,0:T(8,128)(2,1)S(1)}, u32[]{:S(2)}, u32[]{:S(2)}) collective-permute-start(s16[528,512]{1,0:T(8,128)(2,1)S(1)} %get-tuple-element.78), channel_id=1, source_target_pairs={{0,96},{1,33},{2,98},{3,35},{4,100},{5,37},{6,102},{7,39},{8,104},... | collective-permute-start | bytes 1622024 | tf_op jit(solution)/shard_map/ppermute | solution.py:72
  102.8 15.4 %collective-permute-start.19 = (s16[272,512]{1,0:T(8,128)(2,1)S(1)}, s16[272,512]{1,0:T(8,128)(2,1)S(1)}, u32[]{:S(2)}, u32[]{:S(2)}) collective-permute-start(s16[272,512]{1,0:T(8,128)(2,1)S(1)} %get-tuple-element.73), channel_id=1, source_target_pairs={{0,0},{1,8},{2,2},{3,10},{4,4},{5,12},{6,6},{7,14},{8,1},{9,9},{10... | collective-permute-start | bytes 835592 | tf_op jit(solution)/shard_map/ppermute | solution.py:72
  110.5 19.5 %collective-permute-start.31 = (s16[528,512]{1,0:T(8,128)(2,1)S(1)}, s16[528,512]{1,0:T(8,128)(2,1)S(1)}, u32[]{:S(2)}, u32[]{:S(2)}) collective-permute-start(s16[528,512]{1,0:T(8,128)(2,1)S(1)} %get-tuple-element.86), channel_id=1, source_target_pairs={{0,96},{1,33},{2,98},{3,35},{4,100},{5,37},{6,102},{7,39},{8,104},... | collective-permute-start | bytes 1622024 | tf_op jit(solution)/shard_map/ppermute | solution.py:72
  110.6 19.5 %collective-permute-start.32 = (s16[528,512]{1,0:T(8,128)(2,1)S(1)}, s16[528,512]{1,0:T(8,128)(2,1)S(1)}, u32[]{:S(2)}, u32[]{:S(2)}) collective-permute-start(s16[528,512]{1,0:T(8,128)(2,1)S(1)} %get-tuple-element.77), channel_id=1, source_target_pairs={{0,32},{1,97},{2,34},{3,99},{4,36},{5,101},{6,38},{7,103},{8,40},{... | collective-permute-start | bytes 1622024 | tf_op jit(solution)/shard_map/ppermute | solution.py:72
  144.3 13.9 %collective-permute-start.37 = (s16[272,512]{1,0:T(8,128)(2,1)S(1)}, s16[272,512]{1,0:T(8,128)(2,1)S(1)}, u32[]{:S(2)}, u32[]{:S(2)}) collective-permute-start(s16[272,512]{1,0:T(8,128)(2,1)S(1)} %get-tuple-element.93), channel_id=1, source_target_pairs={{0,16},{1,24},{2,18},{3,26},{4,20},{5,28},{6,22},{7,30},{8,17},{9,... | collective-permute-start | bytes 835592 | tf_op jit(solution)/shard_map/ppermute | solution.py:72
  144.9 13.7 %collective-permute-start.38 = (s16[272,512]{1,0:T(8,128)(2,1)S(1)}, s16[272,512]{1,0:T(8,128)(2,1)S(1)}, u32[]{:S(2)}, u32[]{:S(2)}) collective-permute-start(s16[272,512]{1,0:T(8,128)(2,1)S(1)} %get-tuple-element.94), channel_id=1, source_target_pairs={{0,17},{1,25},{2,19},{3,27},{4,21},{5,29},{6,23},{7,31},{8,16},{9,... | collective-permute-start | bytes 835592 | tf_op jit(solution)/shard_map/ppermute | solution.py:72
  146.4 16.4 %collective-permute-start.28 = (bf16[8,8,1024]{2,1,0:T(8,128)(2,1)S(1)}, bf16[8,8,1024]{2,1,0:T(8,128)(2,1)S(1)}, u32[]{:S(2)}, u32[]{:S(2)}) collective-permute-start(bf16[8,8,1024]{2,1,0:T(8,128)(2,1)S(1)} %get-tuple-element.107), channel_id=1, source_target_pairs={{0,2},{1,3},{2,4},{3,5},{4,6},{5,7},{6,0},{7,1},{8,10},{9,11},{10,... | collective-permute-start | bytes 393224 | tf_op jit(solution)/shard_map/ppermute | solution.py:72
  146.5 16.6 %collective-permute-start.29 = (bf16[8,8,1024]{2,1,0:T(8,128)(2,1)S(1)}, bf16[8,8,1024]{2,1,0:T(8,128)(2,1)S(1)}, u32[]{:S(2)}, u32[]{:S(2)}) collective-permute-start(bf16[8,8,1024]{2,1,0:T(8,128)(2,1)S(1)} %get-tuple-element.106), channel_id=1, source_target_pairs={{0,4},{1,5},{2,6},{3,7},{4,0},{5,1},{6,2},{7,3},{8,12},{9,13},{10,... | collective-permute-start | bytes 393224 | tf_op jit(solution)/shard_map/ppermute | solution.py:72
  (25 other events, 228.7 us)
